TPU v7x, 768 devices: a whole 4x8x12 slice. The times are simulated.
768 devices in a mesh: dp: 8 (over x, core), tensor: 4 (over z_hi), expert: 24 (over y, z_lo).
Axes of the slice: x: 4, y: 8, z: 12 (z_hi: 4, z_lo: 3; z = z_hi * 3 + z_lo), core: 2. Of those that a mesh axis runs over, the one named last changes fastest.
Arguments:
- attn_heads: bfloat16 [8, 24, 24, 2560], P('dp', None, 'expert', 'tensor'), may hold values from -13 to 13, as said below
- out_proj: bfloat16 [2560, 5120], P('tensor'), may hold values from -0.125 to 0.125
- norm_gain: float32 [5120], replicated, may hold values from 0.5 to 2
- router: bfloat16 [5120, 24], replicated, may hold values from -0.15625 to 0.15625
- expert_ids: int32 [8, 24, 24], P('dp', 'tensor', 'expert'), may hold values from 0 to 23, as said below
- w_gate: bfloat16 [24, 5120, 4096], P('expert', None, ('dp', 'tensor')), may hold values from -0.078125 to 0.078125
- w_up: bfloat16 [24, 5120, 4096], P('expert', None, ('dp', 'tensor')), may hold values from -0.078125 to 0.078125
- w_down: bfloat16 [24, 4096, 5120], P('expert', ('dp', 'tensor')), may hold values from -0.1875 to 0.1875
Outputs:
- expert_out: bfloat16 [8, 24, 24, 5120], P('dp', 'tensor', 'expert')
Inputs may be any that keep to these rules, and one draw needn't show every extreme that they name: `attn_heads`: values are those of a random draw, possibly with a component shared by all tokens, times a factor for each token. `expert_ids`: among the tokens of one device, at most 2 name the same expert, and some device of each dp and tensor index has exactly 2 naming one. Among the tokens of the 24 devices that share a dp index and a tensor index, at most 8 name the same expert, and in every such group one expert is named exactly 8 times.
All inputs are finite; a program needn't handle non-finite values.
Results may differ from a plain program's by a relative error of at most 0.0095.
Values may be sent and summed in bfloat16 or wider, within the bound.
No kernel may reach another device: no remote copies, remote signals or barrier semaphores. Data moves between devices by JAX's collectives and lax.ppermute only.
A program may use at most 32 MiB of HBM per device.

v0:
```python
import jax
import jax.numpy as jnp
from jax import lax
from jax.sharding import PartitionSpec as P


def on_device(attn_heads, out_proj, norm_gain, router, expert_ids, w_gate, w_up, w_down):
    tensor_count = lax.axis_size("tensor")
    expert_count = lax.axis_size("expert")
    head_rows = attn_heads.reshape(-1, attn_heads.shape[-1])
    tok_rows = head_rows.shape[0] // tensor_count
    model_width = out_proj.shape[1]
    send_cap = max(2, tok_rows // (expert_count // 2))
    recv_cap = min(tok_rows + max(2, tok_rows // 5), send_cap * (expert_count - 2) + 2)
    attended = lax.psum_scatter(
        jnp.dot(head_rows, out_proj, preferred_element_type=jnp.float32),
        "tensor",
        scatter_dimension=0,
        tiled=True,
    )
    inverse = lax.rsqrt(jnp.mean(attended * attended, axis=-1, keepdims=True) + 1e-05)
    normed = attended * inverse * norm_gain
    router_logits = jnp.dot(normed.astype(jnp.bfloat16), router, preferred_element_type=jnp.float32)
    chosen_ids = expert_ids.reshape(-1)
    expert_index = jnp.arange(expert_count, dtype=jnp.int32)
    member_mask = chosen_ids[:, None] == expert_index[None, :]
    router_score = jax.nn.sigmoid(jnp.sum(jnp.where(member_mask, router_logits, 0.0), axis=1))
    routed = (normed * router_score[:, None]).astype(jnp.bfloat16)
    running = jnp.cumsum(member_mask.astype(jnp.int32), axis=0)
    rank_within = jnp.sum(jnp.where(member_mask, running, 0), axis=1) - 1
    slot_index = chosen_ids * send_cap + rank_within
    slot_count = expert_count * send_cap
    slot_range = jnp.arange(slot_count, dtype=jnp.int32)
    placing = (slot_range[:, None] == slot_index[None, :]).astype(jnp.bfloat16)
    outgoing = jnp.dot(placing, routed, preferred_element_type=jnp.float32).astype(jnp.bfloat16)
    outgoing = outgoing.reshape(expert_count, send_cap, model_width)
    filled = jnp.sum(placing, axis=1).reshape(expert_count, send_cap)
    incoming, present = (
        lax.all_to_all(outgoing, "expert", split_axis=0, concat_axis=0, tiled=True),
        lax.all_to_all(filled, "expert", split_axis=0, concat_axis=0, tiled=True),
    )
    source_counts = jnp.sum(present.astype(jnp.int32), axis=1)
    arrived = incoming.reshape(slot_count, model_width)
    source_offsets = jnp.cumsum(source_counts) - source_counts
    within_slot = jnp.arange(send_cap, dtype=jnp.int32)
    compact_position = jnp.where(
        within_slot[None, :] < source_counts[:, None],
        source_offsets[:, None] + within_slot[None, :],
        -1,
    ).reshape(-1)
    selector = (jnp.arange(recv_cap, dtype=jnp.int32)[:, None] == compact_position[None, :]).astype(
        jnp.bfloat16
    )
    compact = jnp.dot(selector, arrived, preferred_element_type=jnp.float32).astype(jnp.bfloat16)
    gate_matrix = w_gate[0]
    up_matrix = w_up[0]
    down_matrix = w_down[0]
    column_weights = lax.all_to_all(
        down_matrix, ("dp", "tensor"), split_axis=1, concat_axis=0, tiled=True
    )
    rows_piece = lax.all_gather(compact, ("dp", "tensor"), axis=0, tiled=True)
    gate_value = jnp.dot(rows_piece, gate_matrix, preferred_element_type=jnp.float32)
    up_value = jnp.dot(rows_piece, up_matrix, preferred_element_type=jnp.float32)
    hidden_rows = (jax.nn.silu(gate_value) * up_value).astype(jnp.bfloat16)
    hidden_whole = lax.all_gather(hidden_rows, ("dp", "tensor"), axis=1, tiled=True)
    column_out = jnp.dot(hidden_whole, column_weights, preferred_element_type=jnp.float32)
    summed = lax.all_to_all(
        column_out.astype(jnp.bfloat16), ("dp", "tensor"), split_axis=0, concat_axis=1, tiled=True
    ).astype(column_out.dtype)
    expert_rows = summed.astype(jnp.bfloat16)
    back_slots = jnp.dot(selector.T, expert_rows, preferred_element_type=jnp.float32).astype(
        jnp.bfloat16
    )
    back_slots = back_slots.reshape(expert_count, send_cap, model_width)
    returned = lax.all_to_all(back_slots, "expert", split_axis=0, concat_axis=0, tiled=True)
    combined = jnp.dot(
        placing.T, returned.reshape(slot_count, model_width), preferred_element_type=jnp.float32
    )
    return combined.astype(jnp.bfloat16).reshape(1, tok_rows, 1, model_width)


def solution(mesh):
    in_specs = (
        P("dp", None, "expert", "tensor"),
        P("tensor", None),
        P(),
        P(),
        P("dp", "tensor", "expert"),
        P("expert", None, ("dp", "tensor")),
        P("expert", None, ("dp", "tensor")),
        P("expert", ("dp", "tensor"), None),
    )
    out_specs = P("dp", "tensor", "expert", None)
    return jax.shard_map(
        on_device, mesh=mesh, in_specs=in_specs, out_specs=out_specs, check_vma=False
    )
```

profile of v0, /device:TPU:8, one launch (start us, length us, event | category | flops | bytes accessed | tf_op | source)
XLA Modules:
  0.0 323.7 jit_solution(5287113078967079213)
XLA Ops:
  6.5 0.0 copy-start
  6.5 4.0 %fusion.26 = f32[24,5120]{1,0:T(8,128)S(1)} fusion(bf16[640,5120]{1,0:T(8,128)(2,1)} %param.9, bf16[1,24,1,640]{3,1,2,0:T(8,128)(2,1)} %param.8), kind=kOutput, calls=%fused_computation.26 | convolution fusion | flops 157286400 | bytes 7075840 | tf_op jit(solution)/shard_map/dot_general | solution.py:16
  10.5 0.0 copy-start.3
  10.5 34.7 %fusion = f32[8,5120]{1,0:T(8,128)S(1)} fusion(f32[24,5120]{1,0:T(8,128)S(1)} %fusion.26), kind=kCustom, calls=%all-reduce-scatter | all-reduce-scatter fusion | flops 163841 | bytes 659456
  45.2 2.2 collective-permute-start
  47.4 0.1 fusion.30
  47.5 0.2 select_reduce_fusion
  47.7 0.1 fusion.32
  47.8 0.7 all_to_all.52
  48.5 18.5 %all-to-all-start = ((bf16[24,1,2]{2,1,0:T(2,128)(2,1)}), bf16[24,1,2]{2,1,0:T(2,128)(2,1)S(1)}, u32[]{:S(2)}, u32[]{:S(2)}) async-start(bf16[24,1,2]{2,1,0:T(2,128)(2,1)} %all_to_all.52), calls=%async_computation | async-start | bytes 24576 | tf_op jit(solution)/shard_map/all_to_all | solution.py:40
  67.0 1.4 dynamic-slice.4
  69.0 0.0 collective-permute-done
  69.0 0.3 concatenate
  69.3 0.2 multiply_reduce_fusion
  69.5 0.0 copy-done.3
  69.5 0.4 fusion.18
  69.9 0.4 convolution_convert_fusion.1
  70.3 1.0 reshape.120
  71.3 3.6 %all-to-all-done = bf16[24,1,2]{2,1,0:T(2,128)(2,1)S(1)} async-done(((bf16[24,1,2]{2,1,0:T(2,128)(2,1)}), bf16[24,1,2]{2,1,0:T(2,128)(2,1)S(1)}, u32[]{:S(2)}, u32[]{:S(2)}) %all-to-all-start) | async-done | bytes 128 | tf_op jit(solution)/shard_map/all_to_all | solution.py:40
  74.9 5.4 %all-to-all-start.1 = ((bf16[24,2,5120]{2,1,0:T(2,128)(2,1)}), bf16[24,2,5120]{2,1,0:T(2,128)(2,1)S(1)}, u32[]{:S(2)}, u32[]{:S(2)}) async-start(bf16[24,2,5120]{2,1,0:T(2,128)(2,1)} %reshape.120), calls=%async_computation.1 | async-start | bytes 983040 | tf_op jit(solution)/shard_map/all_to_all | solution.py:39
  80.4 0.0 all-gather.3.cloned.1.call-start
  80.4 0.5 convert_reduce_fusion
  80.9 0.1 copy.22
  81.1 0.1 reduce.2
  81.2 0.1 add_select_fusion
  81.3 0.1 select_n.21
  81.4 11.2 %all-to-all-done.1 = bf16[24,2,5120]{2,1,0:T(2,128)(2,1)S(1)} async-done(((bf16[24,2,5120]{2,1,0:T(2,128)(2,1)}), bf16[24,2,5120]{2,1,0:T(2,128)(2,1)S(1)}, u32[]{:S(2)}, u32[]{:S(2)}) %all-to-all-start.1) | async-done | bytes 491552 | tf_op jit(solution)/shard_map/all_to_all | solution.py:39
  92.6 0.2 reshape.121
  92.8 0.8 convolution_convert_fusion.3
  93.6 0.0 all-gather.3.cloned.1.call-update
  93.6 0.0 copy-start.5
  93.6 0.0 all-gather.5.cloned.1.call-start
  93.7 73.8 %all-gather.3.cloned.1.call-done = bf16[256,5120]{1,0:T(8,128)(2,1)} async-done(((bf16[8,5120]{1,0:T(8,128)(2,1)}), bf16[256,5120]{1,0:T(8,128)(2,1)}) %all-gather.3.cloned.1.call-update) | async-done | bytes 2621456 | tf_op jit(solution)/shard_map/all_gather | solution.py:61
  167.4 2.7 fusion.7
  170.2 1.5 fusion.15
  171.7 0.0 all-gather.5.cloned.1.call-update
  171.7 1.8 copy.23
  173.5 60.1 %all_to_all.58 = bf16[128,32,160]{0,2,1:T(8,128)(2,1)} all-to-all(bf16[128,32,160]{0,2,1:T(8,128)(2,1)S(1)} %bitcast.42), channel_id=1, replica_groups=mesh['dp'=8,'tensor'=4,'expert'=24] {'dp','tensor'}, dimensions={1} | all-to-all | bytes 2621440 | tf_op jit(solution)/shard_map/all_to_all | solution.py:58
  233.6 35.4 %all-gather.5.cloned.1.call-done = bf16[256,4096]{1,0:T(8,128)(2,1)} async-done(((bf16[256,128]{1,0:T(8,128)(2,1)}), bf16[256,4096]{1,0:T(8,128)(2,1)}) %all-gather.5.cloned.1.call-update) | async-done | bytes 2097168 | tf_op jit(solution)/shard_map/all_gather | solution.py:65
  269.0 2.8 fusion.12
  271.8 0.1 copy.25
  271.9 20.4 %all_to_all.59 = bf16[32,8,160]{2,1,0:T(8,128)(2,1)S(1)} all-to-all(bf16[32,8,160]{2,1,0:T(8,128)(2,1)S(1)} %bitcast.43), channel_id=1, replica_groups=mesh['dp'=8,'tensor'=4,'expert'=24] {'dp','tensor'}, dimensions={0} | all-to-all | bytes 163840 | tf_op jit(solution)/shard_map/all_to_all | solution.py:67
  292.3 0.2 all_to_all.50
  292.5 0.3 convolution_convert_fusion
  292.8 0.2 reshape.122
  293.0 22.7 %all_to_all.60 = bf16[24,2,5120]{2,1,0:T(2,128)(2,1)S(1)} all-to-all(bf16[24,2,5120]{2,1,0:T(2,128)(2,1)S(1)} %reshape.122), channel_id=1, replica_groups=mesh['dp'=8,'tensor'=4,'expert'=24] {'expert'}, dimensions={0} | all-to-all | bytes 983040 | tf_op jit(solution)/shard_map/all_to_all | solution.py:75
  315.7 0.2 reshape.123
  315.9 0.9 fusion.1
  (16 shorter events, 0.2 us)
Async XLA Ops:
  6.5 160.9 %copy-start = (bf16[1,5120,128]{2,1,0:T(8,128)(2,1)S(1)}, bf16[1,5120,128]{2,1,0:T(8,128)(2,1)}, u32[]{:S(2)}) copy-start(bf16[1,5120,128]{2,1,0:T(8,128)(2,1)} %param.13) | copy-start | bytes 3932164
  6.5 40.9 %copy-start.4 = (s32[1,6,1]{1,2,0:T(1,128)S(1)}, s32[1,6,1]{1,2,0:T(1,128)}, u32[]{:S(2)}) copy-start(s32[1,6,1]{1,2,0:T(1,128)} %param.12) | copy-start | bytes 76
  10.5 59.0 %copy-start.2 = (bf16[5120,24]{0,1:T(8,128)(2,1)S(1)}, bf16[5120,24]{0,1:T(8,128)(2,1)}, u32[]{:S(2)}) copy-start(bf16[5120,24]{0,1:T(8,128)(2,1)} %param.11) | copy-start | bytes 737284
  10.5 59.0 %copy-start.3 = (f32[5120]{0:T(1024)S(1)}, f32[5120]{0:T(1024)}, u32[]{:S(2)}) copy-start(f32[5120]{0:T(1024)} %param.10) | copy-start | bytes 61444
  45.2 23.8 %collective-permute-start = (f32[6,5120]{1,0:T(8,128)S(1)}, f32[6,5120]{1,0:T(8,128)S(1)}, u32[]{:S(2)}, u32[]{:S(2)}) collective-permute-start(f32[6,5120]{1,0:T(8,128)S(1)} %slice), channel_id=1, source_target_pairs={{0,24},{24,48},{48,72},{1,25},{25,49},{49,73},{2,26},{26,50},{50,7... | collective-permute-start | bytes 368648
  48.5 26.4 %all-to-all-start = ((bf16[24,1,2]{2,1,0:T(2,128)(2,1)}), bf16[24,1,2]{2,1,0:T(2,128)(2,1)S(1)}, u32[]{:S(2)}, u32[]{:S(2)}) async-start(bf16[24,1,2]{2,1,0:T(2,128)(2,1)} %all_to_all.52), calls=%async_computation | async-start | bytes 24576 | tf_op jit(solution)/shard_map/all_to_all | solution.py:40
  74.9 17.7 %all-to-all-start.1 = ((bf16[24,2,5120]{2,1,0:T(2,128)(2,1)}), bf16[24,2,5120]{2,1,0:T(2,128)(2,1)S(1)}, u32[]{:S(2)}, u32[]{:S(2)}) async-start(bf16[24,2,5120]{2,1,0:T(2,128)(2,1)} %reshape.120), calls=%async_computation.1 | async-start | bytes 983040 | tf_op jit(solution)/shard_map/all_to_all | solution.py:39
  80.4 87.1 %all-gather.3.cloned.1.call-start = ((), (), s32[]{:S(2)}) async-start(), calls=%async_computation.5 | async-start | bytes 2703360 | tf_op jit(solution)/shard_map/all_gather | solution.py:61
  93.6 76.6 %copy-start.5 = (bf16[1,5120,128]{2,1,0:T(8,128)(2,1)S(1)}, bf16[1,5120,128]{2,1,0:T(8,128)(2,1)}, u32[]{:S(2)}) copy-start(bf16[1,5120,128]{2,1,0:T(8,128)(2,1)} %param.14) | copy-start | bytes 3932164
  93.6 175.4 %all-gather.5.cloned.1.call-start = ((), (), s32[]{:S(2)}) async-start(), calls=%async_computation.6 | async-start | bytes 2162688 | tf_op jit(solution)/shard_map/all_gather | solution.py:65
  167.4 2.8 copy-start.1
Sparse Core Ops, SparseCore 0:
  93.7 73.6 all-gather.2
  171.8 97.1 all-gather.4
where the time goes:
time: 324 us
  blocking collectives  138 us (43%)
  waiting for transfers between devices  124 us (38%)
  starting transfers between devices  26.2 us (8%)
  between operations  14.3 us (4%)
  matrix products  13.8 us (4%)
  local copies, waits for them, and re-layouts  6.22 us (2%)
    all_gather x1, waiting for transfers between devices, on_device(): rows_piece = lax.all_gather(compact, ('dp', 'tensor'), axis=0, tiled=True)  73.8 us
    all_to_all x1, blocking collectives, on_device(): lax.all_to_all(down_matrix, ('dp', 'tensor'), split_axis=1, concat_axis=0...  60.1 us
    all_gather x1, waiting for transfers between devices, on_device(): lax.all_gather(hidden_rows, ('dp', 'tensor'), axis=1, tiled=True)  35.4 us
    unnamed x1, blocking collectives  34.7 us
    all_to_all x1, blocking collectives, on_device(): lax.all_to_all(back_slots, 'expert', split_axis=0, concat_axis=0, tiled=T...  22.7 us
    all_to_all x1, blocking collectives, on_device(): lax.all_to_all(column_out.astype(jnp.bfloat16), ('dp', 'tensor'), split_a...  20.4 us
    all_to_all x1, starting transfers between devices, on_device(): lax.all_to_all(filled, 'expert', split_axis=0, concat_axis=0, tiled=True)  18.5 us
    all_to_all x1, waiting for transfers between devices, on_device(): lax.all_to_all(outgoing, 'expert', split_axis=0, concat_axis=0, tiled=True)  11.2 us
  transfers between devices with their start and end apart: 5, of which 4 were waited for; matrix products, arithmetic and copies ran while one was open for 2% of the time, Pallas kernels for 0%

commit v1 on v0

v1 whole, which is shorter than its diff:
```python
import jax
import jax.numpy as jnp
from jax import lax
from jax.sharding import Mesh, PartitionSpec as P

BF = jnp.bfloat16
F32 = jnp.float32
LANES = 128


def exchange(value, axis):
    return lax.all_to_all(value, axis, split_axis=0, concat_axis=0, tiled=True)


def spread(value, axis):
    count = lax.axis_size(axis)
    return exchange(jnp.broadcast_to(value[None], (count,) + value.shape), axis)


def total_over(partial, axis):
    return jnp.sum(exchange(partial.astype(BF), axis).astype(F32), axis=0)


def on_device(attn_heads, out_proj, norm_gain, router, expert_ids, w_gate, w_up, w_down):
    tensor_count = lax.axis_size("tensor")
    x_count = lax.axis_size("x")
    expert_axes = ("y", "w")
    expert_count = lax.axis_size(expert_axes)
    swap = [(0, 1), (1, 0)]
    head_rows = attn_heads.reshape(-1, attn_heads.shape[-1])
    tok_rows = head_rows.shape[0] // tensor_count
    width = out_proj.shape[1]
    send_cap = max(2, tok_rows // (expert_count // 2))
    recv_cap = min(tok_rows + max(2, tok_rows // 5), send_cap * (expert_count - 2) + 2)
    slots = expert_count * send_cap

    partial = jnp.dot(head_rows, out_proj, preferred_element_type=F32)
    attended = total_over(partial.reshape(tensor_count, tok_rows, width), "tensor")

    inverse = lax.rsqrt(jnp.mean(attended * attended, axis=-1, keepdims=True) + 1e-05)
    normed = attended * inverse * norm_gain
    router_logits = jnp.dot(normed.astype(BF), router, preferred_element_type=F32)
    chosen_ids = expert_ids.reshape(-1)
    expert_index = jnp.arange(expert_count, dtype=jnp.int32)
    member_mask = chosen_ids[:, None] == expert_index[None, :]
    router_score = jax.nn.sigmoid(jnp.sum(jnp.where(member_mask, router_logits, 0.0), axis=1))
    routed = (normed * router_score[:, None]).astype(BF)

    same = chosen_ids[:, None] == chosen_ids[None, :]
    earlier = jnp.arange(tok_rows)[None, :] < jnp.arange(tok_rows)[:, None]
    rank_within = jnp.sum((same & earlier).astype(jnp.int32), axis=1)
    slot_index = chosen_ids * send_cap + rank_within
    slot_range = jnp.arange(slots, dtype=jnp.int32)
    placing = (slot_range[:, None] == slot_index[None, :]).astype(BF)
    flagged = jnp.concatenate([routed, jnp.ones((tok_rows, LANES), BF)], axis=1)
    outgoing = jnp.dot(placing, flagged, preferred_element_type=F32).astype(BF)
    arrived = exchange(outgoing.reshape(expert_count, send_cap, width + LANES), expert_axes)
    arrived = arrived.reshape(slots, width + LANES)

    filled = arrived[:, width].astype(F32)
    before = slot_range[:, None] < slot_range[None, :]
    position = jnp.sum(jnp.where(before, filled[:, None], 0.0), axis=0).astype(jnp.int32)
    position = jnp.where(filled > 0.5, position, -1)
    selector = (jnp.arange(recv_cap, dtype=jnp.int32)[:, None] == position[None, :]).astype(BF)
    compact = jnp.dot(selector, arrived[:, :width], preferred_element_type=F32).astype(BF)

    rows = spread(compact, "tensor").reshape(tensor_count * recv_cap, width)
    rows = spread(rows, "x").reshape(x_count * tensor_count * recv_cap, width)
    other_rows = lax.ppermute(rows, "core", swap)

    def expert_part(block):
        gate_value = jnp.dot(block, w_gate[0], preferred_element_type=F32)
        up_value = jnp.dot(block, w_up[0], preferred_element_type=F32)
        hidden = (jax.nn.silu(gate_value) * up_value).astype(BF)
        return jnp.dot(hidden, w_down[0], preferred_element_type=F32)

    own_sum = expert_part(rows)
    other_sum = expert_part(other_rows)
    pair_sum = own_sum + lax.ppermute(other_sum.astype(BF), "core", swap).astype(F32)
    plane_sum = total_over(pair_sum.reshape(x_count, tensor_count * recv_cap, width), "x")
    expert_rows = total_over(plane_sum.reshape(tensor_count, recv_cap, width), "tensor").astype(BF)

    back = jnp.dot(selector.T, expert_rows, preferred_element_type=F32).astype(BF)
    returned = exchange(back.reshape(expert_count, send_cap, width), expert_axes)
    combined = jnp.dot(placing.T, returned.reshape(slots, width), preferred_element_type=F32)
    return combined.astype(BF).reshape(1, tok_rows, 1, width)


def solution(mesh):
    dp, tensor, expert = (mesh.shape[name] for name in ("dp", "tensor", "expert"))
    fine = Mesh(
        mesh.devices.reshape(dp // 2, 2, tensor, expert // 3, 3), ("x", "core", "tensor", "y", "w")
    )
    dp_axes, expert_axes = ("x", "core"), ("y", "w")
    in_specs = (
        P(dp_axes, None, expert_axes, "tensor"),
        P("tensor", None),
        P(),
        P(),
        P(dp_axes, "tensor", expert_axes),
        P(expert_axes, None, (*dp_axes, "tensor")),
        P(expert_axes, None, (*dp_axes, "tensor")),
        P(expert_axes, (*dp_axes, "tensor"), None),
    )
    out_specs = P(dp_axes, "tensor", expert_axes, None)
    return jax.shard_map(
        on_device, mesh=fine, in_specs=in_specs, out_specs=out_specs, check_vma=False
    )
```

time: 324 us -> 186 us (0.57)
  waiting for transfers between devices: 124 us -> 21.4 us
  between operations: 14.3 us -> 0.18 us
  blocking collectives: 138 us -> 124 us
  starting transfers between devices: 26.2 us -> 18.6 us
  local copies, waits for them, and re-layouts: 6.22 us -> 2.88 us
    all_gather x2 -> x0, waiting for transfers between devices: 109 us -> none  [the longest x1 73.8 us: on_device(): rows_piece = lax.all_gather(compact, ('dp', 'tensor'), axis=0, tiled=True)]
    unnamed x1 -> x0, blocking collectives: 34.7 us -> none
    all_to_all x3 -> x6, blocking collectives: 103 us -> 124 us  [exchange(): return lax.all_to_all(value, axis, split_axis=0, concat_axis=0, tiled=True)]
    all_to_all x2 -> x1, starting transfers between devices: 23.9 us -> 14.6 us  [exchange(): return lax.all_to_all(value, axis, split_axis=0, concat_axis=0, tiled=True)]
    ppermute x0 -> x2, waiting for transfers between devices: none -> 4.4 us  [the longest x1 3 us: on_device(): other_rows = lax.ppermute(rows, 'core', swap)]
    ppermute x0 -> x2, starting transfers between devices: none -> 3.95 us  [the longest x1 2.04 us: on_device(): lax.ppermute(other_sum.astype(BF), 'core', swap).astype(F32)]
    dot_general x9 -> x10, matrix products: 13.8 us -> 16.3 us  [the longest x2 7.45 us: expert_part(): return jnp.dot(hidden, w_down[0], preferred_element_type=F32)]
    all_to_all x2 -> x1, waiting for transfers between devices: 14.8 us -> 17 us  [exchange(): return lax.all_to_all(value, axis, split_axis=0, concat_axis=0, tiled=True)]
  transfers between devices with their start and end apart: 5 -> 3, of which waited for: 4 -> 3; matrix products, arithmetic and copies ran while one was open for 2% -> 1% of each run, Pallas kernels for 0% -> 0%
where the time goes in v1:
time: 186 us; the launch traced here: 185 us
  blocking collectives  124 us (67%)
  waiting for transfers between devices  21.4 us (12%)
  starting transfers between devices  18.6 us (10%)
  matrix products  16.3 us (9%)
  local copies, waits for them, and re-layouts  2.88 us (2%)
    all_to_all x6, blocking collectives, exchange(): return lax.all_to_all(value, axis, split_axis=0, concat_axis=0, tiled=True)  124 us
    all_to_all x1, waiting for transfers between devices, exchange(): return lax.all_to_all(value, axis, split_axis=0, concat_axis=0, tiled=True)  17 us
    all_to_all x1, starting transfers between devices, exchange(): return lax.all_to_all(value, axis, split_axis=0, concat_axis=0, tiled=True)  14.6 us
    dot_general x2, matrix products, expert_part(): return jnp.dot(hidden, w_down[0], preferred_element_type=F32)  7.45 us
    dot_general x1, matrix products, on_device(): partial = jnp.dot(head_rows, out_proj, preferred_element_type=F32)  4.6 us
  transfers between devices with their start and end apart: 3, of which 3 were waited for; matrix products, arithmetic and copies ran while one was open for 1% of the time, Pallas kernels for 0%

profile of v1, /device:TPU:8, one launch (start us, length us, event | category | flops | bytes accessed | tf_op | source)
XLA Modules:
  0.0 185.0 jit_solution(11109528770960865427)
XLA Ops:
  0.0 0.0 copy-start
  0.0 0.9 dot_general.38
  0.9 0.0 copy-start.5
  0.9 4.6 %fusion.2 = bf16[4,6,5120]{2,1,0:T(8,128)(2,1)} fusion(bf16[4,6,640]{2,1,0:T(8,128)(2,1)S(1)} %dot_general.38, bf16[640,5120]{1,0:T(8,128)(2,1)} %param.9), kind=kOutput, calls=%fused_computation.5 | convolution fusion | flops 157409280 | bytes 6830080 | tf_op jit(solution)/shard_map/dot_general | solution.py:37
  5.5 0.0 copy-start.3
  5.5 0.0 copy-start.4
  5.5 14.6 %all-to-all-start = ((bf16[4,6,5120]{2,1,0:T(8,128)(2,1)}), bf16[4,6,5120]{2,1,0:T(8,128)(2,1)S(1)}, u32[]{:S(2)}, u32[]{:S(2)}) async-start(bf16[4,6,5120]{2,1,0:T(8,128)(2,1)} %fusion.2), calls=%async_computation | async-start | bytes 655360 | tf_op jit(solution)/shard_map/all_to_all | solution.py:12
  20.1 0.0 copy-done.5
  20.1 0.2 convert_reduce_fusion.2
  20.3 17.0 %all-to-all-done = bf16[4,6,5120]{2,1,0:T(8,128)(2,1)S(1)} async-done(((bf16[4,6,5120]{2,1,0:T(8,128)(2,1)}), bf16[4,6,5120]{2,1,0:T(8,128)(2,1)S(1)}, u32[]{:S(2)}, u32[]{:S(2)}) %all-to-all-start) | async-done | bytes 245792 | tf_op jit(solution)/shard_map/all_to_all | solution.py:12
  37.3 0.1 convert_reduce_fusion
  37.4 0.2 multiply_reduce_fusion
  37.6 0.0 copy-done.3
  37.6 0.0 copy-done.4
  37.6 0.4 fusion.27
  37.9 0.1 multiply_convert_fusion
  38.1 0.3 convolution_convert_fusion
  38.3 0.2 reshape.70
  38.5 23.6 %all_to_all.35 = bf16[24,2,5248]{2,1,0:T(2,128)(2,1)S(1)} all-to-all(bf16[24,2,5248]{2,1,0:T(2,128)(2,1)S(1)} %reshape.70), channel_id=1, replica_groups=mesh['x'=4,'core'=2,'tensor'=4,'y'=8,'w'=3] {'y','w'}, dimensions={0} | all-to-all | bytes 1007616 | tf_op jit(solution)/shard_map/all_to_all | solution.py:12
  62.1 0.2 reshape.71
  62.3 0.1 convert_reduce_fusion.1
  62.4 0.1 fusion.45
  62.5 0.1 select_reduce_fusion
  62.6 0.2 convolution_convert_fusion.4
  62.9 21.1 %all_to_all.36 = bf16[4,8,5120]{2,1,0:T(8,128)(2,1)S(1)} all-to-all(bf16[4,8,5120]{2,1,0:T(8,128)(2,1)S(1)} %broadcast_in_dim.58), channel_id=1, replica_groups=mesh['x'=4,'core'=2,'tensor'=4,'y'=8,'w'=3] {'tensor'}, dimensions={0} | all-to-all | bytes 655360 | tf_op jit(solution)/shard_map/all_to_all | solution.py:12
  83.9 0.1 broadcast_in_dim.60
  84.0 0.0 copy-start.1
  84.1 16.5 %all_to_all.37 = bf16[4,32,5120]{2,1,0:T(8,128)(2,1)S(1)} all-to-all(bf16[4,32,5120]{2,1,0:T(8,128)(2,1)S(1)} %broadcast_in_dim.60), channel_id=1, replica_groups=mesh['x'=4,'core'=2,'tensor'=4,'y'=8,'w'=3] {'x'}, dimensions={0} | all-to-all | bytes 2621440 | tf_op jit(solution)/shard_map/all_to_all | solution.py:12
  100.6 1.9 %collective-permute-start = (bf16[128,5120]{1,0:T(8,128)(2,1)S(1)}, bf16[128,5120]{1,0:T(8,128)(2,1)S(1)}, u32[]{:S(2)}, u32[]{:S(2)}) collective-permute-start(bf16[128,5120]{1,0:T(8,128)(2,1)S(1)} %bitcast.52), channel_id=1, source_target_pairs={{0,96},{96,0},{1,97},{97,1},{2,98},{98,2},{3,99},{99,3},{4,100},{1... | collective-permute-start | bytes 3932168 | tf_op jit(solution)/shard_map/ppermute | solution.py:69
  102.5 3.0 %collective-permute-done = bf16[128,5120]{1,0:T(8,128)(2,1)S(1)} collective-permute-done((bf16[128,5120]{1,0:T(8,128)(2,1)S(1)}, bf16[128,5120]{1,0:T(8,128)(2,1)S(1)}, u32[]{:S(2)}, u32[]{:S(2)}) %collective-permute-start) | collective-permute-done | bytes 1310752 | tf_op jit(solution)/shard_map/ppermute | solution.py:69
  105.5 0.0 copy-start.2
  105.5 1.1 copy-done.2
  106.6 0.0 copy-done.1
  106.6 0.5 fusion.11
  107.1 0.0 copy-done
  107.1 3.7 %convolution_convert_fusion.1 = bf16[128,5120]{1,0:T(8,128)(2,1)} fusion(bf16[1,128,5120]{2,1,0:T(8,128)(2,1)S(1)} %copy-done, f32[128,128]{1,0:T(8,128)S(1)} %fusion.11, bf16[128,5120]{1,0:T(8,128)(2,1)} %copy-done.2, bf16[1,5120,128]{2,1,0:T(8,128)(2,1)} %param.13), kind=kOutput, calls=%fused_computation.3 | convolution fusion | flops 336297984 | bytes 5308416 | tf_op jit(solution)/shard_map/dot_general | solution.py:75
  110.8 2.0 %collective-permute-start.1 = (bf16[128,5120]{1,0:T(8,128)(2,1)}, bf16[128,5120]{1,0:T(8,128)(2,1)}, u32[]{:S(2)}, u32[]{:S(2)}) collective-permute-start(bf16[128,5120]{1,0:T(8,128)(2,1)} %convolution_convert_fusion.1), channel_id=1, source_target_pairs={{0,96},{96,0},{1,97},{97,1},{2,98},{98,2},{3,99},{99,3},{4,100},{1... | collective-permute-start | bytes 3932168 | tf_op jit(solution)/shard_map/ppermute | solution.py:79
  112.9 1.8 fusion.17
  114.7 1.4 collective-permute-done.1
  116.1 3.7 %add_convert_fusion = bf16[128,5120]{1,0:T(8,128)(2,1)} fusion(bf16[128,5120]{1,0:T(8,128)(2,1)} %collective-permute-done.1, bf16[1,128,5120]{2,1,0:T(8,128)(2,1)S(1)} %copy-done, bf16[128,5120]{1,0:T(8,128)(2,1)S(1)} %bitcast.54, bf16[1,5120,128]{2,1,0:T(8,128)(2,1)} %param.14, f32[128,128]{1,0:T(8,128)S(1)} %fusion.17), kind=kOutput, calls=%fused_computation.9 | convolution fusion | flops 337608704 | bytes 6619136 | tf_op jit(solution)/shard_map/dot_general | solution.py:75
  119.8 22.0 %all_to_all.38 = bf16[4,32,5120]{2,1,0:T(8,128)(2,1)S(1)} all-to-all(bf16[4,32,5120]{2,1,0:T(8,128)(2,1)} %bitcast.55), channel_id=1, replica_groups=mesh['x'=4,'core'=2,'tensor'=4,'y'=8,'w'=3] {'x'}, dimensions={0} | all-to-all | bytes 2621440 | tf_op jit(solution)/shard_map/all_to_all | solution.py:12
  141.8 0.3 reduce_sum.74
  142.1 20.4 %all_to_all.39 = bf16[4,8,5120]{2,1,0:T(8,128)(2,1)S(1)} all-to-all(bf16[4,8,5120]{2,1,0:T(8,128)(2,1)S(1)} %bitcast.57), channel_id=1, replica_groups=mesh['x'=4,'core'=2,'tensor'=4,'y'=8,'w'=3] {'tensor'}, dimensions={0} | all-to-all | bytes 655360 | tf_op jit(solution)/shard_map/all_to_all | solution.py:12
  162.5 0.3 convolution_convert_fusion.2
  162.9 0.2 reshape.73
  163.1 20.8 %all_to_all.40 = bf16[24,2,5120]{2,1,0:T(2,128)(2,1)S(1)} all-to-all(bf16[24,2,5120]{2,1,0:T(2,128)(2,1)S(1)} %reshape.73), channel_id=1, replica_groups=mesh['x'=4,'core'=2,'tensor'=4,'y'=8,'w'=3] {'y','w'}, dimensions={0} | all-to-all | bytes 983040 | tf_op jit(solution)/shard_map/all_to_all | solution.py:12
  183.9 0.2 reshape.74
  184.1 0.9 fusion.5
  (6 shorter events, 0.1 us)
Async XLA Ops:
  0.0 107.1 %copy-start = (bf16[1,128,5120]{2,1,0:T(8,128)(2,1)S(1)}, bf16[1,128,5120]{2,1,0:T(8,128)(2,1)}, u32[]{:S(2)}) copy-start(bf16[1,128,5120]{2,1,0:T(8,128)(2,1)} %param.15) | copy-start | bytes 3932164
  0.9 19.2 %copy-start.5 = (s32[1,6,1]{1,2,0:T(1,128)S(1)}, s32[1,6,1]{1,2,0:T(1,128)}, u32[]{:S(2)}) copy-start(s32[1,6,1]{1,2,0:T(1,128)} %param.12) | copy-start | bytes 76
  5.5 32.1 %copy-start.3 = (bf16[5120,24]{0,1:T(8,128)(2,1)S(1)}, bf16[5120,24]{0,1:T(8,128)(2,1)}, u32[]{:S(2)}) copy-start(bf16[5120,24]{0,1:T(8,128)(2,1)} %param.11) | copy-start | bytes 737284
  5.5 32.1 %copy-start.4 = (f32[5120]{0:T(1024)S(1)}, f32[5120]{0:T(1024)}, u32[]{:S(2)}) copy-start(f32[5120]{0:T(1024)} %param.10) | copy-start | bytes 61444
  5.5 31.8 %all-to-all-start = ((bf16[4,6,5120]{2,1,0:T(8,128)(2,1)}), bf16[4,6,5120]{2,1,0:T(8,128)(2,1)S(1)}, u32[]{:S(2)}, u32[]{:S(2)}) async-start(bf16[4,6,5120]{2,1,0:T(8,128)(2,1)} %fusion.2), calls=%async_computation | async-start | bytes 655360 | tf_op jit(solution)/shard_map/all_to_all | solution.py:12
  84.0 22.5 %copy-start.1 = (bf16[1,5120,128]{2,1,0:T(8,128)(2,1)S(1)}, bf16[1,5120,128]{2,1,0:T(8,128)(2,1)}, u32[]{:S(2)}) copy-start(bf16[1,5120,128]{2,1,0:T(8,128)(2,1)} %param.14) | copy-start | bytes 3932164
  100.6 4.9 %collective-permute-start = (bf16[128,5120]{1,0:T(8,128)(2,1)S(1)}, bf16[128,5120]{1,0:T(8,128)(2,1)S(1)}, u32[]{:S(2)}, u32[]{:S(2)}) collective-permute-start(bf16[128,5120]{1,0:T(8,128)(2,1)S(1)} %bitcast.52), channel_id=1, source_target_pairs={{0,96},{96,0},{1,97},{97,1},{2,98},{98,2},{3,99},{99,3},{4,100},{1... | collective-permute-start | bytes 3932168 | tf_op jit(solution)/shard_map/ppermute | solution.py:69
  105.5 1.1 copy-start.2
  110.8 5.3 %collective-permute-start.1 = (bf16[128,5120]{1,0:T(8,128)(2,1)}, bf16[128,5120]{1,0:T(8,128)(2,1)}, u32[]{:S(2)}, u32[]{:S(2)}) collective-permute-start(bf16[128,5120]{1,0:T(8,128)(2,1)} %convolution_convert_fusion.1), channel_id=1, source_target_pairs={{0,96},{96,0},{1,97},{97,1},{2,98},{98,2},{3,99},{99,3},{4,100},{1... | collective-permute-start | bytes 3932168 | tf_op jit(solution)/shard_map/ppermute | solution.py:79

commit v2 on v1

--- a/solution.py
+++ b/solution.py
@@ -1,6 +1,8 @@
 import jax
 import jax.numpy as jnp
 from jax import lax
+from jax.experimental import pallas as pl
+from jax.experimental.pallas import tpu as pltpu
 from jax.sharding import Mesh, PartitionSpec as P
 
 BF = jnp.bfloat16
@@ -17,8 +19,67 @@
     return exchange(jnp.broadcast_to(value[None], (count,) + value.shape), axis)
 
 
-def total_over(partial, axis):
-    return jnp.sum(exchange(partial.astype(BF), axis).astype(F32), axis=0)
+def total_of(parts):
+    total = parts[0].astype(F32)
+    for index in range(1, parts.shape[0]):
+        total = total + parts[index].astype(F32)
+    return total
+
+
+def in_vmem(value):
+    return pltpu.with_memory_space_constraint(value, pltpu.VMEM)
+
+
+def local_call(kernel, shape, *operands):
+    whole = pl.BlockSpec(memory_space=pltpu.VMEM)
+    return pl.pallas_call(
+        kernel,
+        out_shape=pltpu.VMEM(shape, BF),
+        in_specs=[whole] * len(operands),
+        out_specs=whole,
+        compiler_params=pltpu.CompilerParams(vmem_limit_bytes=12 << 20),
+    )(*operands)
+
+
+def project_kernel(heads_ref, weight_ref, out_ref):
+    out_ref[...] = jnp.dot(heads_ref[...], weight_ref[...], preferred_element_type=F32).astype(BF)
+
+
+def project(heads, weight):
+    rows, depth = heads.shape
+    width = weight.shape[1]
+    block = 512
+    return pl.pallas_call(
+        project_kernel,
+        grid=(width // block,),
+        out_shape=pltpu.VMEM((rows, width), BF),
+        in_specs=[
+            pl.BlockSpec((rows, depth), lambda i: (0, 0)),
+            pl.BlockSpec((depth, block), lambda i: (0, i)),
+        ],
+        out_specs=pl.BlockSpec((rows, block), lambda i: (0, i)),
+    )(in_vmem(heads), pltpu.with_memory_space_constraint(weight, pltpu.HBM))
+
+
+def hidden_of(rows_ref, gate_ref, up_ref):
+    rows = rows_ref[...]
+    gate_value = jnp.dot(rows, gate_ref[...], preferred_element_type=F32)
+    up_value = jnp.dot(rows, up_ref[...], preferred_element_type=F32)
+    return (jax.nn.silu(gate_value) * up_value).astype(BF)
+
+
+def hidden_kernel(rows_ref, gate_ref, up_ref, out_ref):
+    out_ref[...] = hidden_of(rows_ref, gate_ref, up_ref)
+
+
+def expert_kernel(rows_ref, gate_ref, up_ref, down_ref, out_ref):
+    hidden = hidden_of(rows_ref, gate_ref, up_ref)
+    out_ref[...] = jnp.dot(hidden, down_ref[...], preferred_element_type=F32).astype(BF)
+
+
+def down_add_kernel(hidden_ref, down_ref, arrived_ref, out_ref):
+    own = jnp.dot(hidden_ref[...], down_ref[...], preferred_element_type=F32)
+    out_ref[...] = (own + arrived_ref[...].astype(F32)).astype(BF)
 
 
 def on_device(attn_heads, out_proj, norm_gain, router, expert_ids, w_gate, w_up, w_down):
@@ -34,8 +95,12 @@
     recv_cap = min(tok_rows + max(2, tok_rows // 5), send_cap * (expert_count - 2) + 2)
     slots = expert_count * send_cap
 
-    partial = jnp.dot(head_rows, out_proj, preferred_element_type=F32)
-    attended = total_over(partial.reshape(tensor_count, tok_rows, width), "tensor")
+    pad_rows = -(-tok_rows // 8) * 8
+    heads = head_rows.reshape(tensor_count, tok_rows, -1)
+    heads = jnp.pad(heads, ((0, 0), (0, pad_rows - tok_rows), (0, 0)))
+    partial = project(heads.reshape(tensor_count * pad_rows, -1), out_proj)
+    partial = exchange(partial.reshape(tensor_count, pad_rows, width), "tensor")
+    attended = total_of(partial)[:tok_rows]
 
     inverse = lax.rsqrt(jnp.mean(attended * attended, axis=-1, keepdims=True) + 1e-05)
     normed = attended * inverse * norm_gain
@@ -68,17 +133,19 @@
     rows = spread(rows, "x").reshape(x_count * tensor_count * recv_cap, width)
     other_rows = lax.ppermute(rows, "core", swap)
 
-    def expert_part(block):
-        gate_value = jnp.dot(block, w_gate[0], preferred_element_type=F32)
-        up_value = jnp.dot(block, w_up[0], preferred_element_type=F32)
-        hidden = (jax.nn.silu(gate_value) * up_value).astype(BF)
-        return jnp.dot(hidden, w_down[0], preferred_element_type=F32)
-
-    own_sum = expert_part(rows)
-    other_sum = expert_part(other_rows)
-    pair_sum = own_sum + lax.ppermute(other_sum.astype(BF), "core", swap).astype(F32)
-    plane_sum = total_over(pair_sum.reshape(x_count, tensor_count * recv_cap, width), "x")
-    expert_rows = total_over(plane_sum.reshape(tensor_count, recv_cap, width), "tensor").astype(BF)
+    gate, up, down = w_gate[0], w_up[0], w_down[0]
+    units = gate.shape[1]
+    own_hidden = local_call(hidden_kernel, (rows.shape[0], units), rows, gate, up)
+    own_hidden, other_rows = lax.optimization_barrier((own_hidden, other_rows))
+    other_sum = local_call(expert_kernel, rows.shape, other_rows, gate, up, down)
+    other_sum = lax.ppermute(other_sum, "core", swap)
+    pair_sum = local_call(down_add_kernel, rows.shape, own_hidden, down, other_sum)
+    plane_sum = total_of(
+        exchange(pair_sum.reshape(x_count, tensor_count * recv_cap, width), "x")
+    ).astype(BF)
+    expert_rows = total_of(
+        exchange(plane_sum.reshape(tensor_count, recv_cap, width), "tensor")
+    ).astype(BF)
 
     back = jnp.dot(selector.T, expert_rows, preferred_element_type=F32).astype(BF)
     returned = exchange(back.reshape(expert_count, send_cap, width), expert_axes)

time: 186 us -> 180 us (0.968)
  matrix products: 16.3 us -> 1.99 us
  Pallas kernels: 0 us -> 10.7 us
    dot_general x5 -> x0, matrix products: 14.3 us -> none  [the longest x2 7.45 us: expert_part(): return jnp.dot(hidden, w_down[0], preferred_element_type=F32)]
    pallas_call x0 -> x4, Pallas kernels: none -> 10.7 us  [the longest x1 8.05 us: project(): pl.pallas_call(project_kernel, grid=(width // block,), out_shape=pltpu.VM...]
  transfers between devices with their start and end apart: 3 -> 3, of which waited for: 3 -> 3; matrix products, arithmetic and copies ran while one was open for 1% -> 0% of each run, Pallas kernels for 0% -> 0%
where the time goes in v2:
time: 180 us
  blocking collectives  123 us (68%)
  waiting for transfers between devices  22 us (12%)
  starting transfers between devices  18.6 us (10%)
  Pallas kernels  10.7 us (6%)
  matrix products  1.99 us (1%)
    all_to_all x6, blocking collectives, exchange(): return lax.all_to_all(value, axis, split_axis=0, concat_axis=0, tiled=True)  123 us
    all_to_all x1, waiting for transfers between devices, exchange(): return lax.all_to_all(value, axis, split_axis=0, concat_axis=0, tiled=True)  17 us
    all_to_all x1, starting transfers between devices, exchange(): return lax.all_to_all(value, axis, split_axis=0, concat_axis=0, tiled=True)  14.6 us
    pallas_call x1, Pallas kernels, project(): pl.pallas_call(project_kernel, grid=(width // block,), out_shape=pltpu.VM...  8.05 us
  transfers between devices with their start and end apart: 3, of which 3 were waited for; matrix products, arithmetic and copies ran while one was open for 0% of the time, Pallas kernels for 0%

profile of v2, /device:TPU:8, one launch (start us, length us, event | category | flops | bytes accessed | tf_op | source)
XLA Modules:
  0.0 179.5 jit_solution(5273773699174232536)
XLA Ops:
  0.0 0.0 copy-start
  0.0 0.8 reshape_reshape.3
  0.8 0.0 copy-start.5
  0.8 8.0 %shard_map.82 = bf16[32,5120]{1,0:T(8,128)(2,1)} custom-call(bf16[32,640]{1,0:T(8,128)(2,1)S(1)} %pad_bitcast_fusion.heads_ref, bf16[640,5120]{1,0:T(8,128)(2,1)} %weight_ref.1), custom_call_target="tpu_custom_call" | custom-call | tf_op jit(solution)/shard_map/pallas_call | solution.py:52
  8.9 0.0 copy-start.4
  8.9 14.6 %all-to-all-start = ((bf16[4,8,5120]{2,1,0:T(8,128)(2,1)}), bf16[4,8,5120]{2,1,0:T(8,128)(2,1)S(1)}, u32[]{:S(2)}, u32[]{:S(2)}) async-start(bf16[4,8,5120]{2,1,0:T(8,128)(2,1)} %bitcast.2), calls=%async_computation | async-start | bytes 655360 | tf_op jit(solution)/shard_map/all_to_all | solution.py:14
  23.5 0.0 copy-done.5
  23.5 0.2 convert_reduce_fusion.1
  23.7 17.0 %all-to-all-done = bf16[4,8,5120]{2,1,0:T(8,128)(2,1)S(1)} async-done(((bf16[4,8,5120]{2,1,0:T(8,128)(2,1)}), bf16[4,8,5120]{2,1,0:T(8,128)(2,1)S(1)}, u32[]{:S(2)}, u32[]{:S(2)}) %all-to-all-start) | async-done | bytes 327712 | tf_op jit(solution)/shard_map/all_to_all | solution.py:14
  40.8 0.2 fusion.4
  40.9 0.0 copy-done
  40.9 0.0 copy-done.4
  41.0 0.4 fusion.1
  41.3 0.1 multiply_convert_fusion
  41.4 0.3 convolution_convert_fusion
  41.7 0.2 reshape.102
  41.9 23.6 %all_to_all.35 = bf16[24,2,5248]{2,1,0:T(2,128)(2,1)S(1)} all-to-all(bf16[24,2,5248]{2,1,0:T(2,128)(2,1)S(1)} %reshape.102), channel_id=1, replica_groups=mesh['x'=4,'core'=2,'tensor'=4,'y'=8,'w'=3] {'y','w'}, dimensions={0} | all-to-all | bytes 1007616 | tf_op jit(solution)/shard_map/all_to_all | solution.py:14
  65.5 0.2 reshape.103
  65.7 0.1 convert_reduce_fusion
  65.8 0.1 fusion.17
  65.9 0.1 select_reduce_fusion
  66.0 0.2 convolution_convert_fusion.3
  66.2 21.1 %all_to_all.36 = bf16[4,8,5120]{2,1,0:T(8,128)(2,1)S(1)} all-to-all(bf16[4,8,5120]{2,1,0:T(8,128)(2,1)S(1)} %broadcast_in_dim.58), channel_id=1, replica_groups=mesh['x'=4,'core'=2,'tensor'=4,'y'=8,'w'=3] {'tensor'}, dimensions={0} | all-to-all | bytes 655360 | tf_op jit(solution)/shard_map/all_to_all | solution.py:14
  87.3 0.1 broadcast_in_dim.60
  87.4 0.0 copy-start.1
  87.4 0.0 copy-start.2
  87.5 16.5 %all_to_all.37 = bf16[4,32,5120]{2,1,0:T(8,128)(2,1)S(1)} all-to-all(bf16[4,32,5120]{2,1,0:T(8,128)(2,1)S(1)} %broadcast_in_dim.60), channel_id=1, replica_groups=mesh['x'=4,'core'=2,'tensor'=4,'y'=8,'w'=3] {'x'}, dimensions={0} | all-to-all | bytes 2621440 | tf_op jit(solution)/shard_map/all_to_all | solution.py:14
  104.0 1.9 %collective-permute-start = (bf16[128,5120]{1,0:T(8,128)(2,1)S(1)}, bf16[128,5120]{1,0:T(8,128)(2,1)S(1)}, u32[]{:S(2)}, u32[]{:S(2)}) collective-permute-start(bf16[128,5120]{1,0:T(8,128)(2,1)S(1)} %bitcast.36), channel_id=1, source_target_pairs={{0,96},{96,0},{1,97},{97,1},{2,98},{98,2},{3,99},{99,3},{4,100},{1... | collective-permute-start | bytes 3932168 | tf_op jit(solution)/shard_map/ppermute | solution.py:134
  105.9 0.0 copy-done.1
  105.9 0.0 copy-done.2
  105.9 0.0 copy-start.3
  105.9 0.8 shard_map.83.hidden_ref
  106.8 2.1 %collective-permute-done.rows_ref = bf16[128,5120]{1,0:T(8,128)(2,1)S(1)} collective-permute-done((bf16[128,5120]{1,0:T(8,128)(2,1)S(1)}, bf16[128,5120]{1,0:T(8,128)(2,1)S(1)}, u32[]{:S(2)}, u32[]{:S(2)}) %collective-permute-start) | collective-permute-done | bytes 1310752 | tf_op jit(solution)/shard_map/ppermute | solution.py:134
  108.9 0.0 copy-done.3
  108.9 1.3 shard_map.84
  110.2 2.0 %collective-permute-start.1 = (bf16[128,5120]{1,0:T(8,128)(2,1)S(1)}, bf16[128,5120]{1,0:T(8,128)(2,1)S(1)}, u32[]{:S(2)}, u32[]{:S(2)}) collective-permute-start(bf16[128,5120]{1,0:T(8,128)(2,1)S(1)} %shard_map.84), channel_id=1, source_target_pairs={{0,96},{96,0},{1,97},{97,1},{2,98},{98,2},{3,99},{99,3},{4,100},{1... | collective-permute-start | bytes 3932168 | tf_op jit(solution)/shard_map/ppermute | solution.py:141
  112.2 2.9 %collective-permute-done.1.arrived_ref = bf16[128,5120]{1,0:T(8,128)(2,1)S(1)} collective-permute-done((bf16[128,5120]{1,0:T(8,128)(2,1)S(1)}, bf16[128,5120]{1,0:T(8,128)(2,1)S(1)}, u32[]{:S(2)}, u32[]{:S(2)}) %collective-permute-start.1) | collective-permute-done | bytes 1310752 | tf_op jit(solution)/shard_map/ppermute | solution.py:141
  115.1 0.5 shard_map.85
  115.6 20.9 %all_to_all.38 = bf16[4,32,5120]{2,1,0:T(8,128)(2,1)S(1)} all-to-all(bf16[4,32,5120]{2,1,0:T(8,128)(2,1)S(1)} %bitcast.38), channel_id=1, replica_groups=mesh['x'=4,'core'=2,'tensor'=4,'y'=8,'w'=3] {'x'}, dimensions={0} | all-to-all | bytes 2621440 | tf_op jit(solution)/shard_map/all_to_all | solution.py:14
  136.5 0.2 fusion.3
  136.7 16.1 %all_to_all.39 = bf16[4,8,5120]{2,1,0:T(8,128)(2,1)S(1)} all-to-all(bf16[4,8,5120]{2,1,0:T(8,128)(2,1)S(1)} %fusion.3), channel_id=1, replica_groups=mesh['x'=4,'core'=2,'tensor'=4,'y'=8,'w'=3] {'tensor'}, dimensions={0} | all-to-all | bytes 655360 | tf_op jit(solution)/shard_map/all_to_all | solution.py:14
  152.8 0.3 convolution_convert_fusion.1
  153.1 0.2 reshape.106
  153.3 25.1 %all_to_all.40 = bf16[24,2,5120]{2,1,0:T(2,128)(2,1)S(1)} all-to-all(bf16[24,2,5120]{2,1,0:T(2,128)(2,1)S(1)} %reshape.106), channel_id=1, replica_groups=mesh['x'=4,'core'=2,'tensor'=4,'y'=8,'w'=3] {'y','w'}, dimensions={0} | all-to-all | bytes 983040 | tf_op jit(solution)/shard_map/all_to_all | solution.py:14
  178.4 0.2 reshape.107
  178.6 0.9 fusion
  (7 shorter events, 0.1 us)
Async XLA Ops:
  0.0 40.9 %copy-start = (bf16[5120,24]{0,1:T(8,128)(2,1)S(1)}, bf16[5120,24]{0,1:T(8,128)(2,1)}, u32[]{:S(2)}) copy-start(bf16[5120,24]{0,1:T(8,128)(2,1)} %param.11) | copy-start | bytes 737284
  0.8 22.7 %copy-start.5 = (s32[1,6,1]{1,2,0:T(1,128)S(1)}, s32[1,6,1]{1,2,0:T(1,128)}, u32[]{:S(2)}) copy-start(s32[1,6,1]{1,2,0:T(1,128)} %param.12) | copy-start | bytes 76
  8.9 32.1 %copy-start.4 = (f32[5120]{0:T(1024)S(1)}, f32[5120]{0:T(1024)}, u32[]{:S(2)}) copy-start(f32[5120]{0:T(1024)} %param.10) | copy-start | bytes 61444
  8.9 31.8 %all-to-all-start = ((bf16[4,8,5120]{2,1,0:T(8,128)(2,1)}), bf16[4,8,5120]{2,1,0:T(8,128)(2,1)S(1)}, u32[]{:S(2)}, u32[]{:S(2)}) async-start(bf16[4,8,5120]{2,1,0:T(8,128)(2,1)} %bitcast.2), calls=%async_computation | async-start | bytes 655360 | tf_op jit(solution)/shard_map/all_to_all | solution.py:14
  87.4 18.5 %copy-start.1 = (bf16[1,5120,128]{2,1,0:T(8,128)(2,1)S(1)}, bf16[1,5120,128]{2,1,0:T(8,128)(2,1)}, u32[]{:S(2)}) copy-start(bf16[1,5120,128]{2,1,0:T(8,128)(2,1)} %param.13) | copy-start | bytes 3932164
  87.4 18.5 %copy-start.2 = (bf16[1,5120,128]{2,1,0:T(8,128)(2,1)S(1)}, bf16[1,5120,128]{2,1,0:T(8,128)(2,1)}, u32[]{:S(2)}) copy-start(bf16[1,5120,128]{2,1,0:T(8,128)(2,1)} %param.14) | copy-start | bytes 3932164
  104.0 4.9 %collective-permute-start = (bf16[128,5120]{1,0:T(8,128)(2,1)S(1)}, bf16[128,5120]{1,0:T(8,128)(2,1)S(1)}, u32[]{:S(2)}, u32[]{:S(2)}) collective-permute-start(bf16[128,5120]{1,0:T(8,128)(2,1)S(1)} %bitcast.36), channel_id=1, source_target_pairs={{0,96},{96,0},{1,97},{97,1},{2,98},{98,2},{3,99},{99,3},{4,100},{1... | collective-permute-start | bytes 3932168 | tf_op jit(solution)/shard_map/ppermute | solution.py:134
  105.9 3.0 %copy-start.3 = (bf16[1,128,5120]{2,1,0:T(8,128)(2,1)S(1)}, bf16[1,128,5120]{2,1,0:T(8,128)(2,1)}, u32[]{:S(2)}) copy-start(bf16[1,128,5120]{2,1,0:T(8,128)(2,1)} %param.15) | copy-start | bytes 3932164
  110.2 4.9 %collective-permute-start.1 = (bf16[128,5120]{1,0:T(8,128)(2,1)S(1)}, bf16[128,5120]{1,0:T(8,128)(2,1)S(1)}, u32[]{:S(2)}, u32[]{:S(2)}) collective-permute-start(bf16[128,5120]{1,0:T(8,128)(2,1)S(1)} %shard_map.84), channel_id=1, source_target_pairs={{0,96},{96,0},{1,97},{97,1},{2,98},{98,2},{3,99},{99,3},{4,100},{1... | collective-permute-start | bytes 3932168 | tf_op jit(solution)/shard_map/ppermute | solution.py:141

commit v3 on v2

--- a/solution.py
+++ b/solution.py
@@ -1,3 +1,5 @@
+import functools
+
 import jax
 import jax.numpy as jnp
 from jax import lax
@@ -32,53 +34,87 @@
 
 def local_call(kernel, shape, *operands):
     whole = pl.BlockSpec(memory_space=pltpu.VMEM)
+    scalars = pl.BlockSpec(memory_space=pltpu.SMEM)
     return pl.pallas_call(
         kernel,
         out_shape=pltpu.VMEM(shape, BF),
-        in_specs=[whole] * len(operands),
+        in_specs=[whole if operand.dtype == BF else scalars for operand in operands],
         out_specs=whole,
         compiler_params=pltpu.CompilerParams(vmem_limit_bytes=12 << 20),
     )(*operands)
 
 
-def project_kernel(heads_ref, weight_ref, out_ref):
-    out_ref[...] = jnp.dot(heads_ref[...], weight_ref[...], preferred_element_type=F32).astype(BF)
+def project_kernel(chunks, heads_ref, weight_ref, out_ref, held, sems):
+    depth = weight_ref.shape[0] // chunks
+    copies = []
+    for i in range(chunks):
+        rows = pl.ds(i * depth, depth)
+        copies.append(pltpu.make_async_copy(weight_ref.at[rows], held.at[rows], sems.at[i]))
+        copies[i].start()
+    total = jnp.zeros(out_ref.shape, F32)
+    for i in range(chunks):
+        copies[i].wait()
+        span = slice(i * depth, (i + 1) * depth)
+        total = total + jnp.dot(heads_ref[:, span], held[span], preferred_element_type=F32)
+    out_ref[...] = total.astype(BF)
 
 
 def project(heads, weight):
-    rows, depth = heads.shape
-    width = weight.shape[1]
-    block = 512
+    chunks = weight.shape[0] // LANES
+    whole = pl.BlockSpec(memory_space=pltpu.VMEM)
     return pl.pallas_call(
-        project_kernel,
-        grid=(width // block,),
-        out_shape=pltpu.VMEM((rows, width), BF),
-        in_specs=[
-            pl.BlockSpec((rows, depth), lambda i: (0, 0)),
-            pl.BlockSpec((depth, block), lambda i: (0, i)),
-        ],
-        out_specs=pl.BlockSpec((rows, block), lambda i: (0, i)),
-    )(in_vmem(heads), pltpu.with_memory_space_constraint(weight, pltpu.HBM))
-
-
-def hidden_of(rows_ref, gate_ref, up_ref):
+        functools.partial(project_kernel, chunks),
+        out_shape=pltpu.VMEM((heads.shape[0], weight.shape[1]), BF),
+        in_specs=[whole, pl.BlockSpec(memory_space=pl.ANY)],
+        out_specs=whole,
+        scratch_shapes=[pltpu.VMEM(weight.shape, BF), pltpu.SemaphoreType.DMA((chunks,))],
+        compiler_params=pltpu.CompilerParams(vmem_limit_bytes=14 << 20),
+    )(heads, pltpu.with_memory_space_constraint(weight, pltpu.HBM))
+
+
+def hidden_of(planes, rows_ref, gate_ref, up_ref):
     rows = rows_ref[...]
     gate_value = jnp.dot(rows, gate_ref[...], preferred_element_type=F32)
     up_value = jnp.dot(rows, up_ref[...], preferred_element_type=F32)
-    return (jax.nn.silu(gate_value) * up_value).astype(BF)
-
-
-def hidden_kernel(rows_ref, gate_ref, up_ref, out_ref):
-    out_ref[...] = hidden_of(rows_ref, gate_ref, up_ref)
-
-
-def expert_kernel(rows_ref, gate_ref, up_ref, down_ref, out_ref):
-    hidden = hidden_of(rows_ref, gate_ref, up_ref)
-    out_ref[...] = jnp.dot(hidden, down_ref[...], preferred_element_type=F32).astype(BF)
-
-
-def down_add_kernel(hidden_ref, down_ref, arrived_ref, out_ref):
-    own = jnp.dot(hidden_ref[...], down_ref[...], preferred_element_type=F32)
+    hidden = jax.nn.silu(gate_value) * up_value
+    x_count, tensor_count = planes
+    cap = hidden.shape[0] // (x_count * tensor_count)
+    order = [x * tensor_count + t for t in range(tensor_count) for x in range(x_count)]
+    return jnp.concatenate([hidden[k * cap : (k + 1) * cap] for k in order], axis=0).astype(BF)
+
+
+def own_kernel(planes, rows_ref, gate_ref, up_ref, out_ref):
+    out_ref[...] = hidden_of(planes, rows_ref, gate_ref, up_ref)
+
+
+def both_kernel(planes, own_ref, rows_ref, gate_ref, up_ref, out_ref):
+    half = own_ref.shape[0]
+    other = hidden_of(planes, rows_ref, gate_ref, up_ref)
+    for peer in range(planes[0]):
+        out_ref[peer, :half] = own_ref[...]
+        out_ref[peer, half:] = other
+
+
+def down_of(start, stop, source_ref, hidden_ref, down_refs):
+    total = None
+    for index, down_ref in enumerate(down_refs):
+        part = jnp.dot(
+            hidden_ref[source_ref[index], start:stop], down_ref[...], preferred_element_type=F32
+        )
+        total = part if total is None else total + part
+    return total
+
+
+def other_down_kernel(source_ref, hidden_ref, *refs):
+    *down_refs, out_ref = refs
+    rows = out_ref.shape[0]
+    out_ref[...] = down_of(rows, 2 * rows, source_ref, hidden_ref, down_refs).astype(BF)
+
+
+def own_down_kernel(source_ref, hidden_ref, arrived_ref, *refs):
+    *down_refs, out_ref = refs
+    rows = out_ref.shape[0]
+    own = down_of(0, rows, source_ref, hidden_ref, down_refs)
     out_ref[...] = (own + arrived_ref[...].astype(F32)).astype(BF)
 
 
@@ -119,7 +155,19 @@
     placing = (slot_range[:, None] == slot_index[None, :]).astype(BF)
     flagged = jnp.concatenate([routed, jnp.ones((tok_rows, LANES), BF)], axis=1)
     outgoing = jnp.dot(placing, flagged, preferred_element_type=F32).astype(BF)
+    place = lax.axis_index("x")
+    columns = width // x_count
+    outgoing, down = lax.optimization_barrier((outgoing, w_down[0]))
+    sources, downs = [place], [lax.dynamic_slice_in_dim(down, place * columns, columns, 1)]
+    for step in range(1, x_count):
+        to = (place + step) % x_count
+        piece = lax.dynamic_slice_in_dim(down, to * columns, columns, 1)
+        ring = [(i, (i + step) % x_count) for i in range(x_count)]
+        sources.append((place + x_count - step) % x_count)
+        downs.append(lax.ppermute(piece, "x", ring))
+    sources = jnp.stack(sources).astype(jnp.int32)
     arrived = exchange(outgoing.reshape(expert_count, send_cap, width + LANES), expert_axes)
+    arrived, downs = lax.optimization_barrier((arrived, downs))
     arrived = arrived.reshape(slots, width + LANES)
 
     filled = arrived[:, width].astype(F32)
@@ -133,19 +181,33 @@
     rows = spread(rows, "x").reshape(x_count * tensor_count * recv_cap, width)
     other_rows = lax.ppermute(rows, "core", swap)
 
-    gate, up, down = w_gate[0], w_up[0], w_down[0]
+    gate, up = w_gate[0], w_up[0]
     units = gate.shape[1]
-    own_hidden = local_call(hidden_kernel, (rows.shape[0], units), rows, gate, up)
+    half = rows.shape[0]
+    planes = (x_count, tensor_count)
+    own_hidden = local_call(
+        functools.partial(own_kernel, planes), (half, units), rows, gate, up
+    )
     own_hidden, other_rows = lax.optimization_barrier((own_hidden, other_rows))
-    other_sum = local_call(expert_kernel, rows.shape, other_rows, gate, up, down)
+    hidden = local_call(
+        functools.partial(both_kernel, planes),
+        (x_count, 2 * half, units),
+        own_hidden,
+        other_rows,
+        gate,
+        up,
+    )
+    hidden = exchange(hidden, "x")
+    other_sum = local_call(other_down_kernel, (half, columns), sources, hidden, *downs)
     other_sum = lax.ppermute(other_sum, "core", swap)
-    pair_sum = local_call(down_add_kernel, rows.shape, own_hidden, down, other_sum)
-    plane_sum = total_of(
-        exchange(pair_sum.reshape(x_count, tensor_count * recv_cap, width), "x")
+    pair_sum = local_call(
+        own_down_kernel, (half, columns), sources, hidden, other_sum, *downs
+    )
+    column_sum = total_of(
+        exchange(pair_sum.reshape(tensor_count, x_count * recv_cap, columns), "tensor")
     ).astype(BF)
-    expert_rows = total_of(
-        exchange(plane_sum.reshape(tensor_count, recv_cap, width), "tensor")
-    ).astype(BF)
+    expert_rows = exchange(column_sum.reshape(x_count, recv_cap, columns), "x")
+    expert_rows = expert_rows.transpose(1, 0, 2).reshape(recv_cap, width)
 
     back = jnp.dot(selector.T, expert_rows, preferred_element_type=F32).astype(BF)
     returned = exchange(back.reshape(expert_count, send_cap, width), expert_axes)

time: 180 us -> 185 us (1.028)
  blocking collectives: 123 us -> 90.4 us
  starting transfers between devices: 18.6 us -> 42.3 us
  waiting for transfers between devices: 22 us -> 37.3 us
  Pallas kernels: 10.7 us -> 8.38 us
    all_to_all x6 -> x5, blocking collectives: 123 us -> 90.4 us  [exchange(): return lax.all_to_all(value, axis, split_axis=0, concat_axis=0, tiled=True)]
    all_to_all x1 -> x3, starting transfers between devices: 14.6 us -> 27.1 us  [exchange(): return lax.all_to_all(value, axis, split_axis=0, concat_axis=0, tiled=True)]
    ppermute x0 -> x3, starting transfers between devices: none -> 11.4 us  [on_device(): downs.append(lax.ppermute(piece, 'x', ring))]
    ppermute x0 -> x3, waiting for transfers between devices: none -> 9.46 us  [on_device(): downs.append(lax.ppermute(piece, 'x', ring))]
    all_to_all x1 -> x3, waiting for transfers between devices: 17 us -> 24.2 us  [exchange(): return lax.all_to_all(value, axis, split_axis=0, concat_axis=0, tiled=True)]
    pallas_call x4 -> x5, Pallas kernels: 10.7 us -> 8.38 us  [the longest x4 4.41 us: local_call(): pl.pallas_call(kernel, out_shape=pltpu.VMEM(shape, BF), in_specs=[whole i...]
  transfers between devices with their start and end apart: 3 -> 8, of which waited for: 3 -> 7; matrix products, arithmetic and copies ran while one was open for 0% -> 0% of each run, Pallas kernels for 0% -> 0%
where the time goes in v3:
time: 185 us; the launch traced here: 184 us
  blocking collectives  90.4 us (49%)
  starting transfers between devices  42.3 us (23%)
  waiting for transfers between devices  37.3 us (20%)
  Pallas kernels  8.38 us (5%)
  local copies, waits for them, and re-layouts  2.7 us (1%)
  matrix products  1.99 us (1%)
    all_to_all x5, blocking collectives, exchange(): return lax.all_to_all(value, axis, split_axis=0, concat_axis=0, tiled=True)  90.4 us
    all_to_all x3, starting transfers between devices, exchange(): return lax.all_to_all(value, axis, split_axis=0, concat_axis=0, tiled=True)  27.1 us
    all_to_all x3, waiting for transfers between devices, exchange(): return lax.all_to_all(value, axis, split_axis=0, concat_axis=0, tiled=True)  24.2 us
    ppermute x3, starting transfers between devices, on_device(): downs.append(lax.ppermute(piece, 'x', ring))  11.4 us
    ppermute x3, waiting for transfers between devices, on_device(): downs.append(lax.ppermute(piece, 'x', ring))  9.46 us
    pallas_call x4, Pallas kernels, local_call(): pl.pallas_call(kernel, out_shape=pltpu.VMEM(shape, BF), in_specs=[whole i...  4.41 us
    pallas_call x1, Pallas kernels, project(): pl.pallas_call(functools.partial(project_kernel, chunks), out_shape=pltpu...  3.97 us
  transfers between devices with their start and end apart: 8, of which 7 were waited for; matrix products, arithmetic and copies ran while one was open for 0% of the time, Pallas kernels for 0%

profile of v3, /device:TPU:8, one launch (start us, length us, event | category | flops | bytes accessed | tf_op | source)
XLA Modules:
  0.0 184.4 jit_solution(8887792969237459160)
XLA Ops:
  0.0 0.8 reshape_reshape.3
  0.8 0.0 copy-start.5
  0.8 4.0 %shard_map.82 = bf16[32,5120]{1,0:T(8,128)(2,1)} custom-call(bf16[32,640]{1,0:T(8,128)(2,1)S(1)} %pad_bitcast_fusion.heads_ref, bf16[640,5120]{1,0:T(8,128)(2,1)} %weight_ref.1), custom_call_target="tpu_custom_call" | custom-call | tf_op jit(solution)/shard_map/pallas_call | solution.py:65
  4.8 0.0 copy-start.4
  4.8 14.5 %all-to-all-start = ((bf16[4,8,5120]{2,1,0:T(8,128)(2,1)}), bf16[4,8,5120]{2,1,0:T(8,128)(2,1)S(1)}, u32[]{:S(2)}, u32[]{:S(2)}) async-start(bf16[4,8,5120]{2,1,0:T(8,128)(2,1)} %bitcast.2), calls=%async_computation | async-start | bytes 655360 | tf_op jit(solution)/shard_map/all_to_all | solution.py:16
  19.4 0.2 convert_reduce_fusion.1
  19.5 17.0 %all-to-all-done = bf16[4,8,5120]{2,1,0:T(8,128)(2,1)S(1)} async-done(((bf16[4,8,5120]{2,1,0:T(8,128)(2,1)}), bf16[4,8,5120]{2,1,0:T(8,128)(2,1)S(1)}, u32[]{:S(2)}, u32[]{:S(2)}) %all-to-all-start) | async-done | bytes 327712 | tf_op jit(solution)/shard_map/all_to_all | solution.py:16
  36.6 0.2 fusion.3
  36.8 0.4 fusion.1
  37.2 0.1 multiply_convert_fusion
  37.3 0.0 copy-start.3
  37.3 0.3 convolution_convert_fusion
  37.6 1.0 reshape.97
  38.5 9.2 %all-to-all-start.1 = ((bf16[24,2,5248]{2,1,0:T(2,128)(2,1)}), bf16[24,2,5248]{2,1,0:T(2,128)(2,1)S(1)}, u32[]{:S(2)}, u32[]{:S(2)}) async-start(bf16[24,2,5248]{2,1,0:T(2,128)(2,1)} %reshape.97), calls=%async_computation.1 | async-start | bytes 1007616 | tf_op jit(solution)/shard_map/all_to_all | solution.py:16
  47.8 0.1 constant_dynamic-slice_fusion
  47.9 3.4 %collective-permute-start = (bf16[128,1280]{1,0:T(8,128)(2,1)S(1)}, bf16[128,1280]{1,0:T(8,128)(2,1)S(1)}, u32[]{:S(2)}, u32[]{:S(2)}) collective-permute-start(bf16[128,1280]{1,0:T(8,128)(2,1)S(1)} %get-tuple-element.25), channel_id=1, source_target_pairs={{0,192},{192,384},{384,576},{576,0},{1,193},{193,385},{385,577},{5... | collective-permute-start | bytes 983048 | tf_op jit(solution)/shard_map/ppermute | solution.py:167
  51.3 4.7 %collective-permute-start.1 = (bf16[128,1280]{1,0:T(8,128)(2,1)S(1)}, bf16[128,1280]{1,0:T(8,128)(2,1)S(1)}, u32[]{:S(2)}, u32[]{:S(2)}) collective-permute-start(bf16[128,1280]{1,0:T(8,128)(2,1)S(1)} %get-tuple-element.24), channel_id=1, source_target_pairs={{0,384},{192,576},{384,0},{576,192},{1,385},{193,577},{385,1},{577... | collective-permute-start | bytes 983048 | tf_op jit(solution)/shard_map/ppermute | solution.py:167
  56.0 3.3 %collective-permute-start.2 = (bf16[128,1280]{1,0:T(8,128)(2,1)S(1)}, bf16[128,1280]{1,0:T(8,128)(2,1)S(1)}, u32[]{:S(2)}, u32[]{:S(2)}) collective-permute-start(bf16[128,1280]{1,0:T(8,128)(2,1)S(1)} %get-tuple-element.23), channel_id=1, source_target_pairs={{0,576},{192,0},{384,192},{576,384},{1,577},{193,1},{385,193},{577... | collective-permute-start | bytes 983048 | tf_op jit(solution)/shard_map/ppermute | solution.py:167
  59.3 1.4 collective-permute-done.refs_1_
  60.7 6.6 %collective-permute-done.1.refs_2_ = bf16[128,1280]{1,0:T(8,128)(2,1)S(1)} collective-permute-done((bf16[128,1280]{1,0:T(8,128)(2,1)S(1)}, bf16[128,1280]{1,0:T(8,128)(2,1)S(1)}, u32[]{:S(2)}, u32[]{:S(2)}) %collective-permute-start.1) | collective-permute-done | bytes 327712 | tf_op jit(solution)/shard_map/ppermute | solution.py:167
  67.3 1.5 collective-permute-done.2.refs_3_
  68.8 0.2 reshape.98
  69.0 0.1 convert_reduce_fusion
  69.1 0.1 fusion.11
  69.2 0.1 select_reduce_fusion
  69.3 0.2 convolution_convert_fusion.3
  69.5 21.1 %all_to_all.40 = bf16[4,8,5120]{2,1,0:T(8,128)(2,1)S(1)} all-to-all(bf16[4,8,5120]{2,1,0:T(8,128)(2,1)S(1)} %broadcast_in_dim.58), channel_id=1, replica_groups=mesh['x'=4,'core'=2,'tensor'=4,'y'=8,'w'=3] {'tensor'}, dimensions={0} | all-to-all | bytes 655360 | tf_op jit(solution)/shard_map/all_to_all | solution.py:16
  90.7 0.1 broadcast_in_dim.60
  90.8 0.0 copy-start.1
  90.8 17.1 %all_to_all.41 = bf16[4,32,5120]{2,1,0:T(8,128)(2,1)S(1)} all-to-all(bf16[4,32,5120]{2,1,0:T(8,128)(2,1)S(1)} %broadcast_in_dim.60), channel_id=1, replica_groups=mesh['x'=4,'core'=2,'tensor'=4,'y'=8,'w'=3] {'x'}, dimensions={0} | all-to-all | bytes 2621440 | tf_op jit(solution)/shard_map/all_to_all | solution.py:16
  107.9 1.9 %collective-permute-start.3 = (bf16[128,5120]{1,0:T(8,128)(2,1)S(1)}, bf16[128,5120]{1,0:T(8,128)(2,1)S(1)}, u32[]{:S(2)}, u32[]{:S(2)}) collective-permute-start(bf16[128,5120]{1,0:T(8,128)(2,1)S(1)} %bitcast.45), channel_id=1, source_target_pairs={{0,96},{96,0},{1,97},{97,1},{2,98},{98,2},{3,99},{99,3},{4,100},{1... | collective-permute-start | bytes 3932168 | tf_op jit(solution)/shard_map/ppermute | solution.py:182
  109.9 0.8 shard_map.83.own_ref
  110.7 2.1 %collective-permute-done.3.rows_ref = bf16[128,5120]{1,0:T(8,128)(2,1)S(1)} collective-permute-done((bf16[128,5120]{1,0:T(8,128)(2,1)S(1)}, bf16[128,5120]{1,0:T(8,128)(2,1)S(1)}, u32[]{:S(2)}, u32[]{:S(2)}) %collective-permute-start.3) | collective-permute-done | bytes 1310752 | tf_op jit(solution)/shard_map/ppermute | solution.py:182
  112.9 1.5 shard_map.84
  114.4 3.4 %all-to-all-start.4 = ((bf16[4,256,128]{2,1,0:T(8,128)(2,1)}), bf16[4,256,128]{2,1,0:T(8,128)(2,1)S(1)}, u32[]{:S(2)}, u32[]{:S(2)}) async-start(bf16[4,256,128]{2,1,0:T(8,128)(2,1)} %shard_map.84), calls=%async_computation.4 | async-start | bytes 524288 | tf_op jit(solution)/shard_map/all_to_all | solution.py:16
  117.8 0.1 pad_add_fusion.source_ref
  117.9 7.1 %all-to-all-done.4.hidden_ref = bf16[4,256,128]{2,1,0:T(8,128)(2,1)S(1)} async-done(((bf16[4,256,128]{2,1,0:T(8,128)(2,1)}), bf16[4,256,128]{2,1,0:T(8,128)(2,1)S(1)}, u32[]{:S(2)}, u32[]{:S(2)}) %all-to-all-start.4) | async-done | bytes 262176 | tf_op jit(solution)/shard_map/all_to_all | solution.py:16
  125.0 1.0 shard_map.85
  126.0 1.9 %collective-permute-start.4 = (bf16[128,1280]{1,0:T(8,128)(2,1)S(1)}, bf16[128,1280]{1,0:T(8,128)(2,1)S(1)}, u32[]{:S(2)}, u32[]{:S(2)}) collective-permute-start(bf16[128,1280]{1,0:T(8,128)(2,1)S(1)} %shard_map.85), channel_id=1, source_target_pairs={{0,96},{96,0},{1,97},{97,1},{2,98},{98,2},{3,99},{99,3},{4,100},{1... | collective-permute-start | bytes 983048 | tf_op jit(solution)/shard_map/ppermute | solution.py:202
  128.0 1.6 collective-permute-done.4.arrived_ref
  129.6 1.0 shard_map.86
  130.6 15.2 %all_to_all.42 = bf16[4,32,1280]{2,1,0:T(8,128)(2,1)S(1)} all-to-all(bf16[4,32,1280]{2,1,0:T(8,128)(2,1)S(1)} %bitcast.47), channel_id=1, replica_groups=mesh['x'=4,'core'=2,'tensor'=4,'y'=8,'w'=3] {'tensor'}, dimensions={0} | all-to-all | bytes 655360 | tf_op jit(solution)/shard_map/all_to_all | solution.py:16
  145.9 8.1 %all_to_all.43 = bf16[4,8,1280]{2,1,0:T(8,128)(2,1)S(1)} all-to-all(bf16[4,8,1280]{2,1,0:T(8,128)(2,1)S(1)} %fusion.8), channel_id=1, replica_groups=mesh['x'=4,'core'=2,'tensor'=4,'y'=8,'w'=3] {'x'}, dimensions={0} | all-to-all | bytes 163840 | tf_op jit(solution)/shard_map/all_to_all | solution.py:16
  154.0 0.3 convolution_convert_fusion.1
  154.3 0.2 reshape.102
  154.5 28.9 %all_to_all.44 = bf16[24,2,5120]{2,1,0:T(2,128)(2,1)S(1)} all-to-all(bf16[24,2,5120]{2,1,0:T(2,128)(2,1)S(1)} %reshape.102), channel_id=1, replica_groups=mesh['x'=4,'core'=2,'tensor'=4,'y'=8,'w'=3] {'y','w'}, dimensions={0} | all-to-all | bytes 983040 | tf_op jit(solution)/shard_map/all_to_all | solution.py:16
  183.4 0.2 reshape.103
  183.5 0.9 fusion
  (17 shorter events, 0.2 us)
Async XLA Ops:
  0.0 36.8 %copy-start = (bf16[5120,24]{0,1:T(8,128)(2,1)S(1)}, bf16[5120,24]{0,1:T(8,128)(2,1)}, u32[]{:S(2)}) copy-start(bf16[5120,24]{0,1:T(8,128)(2,1)} %param.11) | copy-start | bytes 737284
  0.8 18.5 %copy-start.5 = (s32[1,6,1]{1,2,0:T(1,128)S(1)}, s32[1,6,1]{1,2,0:T(1,128)}, u32[]{:S(2)}) copy-start(s32[1,6,1]{1,2,0:T(1,128)} %param.12) | copy-start | bytes 76
  4.8 31.9 %copy-start.4 = (f32[5120]{0:T(1024)S(1)}, f32[5120]{0:T(1024)}, u32[]{:S(2)}) copy-start(f32[5120]{0:T(1024)} %param.10) | copy-start | bytes 61444
  4.8 31.7 %all-to-all-start = ((bf16[4,8,5120]{2,1,0:T(8,128)(2,1)}), bf16[4,8,5120]{2,1,0:T(8,128)(2,1)S(1)}, u32[]{:S(2)}, u32[]{:S(2)}) async-start(bf16[4,8,5120]{2,1,0:T(8,128)(2,1)} %bitcast.2), calls=%async_computation | async-start | bytes 655360 | tf_op jit(solution)/shard_map/all_to_all | solution.py:16
  37.3 10.5 %copy-start.3 = (bf16[1,128,5120]{2,1,0:T(8,128)(2,1)S(1)}, bf16[1,128,5120]{2,1,0:T(8,128)(2,1)}, u32[]{:S(2)}) copy-start(bf16[1,128,5120]{2,1,0:T(8,128)(2,1)} %param.15) | copy-start | bytes 3932164
  38.5 30.3 %all-to-all-start.1 = ((bf16[24,2,5248]{2,1,0:T(2,128)(2,1)}), bf16[24,2,5248]{2,1,0:T(2,128)(2,1)S(1)}, u32[]{:S(2)}, u32[]{:S(2)}) async-start(bf16[24,2,5248]{2,1,0:T(2,128)(2,1)} %reshape.97), calls=%async_computation.1 | async-start | bytes 1007616 | tf_op jit(solution)/shard_map/all_to_all | solution.py:16
  47.9 12.8 %collective-permute-start = (bf16[128,1280]{1,0:T(8,128)(2,1)S(1)}, bf16[128,1280]{1,0:T(8,128)(2,1)S(1)}, u32[]{:S(2)}, u32[]{:S(2)}) collective-permute-start(bf16[128,1280]{1,0:T(8,128)(2,1)S(1)} %get-tuple-element.25), channel_id=1, source_target_pairs={{0,192},{192,384},{384,576},{576,0},{1,193},{193,385},{385,577},{5... | collective-permute-start | bytes 983048 | tf_op jit(solution)/shard_map/ppermute | solution.py:167
  51.3 15.9 %collective-permute-start.1 = (bf16[128,1280]{1,0:T(8,128)(2,1)S(1)}, bf16[128,1280]{1,0:T(8,128)(2,1)S(1)}, u32[]{:S(2)}, u32[]{:S(2)}) collective-permute-start(bf16[128,1280]{1,0:T(8,128)(2,1)S(1)} %get-tuple-element.24), channel_id=1, source_target_pairs={{0,384},{192,576},{384,0},{576,192},{1,385},{193,577},{385,1},{577... | collective-permute-start | bytes 983048 | tf_op jit(solution)/shard_map/ppermute | solution.py:167
  56.0 12.8 %collective-permute-start.2 = (bf16[128,1280]{1,0:T(8,128)(2,1)S(1)}, bf16[128,1280]{1,0:T(8,128)(2,1)S(1)}, u32[]{:S(2)}, u32[]{:S(2)}) collective-permute-start(bf16[128,1280]{1,0:T(8,128)(2,1)S(1)} %get-tuple-element.23), channel_id=1, source_target_pairs={{0,576},{192,0},{384,192},{576,384},{1,577},{193,1},{385,193},{577... | collective-permute-start | bytes 983048 | tf_op jit(solution)/shard_map/ppermute | solution.py:167
  90.8 19.1 %copy-start.1 = (bf16[1,5120,128]{2,1,0:T(8,128)(2,1)S(1)}, bf16[1,5120,128]{2,1,0:T(8,128)(2,1)}, u32[]{:S(2)}) copy-start(bf16[1,5120,128]{2,1,0:T(8,128)(2,1)} %param.13) | copy-start | bytes 3932164
  90.8 19.1 %copy-start.2 = (bf16[1,5120,128]{2,1,0:T(8,128)(2,1)S(1)}, bf16[1,5120,128]{2,1,0:T(8,128)(2,1)}, u32[]{:S(2)}) copy-start(bf16[1,5120,128]{2,1,0:T(8,128)(2,1)} %param.14) | copy-start | bytes 3932164
  107.9 4.9 %collective-permute-start.3 = (bf16[128,5120]{1,0:T(8,128)(2,1)S(1)}, bf16[128,5120]{1,0:T(8,128)(2,1)S(1)}, u32[]{:S(2)}, u32[]{:S(2)}) collective-permute-start(bf16[128,5120]{1,0:T(8,128)(2,1)S(1)} %bitcast.45), channel_id=1, source_target_pairs={{0,96},{96,0},{1,97},{97,1},{2,98},{98,2},{3,99},{99,3},{4,100},{1... | collective-permute-start | bytes 3932168 | tf_op jit(solution)/shard_map/ppermute | solution.py:182
  114.4 10.6 %all-to-all-start.4 = ((bf16[4,256,128]{2,1,0:T(8,128)(2,1)}), bf16[4,256,128]{2,1,0:T(8,128)(2,1)S(1)}, u32[]{:S(2)}, u32[]{:S(2)}) async-start(bf16[4,256,128]{2,1,0:T(8,128)(2,1)} %shard_map.84), calls=%async_computation.4 | async-start | bytes 524288 | tf_op jit(solution)/shard_map/all_to_all | solution.py:16
  126.0 3.5 %collective-permute-start.4 = (bf16[128,1280]{1,0:T(8,128)(2,1)S(1)}, bf16[128,1280]{1,0:T(8,128)(2,1)S(1)}, u32[]{:S(2)}, u32[]{:S(2)}) collective-permute-start(bf16[128,1280]{1,0:T(8,128)(2,1)S(1)} %shard_map.85), channel_id=1, source_target_pairs={{0,96},{96,0},{1,97},{97,1},{2,98},{98,2},{3,99},{99,3},{4,100},{1... | collective-permute-start | bytes 983048 | tf_op jit(solution)/shard_map/ppermute | solution.py:202

commit v4 on v2

--- a/solution.py
+++ b/solution.py
@@ -1,3 +1,5 @@
+import functools
+
 import jax
 import jax.numpy as jnp
 from jax import lax
@@ -37,49 +39,52 @@
         out_shape=pltpu.VMEM(shape, BF),
         in_specs=[whole] * len(operands),
         out_specs=whole,
-        compiler_params=pltpu.CompilerParams(vmem_limit_bytes=12 << 20),
+        compiler_params=pltpu.CompilerParams(vmem_limit_bytes=14 << 20),
     )(*operands)
 
 
-def project_kernel(heads_ref, weight_ref, out_ref):
-    out_ref[...] = jnp.dot(heads_ref[...], weight_ref[...], preferred_element_type=F32).astype(BF)
+def project_kernel(chunks, heads_ref, weight_ref, out_ref, held, sems):
+    depth = weight_ref.shape[0] // chunks
+    copies = []
+    for i in range(chunks):
+        rows = pl.ds(i * depth, depth)
+        copies.append(pltpu.make_async_copy(weight_ref.at[rows], held.at[rows], sems.at[i]))
+        copies[i].start()
+    total = jnp.zeros(out_ref.shape, F32)
+    for i in range(chunks):
+        copies[i].wait()
+        span = slice(i * depth, (i + 1) * depth)
+        total = total + jnp.dot(heads_ref[:, span], held[span], preferred_element_type=F32)
+    out_ref[...] = total.astype(BF)
 
 
 def project(heads, weight):
-    rows, depth = heads.shape
-    width = weight.shape[1]
-    block = 512
+    chunks = weight.shape[0] // LANES
+    whole = pl.BlockSpec(memory_space=pltpu.VMEM)
     return pl.pallas_call(
-        project_kernel,
-        grid=(width // block,),
-        out_shape=pltpu.VMEM((rows, width), BF),
-        in_specs=[
-            pl.BlockSpec((rows, depth), lambda i: (0, 0)),
-            pl.BlockSpec((depth, block), lambda i: (0, i)),
-        ],
-        out_specs=pl.BlockSpec((rows, block), lambda i: (0, i)),
-    )(in_vmem(heads), pltpu.with_memory_space_constraint(weight, pltpu.HBM))
+        functools.partial(project_kernel, chunks),
+        out_shape=pltpu.VMEM((heads.shape[0], weight.shape[1]), BF),
+        in_specs=[whole, pl.BlockSpec(memory_space=pl.ANY)],
+        out_specs=whole,
+        scratch_shapes=[pltpu.VMEM(weight.shape, BF), pltpu.SemaphoreType.DMA((chunks,))],
+        compiler_params=pltpu.CompilerParams(vmem_limit_bytes=14 << 20),
+    )(heads, pltpu.with_memory_space_constraint(weight, pltpu.HBM))
 
 
-def hidden_of(rows_ref, gate_ref, up_ref):
+def expert_kernel(rows_ref, *refs):
+    *weight_refs, out_ref = refs
     rows = rows_ref[...]
-    gate_value = jnp.dot(rows, gate_ref[...], preferred_element_type=F32)
-    up_value = jnp.dot(rows, up_ref[...], preferred_element_type=F32)
-    return (jax.nn.silu(gate_value) * up_value).astype(BF)
-
-
-def hidden_kernel(rows_ref, gate_ref, up_ref, out_ref):
-    out_ref[...] = hidden_of(rows_ref, gate_ref, up_ref)
-
-
-def expert_kernel(rows_ref, gate_ref, up_ref, down_ref, out_ref):
-    hidden = hidden_of(rows_ref, gate_ref, up_ref)
-    out_ref[...] = jnp.dot(hidden, down_ref[...], preferred_element_type=F32).astype(BF)
-
-
-def down_add_kernel(hidden_ref, down_ref, arrived_ref, out_ref):
-    own = jnp.dot(hidden_ref[...], down_ref[...], preferred_element_type=F32)
-    out_ref[...] = (own + arrived_ref[...].astype(F32)).astype(BF)
+    hiddens = []
+    for gate_ref, up_ref in (weight_refs[0:2], weight_refs[3:5]):
+        gate_value = jnp.dot(rows, gate_ref[...], preferred_element_type=F32)
+        up_value = jnp.dot(rows, up_ref[...], preferred_element_type=F32)
+        hiddens.append((jax.nn.silu(gate_value) * up_value).astype(BF))
+    block = 1280
+    for start in range(0, out_ref.shape[1], block):
+        span = slice(start, start + block)
+        total = jnp.dot(hiddens[0], weight_refs[2][:, span], preferred_element_type=F32)
+        total = total + jnp.dot(hiddens[1], weight_refs[5][:, span], preferred_element_type=F32)
+        out_ref[:, span] = total.astype(BF)
 
 
 def on_device(attn_heads, out_proj, norm_gain, router, expert_ids, w_gate, w_up, w_down):
@@ -119,7 +124,11 @@
     placing = (slot_range[:, None] == slot_index[None, :]).astype(BF)
     flagged = jnp.concatenate([routed, jnp.ones((tok_rows, LANES), BF)], axis=1)
     outgoing = jnp.dot(placing, flagged, preferred_element_type=F32).astype(BF)
+    own = [weight[0] for weight in (w_gate, w_up, w_down)]
+    outgoing, own = lax.optimization_barrier((outgoing, own))
+    other = [lax.ppermute(weight, "core", swap) for weight in own]
     arrived = exchange(outgoing.reshape(expert_count, send_cap, width + LANES), expert_axes)
+    arrived, other = lax.optimization_barrier((arrived, other))
     arrived = arrived.reshape(slots, width + LANES)
 
     filled = arrived[:, width].astype(F32)
@@ -131,15 +140,7 @@
 
     rows = spread(compact, "tensor").reshape(tensor_count * recv_cap, width)
     rows = spread(rows, "x").reshape(x_count * tensor_count * recv_cap, width)
-    other_rows = lax.ppermute(rows, "core", swap)
-
-    gate, up, down = w_gate[0], w_up[0], w_down[0]
-    units = gate.shape[1]
-    own_hidden = local_call(hidden_kernel, (rows.shape[0], units), rows, gate, up)
-    own_hidden, other_rows = lax.optimization_barrier((own_hidden, other_rows))
-    other_sum = local_call(expert_kernel, rows.shape, other_rows, gate, up, down)
-    other_sum = lax.ppermute(other_sum, "core", swap)
-    pair_sum = local_call(down_add_kernel, rows.shape, own_hidden, down, other_sum)
+    pair_sum = local_call(expert_kernel, rows.shape, rows, *own, *other)
     plane_sum = total_of(
         exchange(pair_sum.reshape(x_count, tensor_count * recv_cap, width), "x")
     ).astype(BF)

time: 180 us -> 169 us (0.939)
  blocking collectives: 123 us -> 99.6 us
  starting transfers between devices: 18.6 us -> 30 us
  local copies, waits for them, and re-layouts: 1.78 us -> 6.83 us
  Pallas kernels: 10.7 us -> 6.27 us
    all_to_all x6 -> x5, blocking collectives: 123 us -> 99.6 us  [exchange(): return lax.all_to_all(value, axis, split_axis=0, concat_axis=0, tiled=True)]
    all_to_all x1 -> x2, starting transfers between devices: 14.6 us -> 23.7 us  [exchange(): return lax.all_to_all(value, axis, split_axis=0, concat_axis=0, tiled=True)]
    all_to_all x1 -> x2, waiting for transfers between devices: 17 us -> 21.1 us  [exchange(): return lax.all_to_all(value, axis, split_axis=0, concat_axis=0, tiled=True)]
    pallas_call x1, Pallas kernels: 8.05 us -> 3.97 us  [project(): pl.pallas_call(functools.partial(project_kernel, chunks), out_shape=pltpu...]
    ppermute x2 -> x3, waiting for transfers between devices: 5 us -> 1.05 us  [on_device(): other = [lax.ppermute(weight, 'core', swap) for weight in own]]
    unnamed x12 -> x24, local copies, waits for them, and re-layouts: 0.03 us -> 3.26 us
    ppermute x2 -> x3, starting transfers between devices: 3.96 us -> 6.25 us  [on_device(): other = [lax.ppermute(weight, 'core', swap) for weight in own]]
  transfers between devices with their start and end apart: 3 -> 5, of which waited for: 3 -> 3; matrix products, arithmetic and copies ran while one was open for 0% -> 0% of each run, Pallas kernels for 0% -> 0%
where the time goes in v4:
time: 169 us; the launch traced here: 168 us
  blocking collectives  99.6 us (59%)
  starting transfers between devices  30 us (18%)
  waiting for transfers between devices  22.2 us (13%)
  local copies, waits for them, and re-layouts  6.83 us (4%)
  Pallas kernels  6.27 us (4%)
  matrix products  1.99 us (1%)
    all_to_all x5, blocking collectives, exchange(): return lax.all_to_all(value, axis, split_axis=0, concat_axis=0, tiled=True)  99.6 us
    all_to_all x2, starting transfers between devices, exchange(): return lax.all_to_all(value, axis, split_axis=0, concat_axis=0, tiled=True)  23.7 us
    all_to_all x2, waiting for transfers between devices, exchange(): return lax.all_to_all(value, axis, split_axis=0, concat_axis=0, tiled=True)  21.1 us
    ppermute x3, starting transfers between devices, on_device(): other = [lax.ppermute(weight, 'core', swap) for weight in own]  6.25 us
    pallas_call x1, Pallas kernels, project(): pl.pallas_call(functools.partial(project_kernel, chunks), out_shape=pltpu...  3.97 us
  transfers between devices with their start and end apart: 5, of which 3 were waited for; matrix products, arithmetic and copies ran while one was open for 0% of the time, Pallas kernels for 0%

profile of v4, /device:TPU:8, one launch (start us, length us, event | category | flops | bytes accessed | tf_op | source)
XLA Modules:
  0.0 168.1 jit_solution(3631816354542754466)
XLA Ops:
  0.0 0.0 copy-start
  0.0 0.8 reshape_reshape.3
  0.8 0.0 copy-start.11
  0.8 4.0 %shard_map.82 = bf16[32,5120]{1,0:T(8,128)(2,1)} custom-call(bf16[32,640]{1,0:T(8,128)(2,1)S(1)} %pad_bitcast_fusion.heads_ref, bf16[640,5120]{1,0:T(8,128)(2,1)} %weight_ref.1), custom_call_target="tpu_custom_call" | custom-call | tf_op jit(solution)/shard_map/pallas_call | solution.py:64
  4.8 0.0 copy-start.10
  4.8 14.5 %all-to-all-start = ((bf16[4,8,5120]{2,1,0:T(8,128)(2,1)}), bf16[4,8,5120]{2,1,0:T(8,128)(2,1)S(1)}, u32[]{:S(2)}, u32[]{:S(2)}) async-start(bf16[4,8,5120]{2,1,0:T(8,128)(2,1)} %bitcast.2), calls=%async_computation | async-start | bytes 655360 | tf_op jit(solution)/shard_map/all_to_all | solution.py:16
  19.4 0.0 copy-done.11
  19.4 0.2 convert_reduce_fusion.1
  19.5 17.0 %all-to-all-done = bf16[4,8,5120]{2,1,0:T(8,128)(2,1)S(1)} async-done(((bf16[4,8,5120]{2,1,0:T(8,128)(2,1)}), bf16[4,8,5120]{2,1,0:T(8,128)(2,1)S(1)}, u32[]{:S(2)}, u32[]{:S(2)}) %all-to-all-start) | async-done | bytes 327712 | tf_op jit(solution)/shard_map/all_to_all | solution.py:16
  36.6 0.2 fusion.4
  36.8 0.0 copy-done
  36.8 0.0 copy-done.10
  36.8 0.4 fusion.1
  37.2 0.0 copy-start.2
  37.2 0.1 multiply_convert_fusion
  37.3 0.0 copy-start.1
  37.3 0.3 convolution_convert_fusion
  37.6 1.0 reshape.102
  38.5 9.2 %all-to-all-start.1 = ((bf16[24,2,5248]{2,1,0:T(2,128)(2,1)}), bf16[24,2,5248]{2,1,0:T(2,128)(2,1)}, u32[]{:S(2)}, u32[]{:S(2)}) async-start(bf16[24,2,5248]{2,1,0:T(2,128)(2,1)} %reshape.102), calls=%async_computation.1 | async-start | bytes 1007616 | tf_op jit(solution)/shard_map/all_to_all | solution.py:16
  47.8 0.0 copy-done.1
  47.8 1.9 %collective-permute-start = (bf16[5120,128]{1,0:T(8,128)(2,1)S(1)}, bf16[5120,128]{1,0:T(8,128)(2,1)S(1)}, u32[]{:S(2)}, u32[]{:S(2)}) collective-permute-start(bf16[5120,128]{1,0:T(8,128)(2,1)S(1)} %bitcast.38), channel_id=1, source_target_pairs={{0,96},{96,0},{1,97},{97,1},{2,98},{98,2},{3,99},{99,3},{4,100},{1... | collective-permute-start | bytes 3932168 | tf_op jit(solution)/shard_map/ppermute | solution.py:129
  49.7 2.4 %collective-permute-start.1 = (bf16[5120,128]{1,0:T(8,128)(2,1)S(1)}, bf16[5120,128]{1,0:T(8,128)(2,1)S(1)}, u32[]{:S(2)}, u32[]{:S(2)}) collective-permute-start(bf16[5120,128]{1,0:T(8,128)(2,1)S(1)} %bitcast.40), channel_id=1, source_target_pairs={{0,96},{96,0},{1,97},{97,1},{2,98},{98,2},{3,99},{99,3},{4,100},{1... | collective-permute-start | bytes 3932168 | tf_op jit(solution)/shard_map/ppermute | solution.py:129
  52.1 1.9 %collective-permute-start.2 = (bf16[128,5120]{1,0:T(8,128)(2,1)}, bf16[128,5120]{1,0:T(8,128)(2,1)S(1)}, u32[]{:S(2)}, u32[]{:S(2)}) collective-permute-start(bf16[128,5120]{1,0:T(8,128)(2,1)} %bitcast.42), channel_id=1, source_target_pairs={{0,96},{96,0},{1,97},{97,1},{2,98},{98,2},{3,99},{99,3},{4,100},{1... | collective-permute-start | bytes 3932168 | tf_op jit(solution)/shard_map/ppermute | solution.py:129
  54.1 0.0 collective-permute-done.refs_3_
  54.1 1.1 copy-done.4
  55.1 0.0 collective-permute-done.1.refs_4_
  55.1 1.1 copy-done.6
  56.2 1.0 collective-permute-done.2.refs_5_
  57.3 1.1 copy-done.8
  58.3 4.1 %all-to-all-done.1 = bf16[24,2,5248]{2,1,0:T(2,128)(2,1)} async-done(((bf16[24,2,5248]{2,1,0:T(2,128)(2,1)}), bf16[24,2,5248]{2,1,0:T(2,128)(2,1)}, u32[]{:S(2)}, u32[]{:S(2)}) %all-to-all-start.1) | async-done | bytes 503840 | tf_op jit(solution)/shard_map/all_to_all | solution.py:16
  62.4 1.2 reshape.103
  63.7 0.1 convert_reduce_fusion
  63.8 0.1 fusion.17
  63.9 0.1 select_reduce_fusion
  64.0 0.2 convolution_convert_fusion.3
  64.2 21.2 %all_to_all.35 = bf16[4,8,5120]{2,1,0:T(8,128)(2,1)S(1)} all-to-all(bf16[4,8,5120]{2,1,0:T(8,128)(2,1)S(1)} %broadcast_in_dim.58), channel_id=1, replica_groups=mesh['x'=4,'core'=2,'tensor'=4,'y'=8,'w'=3] {'tensor'}, dimensions={0} | all-to-all | bytes 655360 | tf_op jit(solution)/shard_map/all_to_all | solution.py:16
  85.4 0.1 broadcast_in_dim.60
  85.5 0.0 copy-start.3
  85.6 17.1 %all_to_all.36 = bf16[4,32,5120]{2,1,0:T(8,128)(2,1)S(1)} all-to-all(bf16[4,32,5120]{2,1,0:T(8,128)(2,1)S(1)} %broadcast_in_dim.60), channel_id=1, replica_groups=mesh['x'=4,'core'=2,'tensor'=4,'y'=8,'w'=3] {'x'}, dimensions={0} | all-to-all | bytes 2621440 | tf_op jit(solution)/shard_map/all_to_all | solution.py:16
  102.7 2.3 %shard_map.83 = bf16[128,5120]{1,0:T(8,128)(2,1)S(1)} custom-call(bf16[128,5120]{1,0:T(8,128)(2,1)S(1)} %bitcast.36, bf16[5120,128]{1,0:T(8,128)(2,1)S(1)} %bitcast.39, bf16[5120,128]{1,0:T(8,128)(2,1)S(1)} %bitcast.41, bf16[128,5120]{1,0:T(8,128)(2,1)S(1)} %bitcast.43, bf16[5120,128]{1,0:T(8,128)(2,1)S(1)} %copy-done.5, bf16[5120,128]{1,0:T(8,128)(2,1)S(1)} %copy-done.7, ...), custom_call_target="tpu_custom_call" | custom-call | tf_op jit(solution)/shard_map/pallas_call | solution.py:37
  105.0 14.7 %all_to_all.37 = bf16[4,32,5120]{2,1,0:T(8,128)(2,1)S(1)} all-to-all(bf16[4,32,5120]{2,1,0:T(8,128)(2,1)S(1)} %bitcast.37), channel_id=1, replica_groups=mesh['x'=4,'core'=2,'tensor'=4,'y'=8,'w'=3] {'x'}, dimensions={0} | all-to-all | bytes 2621440 | tf_op jit(solution)/shard_map/all_to_all | solution.py:16
  119.7 0.2 fusion.3
  119.9 14.3 %all_to_all.38 = bf16[4,8,5120]{2,1,0:T(8,128)(2,1)S(1)} all-to-all(bf16[4,8,5120]{2,1,0:T(8,128)(2,1)S(1)} %fusion.3), channel_id=1, replica_groups=mesh['x'=4,'core'=2,'tensor'=4,'y'=8,'w'=3] {'tensor'}, dimensions={0} | all-to-all | bytes 655360 | tf_op jit(solution)/shard_map/all_to_all | solution.py:16
  134.2 0.3 convolution_convert_fusion.1
  134.5 0.2 reshape.106
  134.7 32.3 %all_to_all.39 = bf16[24,2,5120]{2,1,0:T(2,128)(2,1)S(1)} all-to-all(bf16[24,2,5120]{2,1,0:T(2,128)(2,1)S(1)} %reshape.106), channel_id=1, replica_groups=mesh['x'=4,'core'=2,'tensor'=4,'y'=8,'w'=3] {'y','w'}, dimensions={0} | all-to-all | bytes 983040 | tf_op jit(solution)/shard_map/all_to_all | solution.py:16
  167.0 0.2 reshape.107
  167.2 0.9 fusion
  (18 shorter events, 0.1 us)
Async XLA Ops:
  0.0 36.8 %copy-start = (bf16[5120,24]{0,1:T(8,128)(2,1)S(1)}, bf16[5120,24]{0,1:T(8,128)(2,1)}, u32[]{:S(2)}) copy-start(bf16[5120,24]{0,1:T(8,128)(2,1)} %param.11) | copy-start | bytes 737284
  0.8 18.5 %copy-start.11 = (s32[1,6,1]{1,2,0:T(1,128)S(1)}, s32[1,6,1]{1,2,0:T(1,128)}, u32[]{:S(2)}) copy-start(s32[1,6,1]{1,2,0:T(1,128)} %param.12) | copy-start | bytes 76
  4.8 31.9 %copy-start.10 = (f32[5120]{0:T(1024)S(1)}, f32[5120]{0:T(1024)}, u32[]{:S(2)}) copy-start(f32[5120]{0:T(1024)} %param.10) | copy-start | bytes 61444
  4.8 31.7 %all-to-all-start = ((bf16[4,8,5120]{2,1,0:T(8,128)(2,1)}), bf16[4,8,5120]{2,1,0:T(8,128)(2,1)S(1)}, u32[]{:S(2)}, u32[]{:S(2)}) async-start(bf16[4,8,5120]{2,1,0:T(8,128)(2,1)} %bitcast.2), calls=%async_computation | async-start | bytes 655360 | tf_op jit(solution)/shard_map/all_to_all | solution.py:16
  37.2 12.5 %copy-start.2 = (bf16[1,5120,128]{2,1,0:T(8,128)(2,1)S(1)}, bf16[1,5120,128]{2,1,0:T(8,128)(2,1)}, u32[]{:S(2)}) copy-start(bf16[1,5120,128]{2,1,0:T(8,128)(2,1)} %param.14) | copy-start | bytes 3932164
  37.3 10.5 %copy-start.1 = (bf16[1,5120,128]{2,1,0:T(8,128)(2,1)S(1)}, bf16[1,5120,128]{2,1,0:T(8,128)(2,1)}, u32[]{:S(2)}) copy-start(bf16[1,5120,128]{2,1,0:T(8,128)(2,1)} %param.13) | copy-start | bytes 3932164
  38.5 23.9 %all-to-all-start.1 = ((bf16[24,2,5248]{2,1,0:T(2,128)(2,1)}), bf16[24,2,5248]{2,1,0:T(2,128)(2,1)}, u32[]{:S(2)}, u32[]{:S(2)}) async-start(bf16[24,2,5248]{2,1,0:T(2,128)(2,1)} %reshape.102), calls=%async_computation.1 | async-start | bytes 1007616 | tf_op jit(solution)/shard_map/all_to_all | solution.py:16
  47.8 6.3 %collective-permute-start = (bf16[5120,128]{1,0:T(8,128)(2,1)S(1)}, bf16[5120,128]{1,0:T(8,128)(2,1)S(1)}, u32[]{:S(2)}, u32[]{:S(2)}) collective-permute-start(bf16[5120,128]{1,0:T(8,128)(2,1)S(1)} %bitcast.38), channel_id=1, source_target_pairs={{0,96},{96,0},{1,97},{97,1},{2,98},{98,2},{3,99},{99,3},{4,100},{1... | collective-permute-start | bytes 3932168 | tf_op jit(solution)/shard_map/ppermute | solution.py:129
  49.7 5.4 %collective-permute-start.1 = (bf16[5120,128]{1,0:T(8,128)(2,1)S(1)}, bf16[5120,128]{1,0:T(8,128)(2,1)S(1)}, u32[]{:S(2)}, u32[]{:S(2)}) collective-permute-start(bf16[5120,128]{1,0:T(8,128)(2,1)S(1)} %bitcast.40), channel_id=1, source_target_pairs={{0,96},{96,0},{1,97},{97,1},{2,98},{98,2},{3,99},{99,3},{4,100},{1... | collective-permute-start | bytes 3932168 | tf_op jit(solution)/shard_map/ppermute | solution.py:129
  52.1 5.1 %collective-permute-start.2 = (bf16[128,5120]{1,0:T(8,128)(2,1)}, bf16[128,5120]{1,0:T(8,128)(2,1)S(1)}, u32[]{:S(2)}, u32[]{:S(2)}) collective-permute-start(bf16[128,5120]{1,0:T(8,128)(2,1)} %bitcast.42), channel_id=1, source_target_pairs={{0,96},{96,0},{1,97},{97,1},{2,98},{98,2},{3,99},{99,3},{4,100},{1... | collective-permute-start | bytes 3932168 | tf_op jit(solution)/shard_map/ppermute | solution.py:129
  54.1 1.1 copy-start.4
  55.1 1.1 copy-start.6
  57.3 1.1 copy-start.8
  64.2 38.5 %copy-start.9 = (bf16[128,5120]{1,0:T(8,128)(2,1)S(1)}, bf16[128,5120]{1,0:T(8,128)(2,1)}, u32[]{:S(2)}) copy-start(bf16[128,5120]{1,0:T(8,128)(2,1)} %copy-done.8) | copy-start | bytes 3932164
  85.4 17.2 %copy-start.7 = (bf16[5120,128]{1,0:T(8,128)(2,1)S(1)}, bf16[5120,128]{1,0:T(8,128)(2,1)}, u32[]{:S(2)}) copy-start(bf16[5120,128]{1,0:T(8,128)(2,1)} %copy-done.6) | copy-start | bytes 3932164
  85.5 17.1 %copy-start.3 = (bf16[1,128,5120]{2,1,0:T(8,128)(2,1)S(1)}, bf16[1,128,5120]{2,1,0:T(8,128)(2,1)}, u32[]{:S(2)}) copy-start(bf16[1,128,5120]{2,1,0:T(8,128)(2,1)} %param.15) | copy-start | bytes 3932164
  85.6 17.1 %copy-start.5 = (bf16[5120,128]{1,0:T(8,128)(2,1)S(1)}, bf16[5120,128]{1,0:T(8,128)(2,1)}, u32[]{:S(2)}) copy-start(bf16[5120,128]{1,0:T(8,128)(2,1)} %copy-done.4) | copy-start | bytes 3932164

commit v5 on v4

--- a/solution.py
+++ b/solution.py
@@ -43,32 +43,96 @@
     )(*operands)
 
 
-def project_kernel(chunks, heads_ref, weight_ref, out_ref, held, sems):
+def folds(tok_rows, width):
+    wide = tok_rows * width // 8
+    rest = width - wide
+    each = wide // rest
+    return wide, [(k, tok_rows + k // each, k % each * rest) for k in range(tok_rows)]
+
+
+def project_kernel(chunks, tok_rows, heads_ref, weight_ref, out_ref, held, packed, sems):
     depth = weight_ref.shape[0] // chunks
+    width = weight_ref.shape[1]
     copies = []
     for i in range(chunks):
         rows = pl.ds(i * depth, depth)
         copies.append(pltpu.make_async_copy(weight_ref.at[rows], held.at[rows], sems.at[i]))
         copies[i].start()
-    total = jnp.zeros(out_ref.shape, F32)
+    total = jnp.zeros((heads_ref.shape[0], width), F32)
     for i in range(chunks):
         copies[i].wait()
         span = slice(i * depth, (i + 1) * depth)
         total = total + jnp.dot(heads_ref[:, span], held[span], preferred_element_type=F32)
-    out_ref[...] = total.astype(BF)
-
-
-def project(heads, weight):
+    wide, places = folds(tok_rows, width)
+    for peer in range(heads_ref.shape[0] // tok_rows):
+        token = peer * tok_rows
+        packed[8 * peer : 8 * peer + tok_rows] = total[token : token + tok_rows, :wide]
+        for k, row, column in places:
+            packed[8 * peer + row : 8 * peer + row + 1, column : column + width - wide] = total[
+                token + k : token + k + 1, wide:
+            ]
+    out_ref[...] = packed[...].astype(BF)
+
+
+def project(heads, weight, tok_rows):
     chunks = weight.shape[0] // LANES
+    wide, _ = folds(tok_rows, weight.shape[1])
+    packed_shape = (heads.shape[0] // tok_rows * 8, wide)
     whole = pl.BlockSpec(memory_space=pltpu.VMEM)
     return pl.pallas_call(
-        functools.partial(project_kernel, chunks),
-        out_shape=pltpu.VMEM((heads.shape[0], weight.shape[1]), BF),
+        functools.partial(project_kernel, chunks, tok_rows),
+        out_shape=pltpu.VMEM(packed_shape, BF),
         in_specs=[whole, pl.BlockSpec(memory_space=pl.ANY)],
         out_specs=whole,
-        scratch_shapes=[pltpu.VMEM(weight.shape, BF), pltpu.SemaphoreType.DMA((chunks,))],
+        scratch_shapes=[
+            pltpu.VMEM(weight.shape, BF),
+            pltpu.VMEM(packed_shape, F32),
+            pltpu.SemaphoreType.DMA((chunks,)),
+        ],
         compiler_params=pltpu.CompilerParams(vmem_limit_bytes=14 << 20),
     )(heads, pltpu.with_memory_space_constraint(weight, pltpu.HBM))
+
+
+def route_kernel(
+    tok_rows, parts_ref, gain_ref, router_ref, member_ref, placing_ref, out_ref, attended_ref
+):
+    width = gain_ref.shape[1]
+    packed = parts_ref[0].astype(F32)
+    for index in range(1, parts_ref.shape[0]):
+        packed = packed + parts_ref[index].astype(F32)
+    wide, places = folds(tok_rows, width)
+    attended_ref[...] = jnp.zeros(attended_ref.shape, F32)
+    attended_ref[:tok_rows, :wide] = packed[:tok_rows]
+    for k, row, column in places:
+        attended_ref[k : k + 1, wide:] = packed[row : row + 1, column : column + width - wide]
+    attended = attended_ref[...]
+    inverse = lax.rsqrt(jnp.mean(attended * attended, axis=1, keepdims=True) + 1e-05)
+    normed = attended * inverse * gain_ref[...]
+    logits = lax.dot_general(
+        normed.astype(BF),
+        router_ref[...],
+        (((1,), (1,)), ((), ())),
+        preferred_element_type=F32,
+    )
+    picked = jnp.sum(jnp.where(member_ref[...] > 0, logits, 0.0), axis=1, keepdims=True)
+    routed = (normed * jax.nn.sigmoid(picked)).astype(BF)
+    placing = placing_ref[...]
+    out_ref[:, :width] = jnp.dot(placing, routed, preferred_element_type=F32).astype(BF)
+    filled = jnp.sum(placing.astype(F32), axis=1, keepdims=True)
+    out_ref[:, width:] = jnp.broadcast_to(filled, (placing.shape[0], LANES)).astype(BF)
+
+
+def route(parts, gain, router_rows, member, placing, tok_rows):
+    whole = pl.BlockSpec(memory_space=pltpu.VMEM)
+    width = gain.shape[1]
+    return pl.pallas_call(
+        functools.partial(route_kernel, tok_rows),
+        out_shape=jax.ShapeDtypeStruct((placing.shape[0], width + LANES), BF),
+        in_specs=[whole] * 5,
+        out_specs=whole,
+        scratch_shapes=[pltpu.VMEM((8, width), F32)],
+        compiler_params=pltpu.CompilerParams(vmem_limit_bytes=8 << 20),
+    )(parts, gain, router_rows, member, placing)
 
 
 def expert_kernel(rows_ref, *refs):
@@ -100,35 +164,33 @@
     recv_cap = min(tok_rows + max(2, tok_rows // 5), send_cap * (expert_count - 2) + 2)
     slots = expert_count * send_cap
 
-    pad_rows = -(-tok_rows // 8) * 8
-    heads = head_rows.reshape(tensor_count, tok_rows, -1)
-    heads = jnp.pad(heads, ((0, 0), (0, pad_rows - tok_rows), (0, 0)))
-    partial = project(heads.reshape(tensor_count * pad_rows, -1), out_proj)
-    partial = exchange(partial.reshape(tensor_count, pad_rows, width), "tensor")
-    attended = total_of(partial)[:tok_rows]
-
-    inverse = lax.rsqrt(jnp.mean(attended * attended, axis=-1, keepdims=True) + 1e-05)
-    normed = attended * inverse * norm_gain
-    router_logits = jnp.dot(normed.astype(BF), router, preferred_element_type=F32)
     chosen_ids = expert_ids.reshape(-1)
     expert_index = jnp.arange(expert_count, dtype=jnp.int32)
-    member_mask = chosen_ids[:, None] == expert_index[None, :]
-    router_score = jax.nn.sigmoid(jnp.sum(jnp.where(member_mask, router_logits, 0.0), axis=1))
-    routed = (normed * router_score[:, None]).astype(BF)
-
+    member = (chosen_ids[:, None] == expert_index[None, :]).astype(F32)
     same = chosen_ids[:, None] == chosen_ids[None, :]
     earlier = jnp.arange(tok_rows)[None, :] < jnp.arange(tok_rows)[:, None]
     rank_within = jnp.sum((same & earlier).astype(jnp.int32), axis=1)
     slot_index = chosen_ids * send_cap + rank_within
     slot_range = jnp.arange(slots, dtype=jnp.int32)
     placing = (slot_range[:, None] == slot_index[None, :]).astype(BF)
-    flagged = jnp.concatenate([routed, jnp.ones((tok_rows, LANES), BF)], axis=1)
-    outgoing = jnp.dot(placing, flagged, preferred_element_type=F32).astype(BF)
-    own = [weight[0] for weight in (w_gate, w_up, w_down)]
-    outgoing, own = lax.optimization_barrier((outgoing, own))
-    other = [lax.ppermute(weight, "core", swap) for weight in own]
+    spare = 8 - tok_rows
+
+    gate, up, down = w_gate[0], w_up[0], w_down[0]
+    partial = project(head_rows, out_proj, tok_rows)
+    parts = exchange(partial.reshape(tensor_count, 8, -1), "tensor")
+    outgoing = route(
+        parts,
+        norm_gain[None],
+        router.T,
+        jnp.pad(member, ((0, spare), (0, 0))),
+        jnp.pad(placing, ((0, 0), (0, spare))),
+        tok_rows,
+    )
+    outgoing, gate, up = lax.optimization_barrier((outgoing, gate, up))
+    other_gate = lax.ppermute(gate, "core", swap)
+    other_up = lax.ppermute(up, "core", swap)
     arrived = exchange(outgoing.reshape(expert_count, send_cap, width + LANES), expert_axes)
-    arrived, other = lax.optimization_barrier((arrived, other))
+    arrived, other_gate, other_up = lax.optimization_barrier((arrived, other_gate, other_up))
     arrived = arrived.reshape(slots, width + LANES)
 
     filled = arrived[:, width].astype(F32)
@@ -138,9 +200,14 @@
     selector = (jnp.arange(recv_cap, dtype=jnp.int32)[:, None] == position[None, :]).astype(BF)
     compact = jnp.dot(selector, arrived[:, :width], preferred_element_type=F32).astype(BF)
 
+    compact, down = lax.optimization_barrier((compact, down))
+    other_down = lax.ppermute(down, "core", swap)
     rows = spread(compact, "tensor").reshape(tensor_count * recv_cap, width)
+    rows, other_down = lax.optimization_barrier((rows, other_down))
     rows = spread(rows, "x").reshape(x_count * tensor_count * recv_cap, width)
-    pair_sum = local_call(expert_kernel, rows.shape, rows, *own, *other)
+    pair_sum = local_call(
+        expert_kernel, rows.shape, rows, gate, up, down, other_gate, other_up, other_down
+    )
     plane_sum = total_of(
         exchange(pair_sum.reshape(x_count, tensor_count * recv_cap, width), "x")
     ).astype(BF)

time: 169 us -> 166 us (0.982)
  blocking collectives: 99.6 us -> 96.9 us
    all_to_all x5, blocking collectives: 99.6 us -> 96.9 us  [exchange(): return lax.all_to_all(value, axis, split_axis=0, concat_axis=0, tiled=True)]
    pallas_call x1 -> x2, Pallas kernels: 3.97 us -> 4.87 us  [the longest x1 4 us: project(): pl.pallas_call(functools.partial(project_kernel, chunks, tok_rows), out_s...]
    unnamed x24 -> x22, local copies, waits for them, and re-layouts: 3.26 us -> 3.88 us
  transfers between devices with their start and end apart: 5 -> 5, of which waited for: 3 -> 4; matrix products, arithmetic and copies ran while one was open for 0% -> 0% of each run, Pallas kernels for 0% -> 0%
where the time goes in v5:
time: 166 us; the launch traced here: 165 us
  blocking collectives  96.9 us (58%)
  starting transfers between devices  30.1 us (18%)
  waiting for transfers between devices  22.3 us (13%)
  Pallas kernels  7.21 us (4%)
  local copies, waits for them, and re-layouts  6.59 us (4%)
    all_to_all x5, blocking collectives, exchange(): return lax.all_to_all(value, axis, split_axis=0, concat_axis=0, tiled=True)  96.9 us
    all_to_all x2, starting transfers between devices, exchange(): return lax.all_to_all(value, axis, split_axis=0, concat_axis=0, tiled=True)  23.9 us
    all_to_all x2, waiting for transfers between devices, exchange(): return lax.all_to_all(value, axis, split_axis=0, concat_axis=0, tiled=True)  20.8 us
    pallas_call x1, Pallas kernels, project(): pl.pallas_call(functools.partial(project_kernel, chunks, tok_rows), out_s...  4 us
    unnamed x22, local copies, waits for them, and re-layouts  3.88 us
  transfers between devices with their start and end apart: 5, of which 4 were waited for; matrix products, arithmetic and copies ran while one was open for 0% of the time, Pallas kernels for 0%

profile of v5, /device:TPU:8, one launch (start us, length us, event | category | flops | bytes accessed | tf_op | source)
XLA Modules:
  0.0 165.5 jit_solution(6935984219071069225)
XLA Ops:
  0.0 0.0 copy-start.8
  0.0 0.8 copy-done.8
  0.8 0.0 copy-start.10
  0.8 0.0 copy-start.9
  0.8 4.0 %shard_map.82 = bf16[32,3840]{1,0:T(8,128)(2,1)} custom-call(bf16[24,640]{1,0:T(8,128)(2,1)S(1)} %bitcast.29, bf16[640,5120]{1,0:T(8,128)(2,1)} %weight_ref.1), custom_call_target="tpu_custom_call" | custom-call | tf_op jit(solution)/shard_map/pallas_call | solution.py:82
  4.8 14.5 %all-to-all-start = ((bf16[4,8,3840]{2,1,0:T(8,128)(2,1)}), bf16[4,8,3840]{2,1,0:T(8,128)(2,1)S(1)}, u32[]{:S(2)}, u32[]{:S(2)}) async-start(bf16[4,8,3840]{2,1,0:T(8,128)(2,1)} %bitcast.2), calls=%async_computation | async-start | bytes 491520 | tf_op jit(solution)/shard_map/all_to_all | solution.py:16
  19.3 0.0 copy-done.10
  19.3 0.2 convert_reduce_fusion.1
  19.5 0.1 iota_compare_fusion.2
  19.6 14.4 %all-to-all-done.parts_ref = bf16[4,8,3840]{2,1,0:T(8,128)(2,1)S(1)} async-done(((bf16[4,8,3840]{2,1,0:T(8,128)(2,1)}), bf16[4,8,3840]{2,1,0:T(8,128)(2,1)S(1)}, u32[]{:S(2)}, u32[]{:S(2)}) %all-to-all-start) | async-done | bytes 245792 | tf_op jit(solution)/shard_map/all_to_all | solution.py:16
  34.0 0.0 copy-done.9
  34.0 0.9 copy-done.7
  35.0 0.9 shard_map.83
  35.8 1.0 reshape.82
  36.8 9.4 %all-to-all-start.1 = ((bf16[24,2,5248]{2,1,0:T(2,128)(2,1)}), bf16[24,2,5248]{2,1,0:T(2,128)(2,1)}, u32[]{:S(2)}, u32[]{:S(2)}) async-start(bf16[24,2,5248]{2,1,0:T(2,128)(2,1)} %reshape.82), calls=%async_computation.1 | async-start | bytes 1007616 | tf_op jit(solution)/shard_map/all_to_all | solution.py:16
  46.2 0.0 copy-done
  46.2 1.9 %collective-permute-start = (bf16[5120,128]{1,0:T(8,128)(2,1)S(1)}, bf16[5120,128]{1,0:T(8,128)(2,1)S(1)}, u32[]{:S(2)}, u32[]{:S(2)}) collective-permute-start(bf16[5120,128]{1,0:T(8,128)(2,1)S(1)} %bitcast.22), channel_id=1, source_target_pairs={{0,96},{96,0},{1,97},{97,1},{2,98},{98,2},{3,99},{99,3},{4,100},{1... | collective-permute-start | bytes 3932168 | tf_op jit(solution)/shard_map/ppermute | solution.py:190
  48.1 0.0 copy-done.1
  48.1 2.4 %collective-permute-start.1 = (bf16[5120,128]{1,0:T(8,128)(2,1)S(1)}, bf16[5120,128]{1,0:T(8,128)(2,1)S(1)}, u32[]{:S(2)}, u32[]{:S(2)}) collective-permute-start(bf16[5120,128]{1,0:T(8,128)(2,1)S(1)} %bitcast.24), channel_id=1, source_target_pairs={{0,96},{96,0},{1,97},{97,1},{2,98},{98,2},{3,99},{99,3},{4,100},{1... | collective-permute-start | bytes 3932168 | tf_op jit(solution)/shard_map/ppermute | solution.py:191
  50.5 0.6 collective-permute-done.refs_3_
  51.1 1.1 copy-done.3
  52.2 1.0 collective-permute-done.1.refs_4_
  53.2 1.1 copy-done.5
  54.2 6.3 %all-to-all-done.1 = bf16[24,2,5248]{2,1,0:T(2,128)(2,1)} async-done(((bf16[24,2,5248]{2,1,0:T(2,128)(2,1)}), bf16[24,2,5248]{2,1,0:T(2,128)(2,1)}, u32[]{:S(2)}, u32[]{:S(2)}) %all-to-all-start.1) | async-done | bytes 503840 | tf_op jit(solution)/shard_map/all_to_all | solution.py:16
  60.6 1.2 reshape.83
  61.8 0.1 convert_reduce_fusion
  61.9 0.1 fusion.9
  62.0 0.1 select_reduce_fusion
  62.1 0.2 convolution_convert_fusion.2
  62.3 1.9 %collective-permute-start.2 = (bf16[128,5120]{1,0:T(8,128)(2,1)}, bf16[128,5120]{1,0:T(8,128)(2,1)S(1)}, u32[]{:S(2)}, u32[]{:S(2)}) collective-permute-start(bf16[128,5120]{1,0:T(8,128)(2,1)} %bitcast.26), channel_id=1, source_target_pairs={{0,96},{96,0},{1,97},{97,1},{2,98},{98,2},{3,99},{99,3},{4,100},{1... | collective-permute-start | bytes 3932168 | tf_op jit(solution)/shard_map/ppermute | solution.py:204
  64.3 22.8 %all_to_all.35 = bf16[4,8,5120]{2,1,0:T(8,128)(2,1)S(1)} all-to-all(bf16[4,8,5120]{2,1,0:T(8,128)(2,1)S(1)} %broadcast_in_dim.52), channel_id=1, replica_groups=mesh['x'=4,'core'=2,'tensor'=4,'y'=8,'w'=3] {'tensor'}, dimensions={0} | all-to-all | bytes 655360 | tf_op jit(solution)/shard_map/all_to_all | solution.py:16
  87.1 0.0 collective-permute-done.2.refs_5_
  87.1 0.1 broadcast_in_dim.53
  87.2 0.0 copy-start.2
  87.2 0.0 copy-start.4
  87.2 16.7 %all_to_all.36 = bf16[4,32,5120]{2,1,0:T(8,128)(2,1)S(1)} all-to-all(bf16[4,32,5120]{2,1,0:T(8,128)(2,1)S(1)} %broadcast_in_dim.53), channel_id=1, replica_groups=mesh['x'=4,'core'=2,'tensor'=4,'y'=8,'w'=3] {'x'}, dimensions={0} | all-to-all | bytes 2621440 | tf_op jit(solution)/shard_map/all_to_all | solution.py:16
  103.9 0.0 copy-done.6
  103.9 0.0 copy-done.2
  103.9 0.0 copy-done.4
  103.9 2.3 %shard_map.84 = bf16[128,5120]{1,0:T(8,128)(2,1)S(1)} custom-call(bf16[128,5120]{1,0:T(8,128)(2,1)S(1)} %bitcast.20, bf16[5120,128]{1,0:T(8,128)(2,1)S(1)} %bitcast.23, bf16[5120,128]{1,0:T(8,128)(2,1)S(1)} %bitcast.25, bf16[128,5120]{1,0:T(8,128)(2,1)S(1)} %bitcast.27, bf16[5120,128]{1,0:T(8,128)(2,1)S(1)} %copy-done.4, bf16[5120,128]{1,0:T(8,128)(2,1)S(1)} %copy-done.6, ...), custom_call_target="tpu_custom_call" | custom-call | tf_op jit(solution)/shard_map/pallas_call | solution.py:37
  106.2 14.7 %all_to_all.37 = bf16[4,32,5120]{2,1,0:T(8,128)(2,1)S(1)} all-to-all(bf16[4,32,5120]{2,1,0:T(8,128)(2,1)S(1)} %bitcast.21), channel_id=1, replica_groups=mesh['x'=4,'core'=2,'tensor'=4,'y'=8,'w'=3] {'x'}, dimensions={0} | all-to-all | bytes 2621440 | tf_op jit(solution)/shard_map/all_to_all | solution.py:16
  121.0 0.2 fusion.2
  121.1 14.8 %all_to_all.38 = bf16[4,8,5120]{2,1,0:T(8,128)(2,1)S(1)} all-to-all(bf16[4,8,5120]{2,1,0:T(8,128)(2,1)S(1)} %fusion.2), channel_id=1, replica_groups=mesh['x'=4,'core'=2,'tensor'=4,'y'=8,'w'=3] {'tensor'}, dimensions={0} | all-to-all | bytes 655360 | tf_op jit(solution)/shard_map/all_to_all | solution.py:16
  136.0 0.3 convolution_convert_fusion
  136.3 0.2 reshape.87
  136.5 27.9 %all_to_all.39 = bf16[24,2,5120]{2,1,0:T(2,128)(2,1)S(1)} all-to-all(bf16[24,2,5120]{2,1,0:T(2,128)(2,1)S(1)} %reshape.87), channel_id=1, replica_groups=mesh['x'=4,'core'=2,'tensor'=4,'y'=8,'w'=3] {'y','w'}, dimensions={0} | all-to-all | bytes 983040 | tf_op jit(solution)/shard_map/all_to_all | solution.py:16
  164.4 0.2 reshape.88
  164.6 0.9 fusion
  (12 shorter events, 0.1 us)
Async XLA Ops:
  0.0 0.8 copy-start.8
  0.8 18.5 %copy-start.10 = (s32[1,6,1]{1,2,0:T(1,128)S(1)}, s32[1,6,1]{1,2,0:T(1,128)}, u32[]{:S(2)}) copy-start(s32[1,6,1]{1,2,0:T(1,128)} %param.12) | copy-start | bytes 76
  0.8 33.2 %copy-start.9 = (f32[5120]{0:T(1024)S(1)}, f32[5120]{0:T(1024)}, u32[]{:S(2)}) copy-start(f32[5120]{0:T(1024)} %param.10) | copy-start | bytes 61444
  4.8 29.2 %all-to-all-start = ((bf16[4,8,3840]{2,1,0:T(8,128)(2,1)}), bf16[4,8,3840]{2,1,0:T(8,128)(2,1)S(1)}, u32[]{:S(2)}, u32[]{:S(2)}) async-start(bf16[4,8,3840]{2,1,0:T(8,128)(2,1)} %bitcast.2), calls=%async_computation | async-start | bytes 491520 | tf_op jit(solution)/shard_map/all_to_all | solution.py:16
  34.0 0.9 copy-start.7
  35.0 11.2 %copy-start = (bf16[1,5120,128]{2,1,0:T(8,128)(2,1)S(1)}, bf16[1,5120,128]{2,1,0:T(8,128)(2,1)}, u32[]{:S(2)}) copy-start(bf16[1,5120,128]{2,1,0:T(8,128)(2,1)} %param.13) | copy-start | bytes 3932164
  35.0 13.2 %copy-start.1 = (bf16[1,5120,128]{2,1,0:T(8,128)(2,1)S(1)}, bf16[1,5120,128]{2,1,0:T(8,128)(2,1)}, u32[]{:S(2)}) copy-start(bf16[1,5120,128]{2,1,0:T(8,128)(2,1)} %param.14) | copy-start | bytes 3932164
  36.8 23.8 %all-to-all-start.1 = ((bf16[24,2,5248]{2,1,0:T(2,128)(2,1)}), bf16[24,2,5248]{2,1,0:T(2,128)(2,1)}, u32[]{:S(2)}, u32[]{:S(2)}) async-start(bf16[24,2,5248]{2,1,0:T(2,128)(2,1)} %reshape.82), calls=%async_computation.1 | async-start | bytes 1007616 | tf_op jit(solution)/shard_map/all_to_all | solution.py:16
  46.2 4.9 %collective-permute-start = (bf16[5120,128]{1,0:T(8,128)(2,1)S(1)}, bf16[5120,128]{1,0:T(8,128)(2,1)S(1)}, u32[]{:S(2)}, u32[]{:S(2)}) collective-permute-start(bf16[5120,128]{1,0:T(8,128)(2,1)S(1)} %bitcast.22), channel_id=1, source_target_pairs={{0,96},{96,0},{1,97},{97,1},{2,98},{98,2},{3,99},{99,3},{4,100},{1... | collective-permute-start | bytes 3932168 | tf_op jit(solution)/shard_map/ppermute | solution.py:190
  48.1 5.1 %collective-permute-start.1 = (bf16[5120,128]{1,0:T(8,128)(2,1)S(1)}, bf16[5120,128]{1,0:T(8,128)(2,1)S(1)}, u32[]{:S(2)}, u32[]{:S(2)}) collective-permute-start(bf16[5120,128]{1,0:T(8,128)(2,1)S(1)} %bitcast.24), channel_id=1, source_target_pairs={{0,96},{96,0},{1,97},{97,1},{2,98},{98,2},{3,99},{99,3},{4,100},{1... | collective-permute-start | bytes 3932168 | tf_op jit(solution)/shard_map/ppermute | solution.py:191
  51.1 1.1 copy-start.3
  53.2 1.1 copy-start.5
  62.3 24.8 %collective-permute-start.2 = (bf16[128,5120]{1,0:T(8,128)(2,1)}, bf16[128,5120]{1,0:T(8,128)(2,1)S(1)}, u32[]{:S(2)}, u32[]{:S(2)}) collective-permute-start(bf16[128,5120]{1,0:T(8,128)(2,1)} %bitcast.26), channel_id=1, source_target_pairs={{0,96},{96,0},{1,97},{97,1},{2,98},{98,2},{3,99},{99,3},{4,100},{1... | collective-permute-start | bytes 3932168 | tf_op jit(solution)/shard_map/ppermute | solution.py:204
  87.1 16.8 %copy-start.6 = (bf16[5120,128]{1,0:T(8,128)(2,1)S(1)}, bf16[5120,128]{1,0:T(8,128)(2,1)}, u32[]{:S(2)}) copy-start(bf16[5120,128]{1,0:T(8,128)(2,1)} %copy-done.5) | copy-start | bytes 3932164
  87.2 16.7 %copy-start.2 = (bf16[1,128,5120]{2,1,0:T(8,128)(2,1)S(1)}, bf16[1,128,5120]{2,1,0:T(8,128)(2,1)}, u32[]{:S(2)}) copy-start(bf16[1,128,5120]{2,1,0:T(8,128)(2,1)} %param.15) | copy-start | bytes 3932164
  87.2 16.7 %copy-start.4 = (bf16[5120,128]{1,0:T(8,128)(2,1)S(1)}, bf16[5120,128]{1,0:T(8,128)(2,1)}, u32[]{:S(2)}) copy-start(bf16[5120,128]{1,0:T(8,128)(2,1)} %copy-done.3) | copy-start | bytes 3932164

commit v6 on v5

--- a/solution.py
+++ b/solution.py
@@ -93,13 +93,27 @@
     )(heads, pltpu.with_memory_space_constraint(weight, pltpu.HBM))
 
 
+def stacked(rows, fold):
+    part = rows.shape[1] // fold
+    return jnp.concatenate([rows[:, q * part : (q + 1) * part] for q in range(fold)], axis=0)
+
+
+def turned(left, right):
+    return lax.dot_general(left, right, (((0,), (0,)), ((), ())), preferred_element_type=F32)
+
+
+def sum_of(parts_ref):
+    total = parts_ref[0].astype(F32)
+    for index in range(1, parts_ref.shape[0]):
+        total = total + parts_ref[index].astype(F32)
+    return total
+
+
 def route_kernel(
-    tok_rows, parts_ref, gain_ref, router_ref, member_ref, placing_ref, out_ref, attended_ref
+    tok_rows, fold, parts_ref, gain_ref, router_ref, member_ref, placing_ref, out_ref, attended_ref
 ):
     width = gain_ref.shape[1]
-    packed = parts_ref[0].astype(F32)
-    for index in range(1, parts_ref.shape[0]):
-        packed = packed + parts_ref[index].astype(F32)
+    packed = sum_of(parts_ref)
     wide, places = folds(tok_rows, width)
     attended_ref[...] = jnp.zeros(attended_ref.shape, F32)
     attended_ref[:tok_rows, :wide] = packed[:tok_rows]
@@ -115,24 +129,93 @@
         preferred_element_type=F32,
     )
     picked = jnp.sum(jnp.where(member_ref[...] > 0, logits, 0.0), axis=1, keepdims=True)
-    routed = (normed * jax.nn.sigmoid(picked)).astype(BF)
-    placing = placing_ref[...]
-    out_ref[:, :width] = jnp.dot(placing, routed, preferred_element_type=F32).astype(BF)
-    filled = jnp.sum(placing.astype(F32), axis=1, keepdims=True)
-    out_ref[:, width:] = jnp.broadcast_to(filled, (placing.shape[0], LANES)).astype(BF)
-
-
-def route(parts, gain, router_rows, member, placing, tok_rows):
+    routed = stacked(normed * jax.nn.sigmoid(picked), fold).astype(BF)
+    out_ref[...] = jnp.dot(placing_ref[...], routed, preferred_element_type=F32).astype(BF)
+
+
+def route(parts, gain, router_rows, member, placing, tok_rows, fold):
     whole = pl.BlockSpec(memory_space=pltpu.VMEM)
     width = gain.shape[1]
     return pl.pallas_call(
-        functools.partial(route_kernel, tok_rows),
-        out_shape=jax.ShapeDtypeStruct((placing.shape[0], width + LANES), BF),
+        functools.partial(route_kernel, tok_rows, fold),
+        out_shape=jax.ShapeDtypeStruct((placing.shape[0], width // fold), BF),
         in_specs=[whole] * 5,
         out_specs=whole,
         scratch_shapes=[pltpu.VMEM((8, width), F32)],
         compiler_params=pltpu.CompilerParams(vmem_limit_bytes=8 << 20),
     )(parts, gain, router_rows, member, placing)
+
+
+def compact_kernel(fold, cap, arrived_ref, out_ref, selector_ref):
+    arrived = arrived_ref[...]
+    rows = arrived.shape[0]
+    square = (rows, rows)
+    first = lax.broadcasted_iota(jnp.int32, square, 0)
+    second = lax.broadcasted_iota(jnp.int32, square, 1)
+    slot_first = lax.div(first, jnp.full(square, fold, jnp.int32))
+    slot_second = lax.div(second, jnp.full(square, fold, jnp.int32))
+    peak = jnp.max(jnp.abs(arrived.astype(F32)), axis=1, keepdims=True)
+    filled = jnp.broadcast_to(jnp.where(peak > 0, 1.0, 0.0), (rows, LANES)).astype(BF)
+    same = jnp.where(slot_first == slot_second, 1.0, 0.0).astype(BF)
+    filled = jnp.dot(same, filled, preferred_element_type=F32) > 0
+    heads = slot_second * fold == second
+    before = jnp.where(heads & (slot_second < slot_first), 1.0, 0.0).astype(BF)
+    ones = jnp.where(filled, 1.0, 0.0).astype(BF)
+    position = jnp.dot(before, ones, preferred_element_type=F32).astype(jnp.int32)
+    wide = (rows, LANES)
+    row = lax.broadcasted_iota(jnp.int32, wide, 0)
+    column = lax.broadcasted_iota(jnp.int32, wide, 1)
+    piece = lax.div(column, jnp.full(wide, cap, jnp.int32))
+    mine = lax.rem(row, jnp.full(wide, fold, jnp.int32)) == piece
+    taken = filled & mine & (position == column - piece * cap)
+    selector = jnp.where(taken, 1.0, 0.0).astype(BF)[:, : fold * cap]
+    selector_ref[...] = selector
+    compact = turned(selector, arrived)
+    part = arrived.shape[1]
+    for peer in range(out_ref.shape[0]):
+        for q in range(fold):
+            out_ref[peer, :, q * part : (q + 1) * part] = compact[
+                q * cap : (q + 1) * cap
+            ].astype(BF)
+
+
+def compact_rows(arrived, fold, cap, peers):
+    whole = pl.BlockSpec(memory_space=pltpu.VMEM)
+    rows, part = arrived.shape
+    return pl.pallas_call(
+        functools.partial(compact_kernel, fold, cap),
+        out_shape=(
+            pltpu.VMEM((peers, cap, fold * part), BF),
+            jax.ShapeDtypeStruct((rows, fold * cap), BF),
+        ),
+        in_specs=[whole],
+        out_specs=(whole, whole),
+        compiler_params=pltpu.CompilerParams(vmem_limit_bytes=8 << 20),
+    )(arrived)
+
+
+def return_kernel(fold, parts_ref, selector_ref, out_ref):
+    expert_rows = stacked(sum_of(parts_ref), fold).astype(BF)
+    out_ref[...] = jnp.dot(selector_ref[...], expert_rows, preferred_element_type=F32).astype(BF)
+
+
+def combine_kernel(tok_rows, fold, returned_ref, placing_ref, out_ref):
+    combined = turned(placing_ref[...], returned_ref[...])
+    part = returned_ref.shape[1]
+    rows = combined.shape[0] // fold
+    for q in range(fold):
+        out_ref[:, q * part : (q + 1) * part] = combined[q * rows : q * rows + tok_rows].astype(BF)
+
+
+def combine(returned, placing, tok_rows, fold):
+    whole = pl.BlockSpec(memory_space=pltpu.VMEM)
+    return pl.pallas_call(
+        functools.partial(combine_kernel, tok_rows, fold),
+        out_shape=jax.ShapeDtypeStruct((tok_rows, fold * returned.shape[1]), BF),
+        in_specs=[whole] * 2,
+        out_specs=whole,
+        compiler_params=pltpu.CompilerParams(vmem_limit_bytes=8 << 20),
+    )(returned, placing)
 
 
 def expert_kernel(rows_ref, *refs):
@@ -171,9 +254,13 @@
     earlier = jnp.arange(tok_rows)[None, :] < jnp.arange(tok_rows)[:, None]
     rank_within = jnp.sum((same & earlier).astype(jnp.int32), axis=1)
     slot_index = chosen_ids * send_cap + rank_within
-    slot_range = jnp.arange(slots, dtype=jnp.int32)
-    placing = (slot_range[:, None] == slot_index[None, :]).astype(BF)
     spare = 8 - tok_rows
+    fold = 8 // send_cap
+    row_range = jnp.arange(slots * fold, dtype=jnp.int32)
+    slot_columns = jnp.tile(jnp.pad(slot_index, (0, spare), constant_values=-1), fold)
+    piece_columns = jnp.arange(fold * 8, dtype=jnp.int32) // 8
+    target = jnp.where(slot_columns < 0, -1, slot_columns * fold + piece_columns)
+    placing = (row_range[:, None] == target[None, :]).astype(BF)
 
     gate, up, down = w_gate[0], w_up[0], w_down[0]
     partial = project(head_rows, out_proj, tok_rows)
@@ -183,26 +270,19 @@
         norm_gain[None],
         router.T,
         jnp.pad(member, ((0, spare), (0, 0))),
-        jnp.pad(placing, ((0, 0), (0, spare))),
+        placing,
         tok_rows,
+        fold,
     )
     outgoing, gate, up = lax.optimization_barrier((outgoing, gate, up))
     other_gate = lax.ppermute(gate, "core", swap)
     other_up = lax.ppermute(up, "core", swap)
-    arrived = exchange(outgoing.reshape(expert_count, send_cap, width + LANES), expert_axes)
+    arrived = exchange(outgoing, expert_axes)
     arrived, other_gate, other_up = lax.optimization_barrier((arrived, other_gate, other_up))
-    arrived = arrived.reshape(slots, width + LANES)
-
-    filled = arrived[:, width].astype(F32)
-    before = slot_range[:, None] < slot_range[None, :]
-    position = jnp.sum(jnp.where(before, filled[:, None], 0.0), axis=0).astype(jnp.int32)
-    position = jnp.where(filled > 0.5, position, -1)
-    selector = (jnp.arange(recv_cap, dtype=jnp.int32)[:, None] == position[None, :]).astype(BF)
-    compact = jnp.dot(selector, arrived[:, :width], preferred_element_type=F32).astype(BF)
-
+    compact, selector = compact_rows(arrived, fold, recv_cap, tensor_count)
     compact, down = lax.optimization_barrier((compact, down))
     other_down = lax.ppermute(down, "core", swap)
-    rows = spread(compact, "tensor").reshape(tensor_count * recv_cap, width)
+    rows = exchange(compact, "tensor").reshape(tensor_count * recv_cap, width)
     rows, other_down = lax.optimization_barrier((rows, other_down))
     rows = spread(rows, "x").reshape(x_count * tensor_count * recv_cap, width)
     pair_sum = local_call(
@@ -211,14 +291,16 @@
     plane_sum = total_of(
         exchange(pair_sum.reshape(x_count, tensor_count * recv_cap, width), "x")
     ).astype(BF)
-    expert_rows = total_of(
-        exchange(plane_sum.reshape(tensor_count, recv_cap, width), "tensor")
-    ).astype(BF)
-
-    back = jnp.dot(selector.T, expert_rows, preferred_element_type=F32).astype(BF)
-    returned = exchange(back.reshape(expert_count, send_cap, width), expert_axes)
-    combined = jnp.dot(placing.T, returned.reshape(slots, width), preferred_element_type=F32)
-    return combined.astype(BF).reshape(1, tok_rows, 1, width)
+    parts = exchange(plane_sum.reshape(tensor_count, recv_cap, width), "tensor")
+    back = local_call(
+        functools.partial(return_kernel, fold),
+        (slots * fold, width // fold),
+        parts,
+        selector,
+    )
+    returned = exchange(back, expert_axes)
+    combined = combine(returned, placing, tok_rows, fold)
+    return combined.reshape(1, tok_rows, 1, width)
 
 
 def solution(mesh):

time: 166 us -> 164 us (0.988)
  the two profiles are of different devices: /device:TPU:8 before, /device:TPU:2 now
where the time goes in v6:
time: 164 us; the launch traced here: 163 us
  blocking collectives  96.8 us (59%)
  starting transfers between devices  30 us (18%)
  waiting for transfers between devices  22.5 us (14%)
  Pallas kernels  9.89 us (6%)
  local copies, waits for them, and re-layouts  3.24 us (2%)
    all_to_all x5, blocking collectives, exchange(): return lax.all_to_all(value, axis, split_axis=0, concat_axis=0, tiled=True)  96.8 us
    all_to_all x2, starting transfers between devices, exchange(): return lax.all_to_all(value, axis, split_axis=0, concat_axis=0, tiled=True)  23.7 us
    all_to_all x2, waiting for transfers between devices, exchange(): return lax.all_to_all(value, axis, split_axis=0, concat_axis=0, tiled=True)  20.9 us
    pallas_call x1, Pallas kernels, project(): pl.pallas_call(functools.partial(project_kernel, chunks, tok_rows), out_s...  4.1 us
  transfers between devices with their start and end apart: 5, of which 4 were waited for; matrix products, arithmetic and copies ran while one was open for 0% of the time, Pallas kernels for 0%

profile of v6, /device:TPU:2, one launch (start us, length us, event | category | flops | bytes accessed | tf_op | source)
XLA Modules:
  0.0 163.0 jit_solution(1738698371157774880)
XLA Ops:
  0.0 0.0 copy-start.8
  0.0 0.8 copy-done.8
  0.8 0.0 copy-start.10
  0.8 0.0 copy-start.7
  0.8 0.0 copy-start.9
  0.8 0.0 copy-start.1
  0.8 4.1 %shard_map.82 = bf16[32,3840]{1,0:T(8,128)(2,1)} custom-call(bf16[24,640]{1,0:T(8,128)(2,1)S(1)} %bitcast.31, bf16[640,5120]{1,0:T(8,128)(2,1)} %weight_ref.1), custom_call_target="tpu_custom_call" | custom-call | tf_op jit(solution)/shard_map/pallas_call | solution.py:82
  4.9 0.0 copy-start
  4.9 14.6 %all-to-all-start = ((bf16[4,8,3840]{2,1,0:T(8,128)(2,1)}), bf16[4,8,3840]{2,1,0:T(8,128)(2,1)S(1)}, u32[]{:S(2)}, u32[]{:S(2)}) async-start(bf16[4,8,3840]{2,1,0:T(8,128)(2,1)} %bitcast.1), calls=%async_computation | async-start | bytes 491520 | tf_op jit(solution)/shard_map/all_to_all | solution.py:16
  19.5 0.0 copy-done.10
  19.5 0.2 convert_reduce_fusion
  19.7 0.1 iota_compare_fusion.2
  19.8 0.1 lt.34
  19.9 0.1 mul.20
  20.0 14.2 %all-to-all-done.parts_ref = bf16[4,8,3840]{2,1,0:T(8,128)(2,1)S(1)} async-done(((bf16[4,8,3840]{2,1,0:T(8,128)(2,1)}), bf16[4,8,3840]{2,1,0:T(8,128)(2,1)S(1)}, u32[]{:S(2)}, u32[]{:S(2)}) %all-to-all-start) | async-done | bytes 245792 | tf_op jit(solution)/shard_map/all_to_all | solution.py:16
  34.2 0.0 copy-done.7
  34.2 0.0 copy-done.9
  34.2 1.7 %shard_map.83 = bf16[192,1280]{1,0:T(8,128)(2,1)} custom-call(bf16[4,8,3840]{2,1,0:T(8,128)(2,1)S(1)} %all-to-all-done.parts_ref, f32[1,5120]{1,0:T(1,128)S(1)} %bitcast.32, bf16[24,5120]{1,0:T(8,128)(2,1)S(1)} %bitcast.30, f32[8,24]{1,0:T(8,128)S(1)} %pad_convert_fusion.member_ref, bf16[192,32]{1,0:T(8,128)(2,1)S(1)} %fusion.1.placing_ref), custom_call_target="tpu_custom_call" | custom-call | tf_op jit(solution)/shard_map/pallas_call | solution.py:139
  35.9 9.1 %all-to-all-start.1 = ((bf16[24,8,1280]{2,1,0:T(8,128)(2,1)}), bf16[24,8,1280]{2,1,0:T(8,128)(2,1)S(1)}, u32[]{:S(2)}, u32[]{:S(2)}) async-start(bf16[24,8,1280]{2,1,0:T(8,128)(2,1)} %bitcast.7), calls=%async_computation.1 | async-start | bytes 983040 | tf_op jit(solution)/shard_map/all_to_all | solution.py:16
  45.0 0.0 copy-done
  45.0 1.9 %collective-permute-start = (bf16[5120,128]{1,0:T(8,128)(2,1)S(1)}, bf16[5120,128]{1,0:T(8,128)(2,1)S(1)}, u32[]{:S(2)}, u32[]{:S(2)}) collective-permute-start(bf16[5120,128]{1,0:T(8,128)(2,1)S(1)} %bitcast.24), channel_id=1, source_target_pairs={{0,96},{96,0},{1,97},{97,1},{2,98},{98,2},{3,99},{99,3},{4,100},{1... | collective-permute-start | bytes 3932168 | tf_op jit(solution)/shard_map/ppermute | solution.py:278
  46.9 0.0 copy-done.1
  46.9 2.4 %collective-permute-start.1 = (bf16[5120,128]{1,0:T(8,128)(2,1)S(1)}, bf16[5120,128]{1,0:T(8,128)(2,1)S(1)}, u32[]{:S(2)}, u32[]{:S(2)}) collective-permute-start(bf16[5120,128]{1,0:T(8,128)(2,1)S(1)} %bitcast.26), channel_id=1, source_target_pairs={{0,96},{96,0},{1,97},{97,1},{2,98},{98,2},{3,99},{99,3},{4,100},{1... | collective-permute-start | bytes 3932168 | tf_op jit(solution)/shard_map/ppermute | solution.py:279
  49.4 0.6 collective-permute-done.refs_3_
  49.9 0.0 copy-start.3
  49.9 1.1 copy-done.3
  51.0 1.0 collective-permute-done.1.refs_4_
  52.0 0.0 copy-start.5
  52.0 1.1 copy-done.5
  53.1 6.7 %all-to-all-done.1 = bf16[24,8,1280]{2,1,0:T(8,128)(2,1)S(1)} async-done(((bf16[24,8,1280]{2,1,0:T(8,128)(2,1)}), bf16[24,8,1280]{2,1,0:T(8,128)(2,1)S(1)}, u32[]{:S(2)}, u32[]{:S(2)}) %all-to-all-start.1) | async-done | bytes 491552 | tf_op jit(solution)/shard_map/all_to_all | solution.py:16
  59.8 0.7 shard_map.84
  60.5 1.9 %collective-permute-start.2 = (bf16[128,5120]{1,0:T(8,128)(2,1)}, bf16[128,5120]{1,0:T(8,128)(2,1)S(1)}, u32[]{:S(2)}, u32[]{:S(2)}) collective-permute-start(bf16[128,5120]{1,0:T(8,128)(2,1)} %bitcast.28), channel_id=1, source_target_pairs={{0,96},{96,0},{1,97},{97,1},{2,98},{98,2},{3,99},{99,3},{4,100},{1... | collective-permute-start | bytes 3932168 | tf_op jit(solution)/shard_map/ppermute | solution.py:284
  62.4 22.3 %all_to_all.48 = bf16[4,8,5120]{2,1,0:T(8,128)(2,1)S(1)} all-to-all(bf16[4,8,5120]{2,1,0:T(8,128)(2,1)S(1)} %get-tuple-element.22), channel_id=1, replica_groups=mesh['x'=4,'core'=2,'tensor'=4,'y'=8,'w'=3] {'tensor'}, dimensions={0} | all-to-all | bytes 655360 | tf_op jit(solution)/shard_map/all_to_all | solution.py:16
  84.7 0.0 collective-permute-done.2.refs_5_
  84.7 0.1 broadcast_in_dim.10
  84.8 0.0 copy-start.2
  84.8 0.0 copy-start.4
  84.8 15.8 %all_to_all.49 = bf16[4,32,5120]{2,1,0:T(8,128)(2,1)S(1)} all-to-all(bf16[4,32,5120]{2,1,0:T(8,128)(2,1)S(1)} %broadcast_in_dim.10), channel_id=1, replica_groups=mesh['x'=4,'core'=2,'tensor'=4,'y'=8,'w'=3] {'x'}, dimensions={0} | all-to-all | bytes 2621440 | tf_op jit(solution)/shard_map/all_to_all | solution.py:16
  100.6 0.0 copy-done.6
  100.6 0.0 copy-done.2
  100.6 0.0 copy-done.4
  100.6 2.3 %shard_map.85 = bf16[128,5120]{1,0:T(8,128)(2,1)S(1)} custom-call(bf16[128,5120]{1,0:T(8,128)(2,1)S(1)} %bitcast.19, bf16[5120,128]{1,0:T(8,128)(2,1)S(1)} %bitcast.25, bf16[5120,128]{1,0:T(8,128)(2,1)S(1)} %bitcast.27, bf16[128,5120]{1,0:T(8,128)(2,1)S(1)} %bitcast.29, bf16[5120,128]{1,0:T(8,128)(2,1)S(1)} %copy-done.4, bf16[5120,128]{1,0:T(8,128)(2,1)S(1)} %copy-done.6, ...), custom_call_target="tpu_custom_call" | custom-call | tf_op jit(solution)/shard_map/pallas_call | solution.py:37
  102.9 14.7 %all_to_all.50 = bf16[4,32,5120]{2,1,0:T(8,128)(2,1)S(1)} all-to-all(bf16[4,32,5120]{2,1,0:T(8,128)(2,1)S(1)} %bitcast.20), channel_id=1, replica_groups=mesh['x'=4,'core'=2,'tensor'=4,'y'=8,'w'=3] {'x'}, dimensions={0} | all-to-all | bytes 2621440 | tf_op jit(solution)/shard_map/all_to_all | solution.py:16
  117.7 0.2 fusion
  117.9 21.8 %all_to_all.51.parts_ref = bf16[4,8,5120]{2,1,0:T(8,128)(2,1)S(1)} all-to-all(bf16[4,8,5120]{2,1,0:T(8,128)(2,1)S(1)} %fusion), channel_id=1, replica_groups=mesh['x'=4,'core'=2,'tensor'=4,'y'=8,'w'=3] {'tensor'}, dimensions={0} | all-to-all | bytes 655360 | tf_op jit(solution)/shard_map/all_to_all | solution.py:16
  139.7 0.3 shard_map.86
  140.0 22.1 %all_to_all.52 = bf16[24,8,1280]{2,1,0:T(8,128)(2,1)S(1)} all-to-all(bf16[24,8,1280]{2,1,0:T(8,128)(2,1)S(1)} %bitcast.22), channel_id=1, replica_groups=mesh['x'=4,'core'=2,'tensor'=4,'y'=8,'w'=3] {'y','w'}, dimensions={0} | all-to-all | bytes 983040 | tf_op jit(solution)/shard_map/all_to_all | solution.py:16
  162.1 0.9 shard_map.87
  (9 shorter events, 0.1 us)
Async XLA Ops:
  0.0 0.8 copy-start.8
  0.8 18.8 %copy-start.10 = (s32[1,6,1]{1,2,0:T(1,128)S(1)}, s32[1,6,1]{1,2,0:T(1,128)}, u32[]{:S(2)}) copy-start(s32[1,6,1]{1,2,0:T(1,128)} %param.12) | copy-start | bytes 76
  0.8 33.5 %copy-start.7 = (bf16[5120,24]{0,1:T(8,128)(2,1)S(1)}, bf16[5120,24]{0,1:T(8,128)(2,1)}, u32[]{:S(2)}) copy-start(bf16[5120,24]{0,1:T(8,128)(2,1)} %param.11) | copy-start | bytes 737284
  0.8 33.5 %copy-start.9 = (f32[5120]{0:T(1024)S(1)}, f32[5120]{0:T(1024)}, u32[]{:S(2)}) copy-start(f32[5120]{0:T(1024)} %param.10) | copy-start | bytes 61444
  0.8 46.2 %copy-start.1 = (bf16[1,5120,128]{2,1,0:T(8,128)(2,1)S(1)}, bf16[1,5120,128]{2,1,0:T(8,128)(2,1)}, u32[]{:S(2)}) copy-start(bf16[1,5120,128]{2,1,0:T(8,128)(2,1)} %param.14) | copy-start | bytes 3932164
  4.9 40.1 %copy-start = (bf16[1,5120,128]{2,1,0:T(8,128)(2,1)S(1)}, bf16[1,5120,128]{2,1,0:T(8,128)(2,1)}, u32[]{:S(2)}) copy-start(bf16[1,5120,128]{2,1,0:T(8,128)(2,1)} %param.13) | copy-start | bytes 3932164
  4.9 29.4 %all-to-all-start = ((bf16[4,8,3840]{2,1,0:T(8,128)(2,1)}), bf16[4,8,3840]{2,1,0:T(8,128)(2,1)S(1)}, u32[]{:S(2)}, u32[]{:S(2)}) async-start(bf16[4,8,3840]{2,1,0:T(8,128)(2,1)} %bitcast.1), calls=%async_computation | async-start | bytes 491520 | tf_op jit(solution)/shard_map/all_to_all | solution.py:16
  35.9 23.9 %all-to-all-start.1 = ((bf16[24,8,1280]{2,1,0:T(8,128)(2,1)}), bf16[24,8,1280]{2,1,0:T(8,128)(2,1)S(1)}, u32[]{:S(2)}, u32[]{:S(2)}) async-start(bf16[24,8,1280]{2,1,0:T(8,128)(2,1)} %bitcast.7), calls=%async_computation.1 | async-start | bytes 983040 | tf_op jit(solution)/shard_map/all_to_all | solution.py:16
  45.0 4.9 %collective-permute-start = (bf16[5120,128]{1,0:T(8,128)(2,1)S(1)}, bf16[5120,128]{1,0:T(8,128)(2,1)S(1)}, u32[]{:S(2)}, u32[]{:S(2)}) collective-permute-start(bf16[5120,128]{1,0:T(8,128)(2,1)S(1)} %bitcast.24), channel_id=1, source_target_pairs={{0,96},{96,0},{1,97},{97,1},{2,98},{98,2},{3,99},{99,3},{4,100},{1... | collective-permute-start | bytes 3932168 | tf_op jit(solution)/shard_map/ppermute | solution.py:278
  46.9 5.1 %collective-permute-start.1 = (bf16[5120,128]{1,0:T(8,128)(2,1)S(1)}, bf16[5120,128]{1,0:T(8,128)(2,1)S(1)}, u32[]{:S(2)}, u32[]{:S(2)}) collective-permute-start(bf16[5120,128]{1,0:T(8,128)(2,1)S(1)} %bitcast.26), channel_id=1, source_target_pairs={{0,96},{96,0},{1,97},{97,1},{2,98},{98,2},{3,99},{99,3},{4,100},{1... | collective-permute-start | bytes 3932168 | tf_op jit(solution)/shard_map/ppermute | solution.py:279
  49.9 1.1 copy-start.3
  52.0 1.1 copy-start.5
  60.5 24.2 %collective-permute-start.2 = (bf16[128,5120]{1,0:T(8,128)(2,1)}, bf16[128,5120]{1,0:T(8,128)(2,1)S(1)}, u32[]{:S(2)}, u32[]{:S(2)}) collective-permute-start(bf16[128,5120]{1,0:T(8,128)(2,1)} %bitcast.28), channel_id=1, source_target_pairs={{0,96},{96,0},{1,97},{97,1},{2,98},{98,2},{3,99},{99,3},{4,100},{1... | collective-permute-start | bytes 3932168 | tf_op jit(solution)/shard_map/ppermute | solution.py:284
  84.7 16.0 %copy-start.6 = (bf16[5120,128]{1,0:T(8,128)(2,1)S(1)}, bf16[5120,128]{1,0:T(8,128)(2,1)}, u32[]{:S(2)}) copy-start(bf16[5120,128]{1,0:T(8,128)(2,1)} %copy-done.5) | copy-start | bytes 3932164
  84.8 15.8 %copy-start.2 = (bf16[1,128,5120]{2,1,0:T(8,128)(2,1)S(1)}, bf16[1,128,5120]{2,1,0:T(8,128)(2,1)}, u32[]{:S(2)}) copy-start(bf16[1,128,5120]{2,1,0:T(8,128)(2,1)} %param.15) | copy-start | bytes 3932164
  84.8 15.8 %copy-start.4 = (bf16[5120,128]{1,0:T(8,128)(2,1)S(1)}, bf16[5120,128]{1,0:T(8,128)(2,1)}, u32[]{:S(2)}) copy-start(bf16[5120,128]{1,0:T(8,128)(2,1)} %copy-done.3) | copy-start | bytes 3932164

commit v7 on v6

--- a/solution.py
+++ b/solution.py
@@ -50,14 +50,17 @@
     return wide, [(k, tok_rows + k // each, k % each * rest) for k in range(tok_rows)]
 
 
-def project_kernel(chunks, tok_rows, heads_ref, weight_ref, out_ref, held, packed, sems):
+def project_kernel(chunks, tok_rows, source_ref, weight_ref, out_ref, heads_ref, held, packed, sems):
     depth = weight_ref.shape[0] // chunks
     width = weight_ref.shape[1]
+    fetch = pltpu.make_async_copy(source_ref, heads_ref, sems.at[chunks])
+    fetch.start()
     copies = []
     for i in range(chunks):
         rows = pl.ds(i * depth, depth)
         copies.append(pltpu.make_async_copy(weight_ref.at[rows], held.at[rows], sems.at[i]))
         copies[i].start()
+    fetch.wait()
     total = jnp.zeros((heads_ref.shape[0], width), F32)
     for i in range(chunks):
         copies[i].wait()
@@ -82,15 +85,16 @@
     return pl.pallas_call(
         functools.partial(project_kernel, chunks, tok_rows),
         out_shape=pltpu.VMEM(packed_shape, BF),
-        in_specs=[whole, pl.BlockSpec(memory_space=pl.ANY)],
+        in_specs=[pl.BlockSpec(memory_space=pl.ANY)] * 2,
         out_specs=whole,
         scratch_shapes=[
+            pltpu.VMEM(heads.shape, BF),
             pltpu.VMEM(weight.shape, BF),
             pltpu.VMEM(packed_shape, F32),
-            pltpu.SemaphoreType.DMA((chunks,)),
+            pltpu.SemaphoreType.DMA((chunks + 1,)),
         ],
         compiler_params=pltpu.CompilerParams(vmem_limit_bytes=14 << 20),
-    )(heads, pltpu.with_memory_space_constraint(weight, pltpu.HBM))
+    )(*[pltpu.with_memory_space_constraint(operand, pltpu.HBM) for operand in (heads, weight)])
 
 
 def stacked(rows, fold):
@@ -218,20 +222,46 @@
     )(returned, placing)
 
 
-def expert_kernel(rows_ref, *refs):
-    *weight_refs, out_ref = refs
+def hidden_of(rows, gate_ref, up_ref):
+    gate_value = jnp.dot(rows, gate_ref[...], preferred_element_type=F32)
+    up_value = jnp.dot(rows, up_ref[...], preferred_element_type=F32)
+    return (jax.nn.silu(gate_value) * up_value).astype(BF)
+
+
+def expert_kernel(rows_ref, gate_ref, up_ref, down_ref, *refs):
+    sources, out_ref, held, sems = refs[0:3], refs[3], refs[4:7], refs[7]
+    copies = [
+        pltpu.make_async_copy(source, target, sems.at[i])
+        for i, (source, target) in enumerate(zip(sources, held))
+    ]
+    for copy in copies:
+        copy.start()
     rows = rows_ref[...]
-    hiddens = []
-    for gate_ref, up_ref in (weight_refs[0:2], weight_refs[3:5]):
-        gate_value = jnp.dot(rows, gate_ref[...], preferred_element_type=F32)
-        up_value = jnp.dot(rows, up_ref[...], preferred_element_type=F32)
-        hiddens.append((jax.nn.silu(gate_value) * up_value).astype(BF))
+    first = hidden_of(rows, gate_ref, up_ref)
+    copies[0].wait()
+    copies[1].wait()
+    second = hidden_of(rows, held[0], held[1])
+    copies[2].wait()
     block = 1280
     for start in range(0, out_ref.shape[1], block):
         span = slice(start, start + block)
-        total = jnp.dot(hiddens[0], weight_refs[2][:, span], preferred_element_type=F32)
-        total = total + jnp.dot(hiddens[1], weight_refs[5][:, span], preferred_element_type=F32)
+        total = jnp.dot(first, down_ref[:, span], preferred_element_type=F32)
+        total = total + jnp.dot(second, held[2][:, span], preferred_element_type=F32)
         out_ref[:, span] = total.astype(BF)
+
+
+def expert(rows, own, other):
+    whole = pl.BlockSpec(memory_space=pltpu.VMEM)
+    outside = pl.BlockSpec(memory_space=pl.ANY)
+    return pl.pallas_call(
+        expert_kernel,
+        out_shape=pltpu.VMEM(rows.shape, BF),
+        in_specs=[whole] * 4 + [outside] * 3,
+        out_specs=whole,
+        scratch_shapes=[pltpu.VMEM(weight.shape, BF) for weight in other]
+        + [pltpu.SemaphoreType.DMA((3,))],
+        compiler_params=pltpu.CompilerParams(vmem_limit_bytes=14 << 20),
+    )(rows, *own, *[pltpu.with_memory_space_constraint(weight, pltpu.HBM) for weight in other])
 
 
 def on_device(attn_heads, out_proj, norm_gain, router, expert_ids, w_gate, w_up, w_down):
@@ -262,7 +292,6 @@
     target = jnp.where(slot_columns < 0, -1, slot_columns * fold + piece_columns)
     placing = (row_range[:, None] == target[None, :]).astype(BF)
 
-    gate, up, down = w_gate[0], w_up[0], w_down[0]
     partial = project(head_rows, out_proj, tok_rows)
     parts = exchange(partial.reshape(tensor_count, 8, -1), "tensor")
     outgoing = route(
@@ -274,20 +303,15 @@
         tok_rows,
         fold,
     )
-    outgoing, gate, up = lax.optimization_barrier((outgoing, gate, up))
-    other_gate = lax.ppermute(gate, "core", swap)
-    other_up = lax.ppermute(up, "core", swap)
+    own = [w_gate[0], w_up[0], w_down[0]]
+    outgoing, own = lax.optimization_barrier((outgoing, own))
+    other = [lax.ppermute(weight, "core", swap) for weight in own]
     arrived = exchange(outgoing, expert_axes)
-    arrived, other_gate, other_up = lax.optimization_barrier((arrived, other_gate, other_up))
+    arrived, own, other = lax.optimization_barrier((arrived, own, other))
     compact, selector = compact_rows(arrived, fold, recv_cap, tensor_count)
-    compact, down = lax.optimization_barrier((compact, down))
-    other_down = lax.ppermute(down, "core", swap)
     rows = exchange(compact, "tensor").reshape(tensor_count * recv_cap, width)
-    rows, other_down = lax.optimization_barrier((rows, other_down))
     rows = spread(rows, "x").reshape(x_count * tensor_count * recv_cap, width)
-    pair_sum = local_call(
-        expert_kernel, rows.shape, rows, gate, up, down, other_gate, other_up, other_down
-    )
+    pair_sum = expert(rows, own, other)
     plane_sum = total_of(
         exchange(pair_sum.reshape(x_count, tensor_count * recv_cap, width), "x")
     ).astype(BF)

time: 164 us -> 162 us (0.988)
  the two profiles are of different devices: /device:TPU:2 before, /device:TPU:8 now
where the time goes in v7:
time: 162 us; the launch traced here: 161 us
  blocking collectives  96.2 us (59%)
  starting transfers between devices  31.5 us (19%)
  waiting for transfers between devices  19.3 us (12%)
  Pallas kernels  11.6 us (7%)
  local copies, waits for them, and re-layouts  1.77 us (1%)
    all_to_all x5, blocking collectives, exchange(): return lax.all_to_all(value, axis, split_axis=0, concat_axis=0, tiled=True)  96.2 us
    all_to_all x2, starting transfers between devices, exchange(): return lax.all_to_all(value, axis, split_axis=0, concat_axis=0, tiled=True)  25.3 us
    all_to_all x2, waiting for transfers between devices, exchange(): return lax.all_to_all(value, axis, split_axis=0, concat_axis=0, tiled=True)  17.5 us
    ppermute x3, starting transfers between devices, on_device(): other = [lax.ppermute(weight, 'core', swap) for weight in own]  6.25 us
    pallas_call x1, Pallas kernels, expert(): pl.pallas_call(expert_kernel, out_shape=pltpu.VMEM(rows.shape, BF), in_sp...  4.08 us
    pallas_call x1, Pallas kernels, project(): pl.pallas_call(functools.partial(project_kernel, chunks, tok_rows), out_s...  4.05 us
  transfers between devices with their start and end apart: 5, of which 4 were waited for; matrix products, arithmetic and copies ran while one was open for 0% of the time, Pallas kernels for 0%

profile of v7, /device:TPU:8, one launch (start us, length us, event | category | flops | bytes accessed | tf_op | source)
XLA Modules:
  0.0 161.1 jit_solution(10079486499942895611)
XLA Ops:
  0.0 0.0 copy-start.7
  0.0 0.0 copy-start.3
  0.0 0.0 copy-start.4
  0.0 4.0 %shard_map.82 = bf16[32,3840]{1,0:T(8,128)(2,1)} custom-call(bf16[24,640]{1,0:T(8,128)(2,1)} %bitcast.33, bf16[640,5120]{1,0:T(8,128)(2,1)} %weight_ref.1), custom_call_target="tpu_custom_call" | custom-call | tf_op jit(solution)/shard_map/pallas_call | solution.py:85
  4.1 0.0 copy-start
  4.1 0.0 copy-start.1
  4.1 14.6 %all-to-all-start = ((bf16[4,8,3840]{2,1,0:T(8,128)(2,1)}), bf16[4,8,3840]{2,1,0:T(8,128)(2,1)S(1)}, u32[]{:S(2)}, u32[]{:S(2)}) async-start(bf16[4,8,3840]{2,1,0:T(8,128)(2,1)} %bitcast.1), calls=%async_computation | async-start | bytes 491520 | tf_op jit(solution)/shard_map/all_to_all | solution.py:16
  18.7 0.0 copy-done.7
  18.7 0.2 convert_reduce_fusion
  18.9 0.1 iota_compare_fusion.2
  19.0 0.1 lt.34
  19.1 0.1 mul.20
  19.2 14.2 %all-to-all-done.parts_ref = bf16[4,8,3840]{2,1,0:T(8,128)(2,1)S(1)} async-done(((bf16[4,8,3840]{2,1,0:T(8,128)(2,1)}), bf16[4,8,3840]{2,1,0:T(8,128)(2,1)S(1)}, u32[]{:S(2)}, u32[]{:S(2)}) %all-to-all-start) | async-done | bytes 245792 | tf_op jit(solution)/shard_map/all_to_all | solution.py:16
  33.5 0.0 copy-done.3
  33.5 0.0 copy-done.4
  33.5 1.6 %shard_map.83 = bf16[192,1280]{1,0:T(8,128)(2,1)} custom-call(bf16[4,8,3840]{2,1,0:T(8,128)(2,1)S(1)} %all-to-all-done.parts_ref, f32[1,5120]{1,0:T(1,128)S(1)} %bitcast.31, bf16[24,5120]{1,0:T(8,128)(2,1)S(1)} %bitcast.30, f32[8,24]{1,0:T(8,128)S(1)} %pad_convert_fusion.member_ref, bf16[192,32]{1,0:T(8,128)(2,1)S(1)} %fusion.1.placing_ref), custom_call_target="tpu_custom_call" | custom-call | tf_op jit(solution)/shard_map/pallas_call | solution.py:143
  35.1 10.7 %all-to-all-start.1 = ((bf16[24,8,1280]{2,1,0:T(8,128)(2,1)}), bf16[24,8,1280]{2,1,0:T(8,128)(2,1)S(1)}, u32[]{:S(2)}, u32[]{:S(2)}) async-start(bf16[24,8,1280]{2,1,0:T(8,128)(2,1)} %bitcast.8), calls=%async_computation.1 | async-start | bytes 983040 | tf_op jit(solution)/shard_map/all_to_all | solution.py:16
  45.8 0.0 copy-done
  45.8 1.9 %collective-permute-start = (bf16[5120,128]{1,0:T(8,128)(2,1)S(1)}, bf16[5120,128]{1,0:T(8,128)(2,1)S(1)}, u32[]{:S(2)}, u32[]{:S(2)}) collective-permute-start(bf16[5120,128]{1,0:T(8,128)(2,1)S(1)} %bitcast.24), channel_id=1, source_target_pairs={{0,96},{96,0},{1,97},{97,1},{2,98},{98,2},{3,99},{99,3},{4,100},{1... | collective-permute-start | bytes 3932168 | tf_op jit(solution)/shard_map/ppermute | solution.py:308
  47.7 0.0 copy-done.1
  47.7 2.4 %collective-permute-start.1 = (bf16[5120,128]{1,0:T(8,128)(2,1)S(1)}, bf16[5120,128]{1,0:T(8,128)(2,1)S(1)}, u32[]{:S(2)}, u32[]{:S(2)}) collective-permute-start(bf16[5120,128]{1,0:T(8,128)(2,1)S(1)} %bitcast.26), channel_id=1, source_target_pairs={{0,96},{96,0},{1,97},{97,1},{2,98},{98,2},{3,99},{99,3},{4,100},{1... | collective-permute-start | bytes 3932168 | tf_op jit(solution)/shard_map/ppermute | solution.py:308
  50.1 1.9 %collective-permute-start.2 = (bf16[128,5120]{1,0:T(8,128)(2,1)}, bf16[128,5120]{1,0:T(8,128)(2,1)}, u32[]{:S(2)}, u32[]{:S(2)}) collective-permute-start(bf16[128,5120]{1,0:T(8,128)(2,1)} %bitcast.28), channel_id=1, source_target_pairs={{0,96},{96,0},{1,97},{97,1},{2,98},{98,2},{3,99},{99,3},{4,100},{1... | collective-permute-start | bytes 3932168 | tf_op jit(solution)/shard_map/ppermute | solution.py:308
  52.1 0.0 collective-permute-done.refs_0_
  52.1 0.0 copy-start.5
  52.1 0.7 collective-permute-done.1.refs_1_
  52.8 0.4 copy-done.5
  53.2 0.0 copy-start.6
  53.2 1.1 copy-done.6
  54.2 1.2 collective-permute-done.2.refs_2_
  55.4 3.2 %all-to-all-done.1 = bf16[24,8,1280]{2,1,0:T(8,128)(2,1)S(1)} async-done(((bf16[24,8,1280]{2,1,0:T(8,128)(2,1)}), bf16[24,8,1280]{2,1,0:T(8,128)(2,1)S(1)}, u32[]{:S(2)}, u32[]{:S(2)}) %all-to-all-start.1) | async-done | bytes 491552 | tf_op jit(solution)/shard_map/all_to_all | solution.py:16
  58.7 0.7 shard_map.84
  59.4 20.9 %all_to_all.48 = bf16[4,8,5120]{2,1,0:T(8,128)(2,1)S(1)} all-to-all(bf16[4,8,5120]{2,1,0:T(8,128)(2,1)S(1)} %get-tuple-element.23), channel_id=1, replica_groups=mesh['x'=4,'core'=2,'tensor'=4,'y'=8,'w'=3] {'tensor'}, dimensions={0} | all-to-all | bytes 655360 | tf_op jit(solution)/shard_map/all_to_all | solution.py:16
  80.3 0.1 broadcast_in_dim.22
  80.4 0.0 copy-start.2
  80.4 16.5 %all_to_all.49 = bf16[4,32,5120]{2,1,0:T(8,128)(2,1)S(1)} all-to-all(bf16[4,32,5120]{2,1,0:T(8,128)(2,1)S(1)} %broadcast_in_dim.22), channel_id=1, replica_groups=mesh['x'=4,'core'=2,'tensor'=4,'y'=8,'w'=3] {'x'}, dimensions={0} | all-to-all | bytes 2621440 | tf_op jit(solution)/shard_map/all_to_all | solution.py:16
  96.9 0.0 copy-done.2
  96.9 4.1 %shard_map.85 = bf16[128,5120]{1,0:T(8,128)(2,1)S(1)} custom-call(bf16[128,5120]{1,0:T(8,128)(2,1)S(1)} %bitcast.19, bf16[5120,128]{1,0:T(8,128)(2,1)S(1)} %bitcast.25, bf16[5120,128]{1,0:T(8,128)(2,1)S(1)} %bitcast.27, bf16[128,5120]{1,0:T(8,128)(2,1)S(1)} %bitcast.29, bf16[5120,128]{1,0:T(8,128)(2,1)} %copy-done.5, bf16[5120,128]{1,0:T(8,128)(2,1)} %copy-done.6, ...), custom_call_target="tpu_custom_call" | custom-call | tf_op jit(solution)/shard_map/pallas_call | solution.py:256
  101.0 14.7 %all_to_all.50 = bf16[4,32,5120]{2,1,0:T(8,128)(2,1)S(1)} all-to-all(bf16[4,32,5120]{2,1,0:T(8,128)(2,1)S(1)} %bitcast.20), channel_id=1, replica_groups=mesh['x'=4,'core'=2,'tensor'=4,'y'=8,'w'=3] {'x'}, dimensions={0} | all-to-all | bytes 2621440 | tf_op jit(solution)/shard_map/all_to_all | solution.py:16
  115.8 0.2 fusion
  115.9 15.1 %all_to_all.51.parts_ref = bf16[4,8,5120]{2,1,0:T(8,128)(2,1)S(1)} all-to-all(bf16[4,8,5120]{2,1,0:T(8,128)(2,1)S(1)} %fusion), channel_id=1, replica_groups=mesh['x'=4,'core'=2,'tensor'=4,'y'=8,'w'=3] {'tensor'}, dimensions={0} | all-to-all | bytes 655360 | tf_op jit(solution)/shard_map/all_to_all | solution.py:16
  131.0 0.3 shard_map.86
  131.3 28.9 %all_to_all.52 = bf16[24,8,1280]{2,1,0:T(8,128)(2,1)S(1)} all-to-all(bf16[24,8,1280]{2,1,0:T(8,128)(2,1)S(1)} %bitcast.22), channel_id=1, replica_groups=mesh['x'=4,'core'=2,'tensor'=4,'y'=8,'w'=3] {'y','w'}, dimensions={0} | all-to-all | bytes 983040 | tf_op jit(solution)/shard_map/all_to_all | solution.py:16
  160.2 0.9 shard_map.87
  (8 shorter events, 0.1 us)
Async XLA Ops:
  0.0 18.7 %copy-start.7 = (s32[1,6,1]{1,2,0:T(1,128)S(1)}, s32[1,6,1]{1,2,0:T(1,128)}, u32[]{:S(2)}) copy-start(s32[1,6,1]{1,2,0:T(1,128)} %param.12) | copy-start | bytes 76
  0.0 33.5 %copy-start.3 = (bf16[5120,24]{0,1:T(8,128)(2,1)S(1)}, bf16[5120,24]{0,1:T(8,128)(2,1)}, u32[]{:S(2)}) copy-start(bf16[5120,24]{0,1:T(8,128)(2,1)} %param.11) | copy-start | bytes 737284
  0.0 33.5 %copy-start.4 = (f32[5120]{0:T(1024)S(1)}, f32[5120]{0:T(1024)}, u32[]{:S(2)}) copy-start(f32[5120]{0:T(1024)} %param.10) | copy-start | bytes 61444
  4.1 41.7 %copy-start = (bf16[1,5120,128]{2,1,0:T(8,128)(2,1)S(1)}, bf16[1,5120,128]{2,1,0:T(8,128)(2,1)}, u32[]{:S(2)}) copy-start(bf16[1,5120,128]{2,1,0:T(8,128)(2,1)} %param.13) | copy-start | bytes 3932164
  4.1 43.6 %copy-start.1 = (bf16[1,5120,128]{2,1,0:T(8,128)(2,1)S(1)}, bf16[1,5120,128]{2,1,0:T(8,128)(2,1)}, u32[]{:S(2)}) copy-start(bf16[1,5120,128]{2,1,0:T(8,128)(2,1)} %param.14) | copy-start | bytes 3932164
  4.1 29.4 %all-to-all-start = ((bf16[4,8,3840]{2,1,0:T(8,128)(2,1)}), bf16[4,8,3840]{2,1,0:T(8,128)(2,1)S(1)}, u32[]{:S(2)}, u32[]{:S(2)}) async-start(bf16[4,8,3840]{2,1,0:T(8,128)(2,1)} %bitcast.1), calls=%async_computation | async-start | bytes 491520 | tf_op jit(solution)/shard_map/all_to_all | solution.py:16
  35.1 23.5 %all-to-all-start.1 = ((bf16[24,8,1280]{2,1,0:T(8,128)(2,1)}), bf16[24,8,1280]{2,1,0:T(8,128)(2,1)S(1)}, u32[]{:S(2)}, u32[]{:S(2)}) async-start(bf16[24,8,1280]{2,1,0:T(8,128)(2,1)} %bitcast.8), calls=%async_computation.1 | async-start | bytes 983040 | tf_op jit(solution)/shard_map/all_to_all | solution.py:16
  45.8 6.3 %collective-permute-start = (bf16[5120,128]{1,0:T(8,128)(2,1)S(1)}, bf16[5120,128]{1,0:T(8,128)(2,1)S(1)}, u32[]{:S(2)}, u32[]{:S(2)}) collective-permute-start(bf16[5120,128]{1,0:T(8,128)(2,1)S(1)} %bitcast.24), channel_id=1, source_target_pairs={{0,96},{96,0},{1,97},{97,1},{2,98},{98,2},{3,99},{99,3},{4,100},{1... | collective-permute-start | bytes 3932168 | tf_op jit(solution)/shard_map/ppermute | solution.py:308
  47.7 5.1 %collective-permute-start.1 = (bf16[5120,128]{1,0:T(8,128)(2,1)S(1)}, bf16[5120,128]{1,0:T(8,128)(2,1)S(1)}, u32[]{:S(2)}, u32[]{:S(2)}) collective-permute-start(bf16[5120,128]{1,0:T(8,128)(2,1)S(1)} %bitcast.26), channel_id=1, source_target_pairs={{0,96},{96,0},{1,97},{97,1},{2,98},{98,2},{3,99},{99,3},{4,100},{1... | collective-permute-start | bytes 3932168 | tf_op jit(solution)/shard_map/ppermute | solution.py:308
  50.1 5.3 %collective-permute-start.2 = (bf16[128,5120]{1,0:T(8,128)(2,1)}, bf16[128,5120]{1,0:T(8,128)(2,1)}, u32[]{:S(2)}, u32[]{:S(2)}) collective-permute-start(bf16[128,5120]{1,0:T(8,128)(2,1)} %bitcast.28), channel_id=1, source_target_pairs={{0,96},{96,0},{1,97},{97,1},{2,98},{98,2},{3,99},{99,3},{4,100},{1... | collective-permute-start | bytes 3932168 | tf_op jit(solution)/shard_map/ppermute | solution.py:308
  52.1 1.1 copy-start.5
  53.2 1.1 copy-start.6
  80.4 16.5 %copy-start.2 = (bf16[1,128,5120]{2,1,0:T(8,128)(2,1)S(1)}, bf16[1,128,5120]{2,1,0:T(8,128)(2,1)}, u32[]{:S(2)}) copy-start(bf16[1,128,5120]{2,1,0:T(8,128)(2,1)} %param.15) | copy-start | bytes 3932164

commit v8 on v7

--- a/solution.py
+++ b/solution.py
@@ -10,6 +10,7 @@
 BF = jnp.bfloat16
 F32 = jnp.float32
 LANES = 128
+PIECES = 4
 
 
 def exchange(value, axis):
@@ -53,17 +54,18 @@
 def project_kernel(chunks, tok_rows, source_ref, weight_ref, out_ref, heads_ref, held, packed, sems):
     depth = weight_ref.shape[0] // chunks
     width = weight_ref.shape[1]
-    fetch = pltpu.make_async_copy(source_ref, heads_ref, sems.at[chunks])
+    fetch = pltpu.make_async_copy(source_ref, heads_ref, sems.at[chunks * PIECES])
     fetch.start()
     copies = []
-    for i in range(chunks):
-        rows = pl.ds(i * depth, depth)
+    for i in range(chunks * PIECES):
+        rows = pl.ds(i * (depth // PIECES), depth // PIECES)
         copies.append(pltpu.make_async_copy(weight_ref.at[rows], held.at[rows], sems.at[i]))
         copies[i].start()
     fetch.wait()
     total = jnp.zeros((heads_ref.shape[0], width), F32)
     for i in range(chunks):
-        copies[i].wait()
+        for copy in copies[i * PIECES : (i + 1) * PIECES]:
+            copy.wait()
         span = slice(i * depth, (i + 1) * depth)
         total = total + jnp.dot(heads_ref[:, span], held[span], preferred_element_type=F32)
     wide, places = folds(tok_rows, width)
@@ -91,7 +93,7 @@
             pltpu.VMEM(heads.shape, BF),
             pltpu.VMEM(weight.shape, BF),
             pltpu.VMEM(packed_shape, F32),
-            pltpu.SemaphoreType.DMA((chunks + 1,)),
+            pltpu.SemaphoreType.DMA((chunks * PIECES + 1,)),
         ],
         compiler_params=pltpu.CompilerParams(vmem_limit_bytes=14 << 20),
     )(*[pltpu.with_memory_space_constraint(operand, pltpu.HBM) for operand in (heads, weight)])
@@ -228,40 +230,33 @@
     return (jax.nn.silu(gate_value) * up_value).astype(BF)
 
 
-def expert_kernel(rows_ref, gate_ref, up_ref, down_ref, *refs):
-    sources, out_ref, held, sems = refs[0:3], refs[3], refs[4:7], refs[7]
-    copies = [
-        pltpu.make_async_copy(source, target, sems.at[i])
-        for i, (source, target) in enumerate(zip(sources, held))
-    ]
-    for copy in copies:
-        copy.start()
+def expert_kernel(rows_ref, gate_ref, up_ref, down_ref, gate2_ref, up2_ref, source_ref, *refs):
+    out_ref, down2_ref, sem = refs
+    fetch = pltpu.make_async_copy(source_ref, down2_ref, sem)
+    fetch.start()
     rows = rows_ref[...]
     first = hidden_of(rows, gate_ref, up_ref)
-    copies[0].wait()
-    copies[1].wait()
-    second = hidden_of(rows, held[0], held[1])
-    copies[2].wait()
+    second = hidden_of(rows, gate2_ref, up2_ref)
+    fetch.wait()
     block = 1280
     for start in range(0, out_ref.shape[1], block):
         span = slice(start, start + block)
         total = jnp.dot(first, down_ref[:, span], preferred_element_type=F32)
-        total = total + jnp.dot(second, held[2][:, span], preferred_element_type=F32)
+        total = total + jnp.dot(second, down2_ref[:, span], preferred_element_type=F32)
         out_ref[:, span] = total.astype(BF)
 
 
 def expert(rows, own, other):
     whole = pl.BlockSpec(memory_space=pltpu.VMEM)
-    outside = pl.BlockSpec(memory_space=pl.ANY)
+    down = pltpu.with_memory_space_constraint(other[2], pltpu.HBM)
     return pl.pallas_call(
         expert_kernel,
         out_shape=pltpu.VMEM(rows.shape, BF),
-        in_specs=[whole] * 4 + [outside] * 3,
-        out_specs=whole,
-        scratch_shapes=[pltpu.VMEM(weight.shape, BF) for weight in other]
-        + [pltpu.SemaphoreType.DMA((3,))],
+        in_specs=[whole] * 6 + [pl.BlockSpec(memory_space=pl.ANY)],
+        out_specs=whole,
+        scratch_shapes=[pltpu.VMEM(down.shape, BF), pltpu.SemaphoreType.DMA],
         compiler_params=pltpu.CompilerParams(vmem_limit_bytes=14 << 20),
-    )(rows, *own, *[pltpu.with_memory_space_constraint(weight, pltpu.HBM) for weight in other])
+    )(rows, *own, *other[:2], down)
 
 
 def on_device(attn_heads, out_proj, norm_gain, router, expert_ids, w_gate, w_up, w_down):

time: 162 us -> 161 us (level)
  transfers between devices with their start and end apart: 5 -> 5, of which waited for: 4 -> 3; matrix products, arithmetic and copies ran while one was open for 0% -> 0% of each run, Pallas kernels for 0% -> 0%
where the time goes in v8:
time: 161 us
  blocking collectives  96.6 us (60%)
  starting transfers between devices  30.2 us (19%)
  waiting for transfers between devices  19.8 us (12%)
  Pallas kernels  11.1 us (7%)
  local copies, waits for them, and re-layouts  2.46 us (2%)
    all_to_all x5, blocking collectives, exchange(): return lax.all_to_all(value, axis, split_axis=0, concat_axis=0, tiled=True)  96.6 us
    all_to_all x2, starting transfers between devices, exchange(): return lax.all_to_all(value, axis, split_axis=0, concat_axis=0, tiled=True)  24 us
    all_to_all x2, waiting for transfers between devices, exchange(): return lax.all_to_all(value, axis, split_axis=0, concat_axis=0, tiled=True)  18.5 us
    ppermute x3, starting transfers between devices, on_device(): other = [lax.ppermute(weight, 'core', swap) for weight in own]  6.25 us
    pallas_call x1, Pallas kernels, project(): pl.pallas_call(functools.partial(project_kernel, chunks, tok_rows), out_s...  4.13 us
    pallas_call x1, Pallas kernels, expert(): pl.pallas_call(expert_kernel, out_shape=pltpu.VMEM(rows.shape, BF), in_sp...  3.51 us
  transfers between devices with their start and end apart: 5, of which 3 were waited for; matrix products, arithmetic and copies ran while one was open for 0% of the time, Pallas kernels for 0%

profile of v8, /device:TPU:8, one launch (start us, length us, event | category | flops | bytes accessed | tf_op | source)
XLA Modules:
  0.0 160.8 jit_solution(1112637556199945155)
XLA Ops:
  0.0 0.0 copy-start.9
  0.0 0.0 copy-start.7
  0.0 0.0 copy-start.8
  0.0 4.1 %shard_map.82 = bf16[32,3840]{1,0:T(8,128)(2,1)} custom-call(bf16[24,640]{1,0:T(8,128)(2,1)} %bitcast.33, bf16[640,5120]{1,0:T(8,128)(2,1)} %weight_ref.1), custom_call_target="tpu_custom_call" | custom-call | tf_op jit(solution)/shard_map/pallas_call | solution.py:87
  4.2 0.0 copy-start
  4.2 0.0 copy-start.1
  4.2 14.6 %all-to-all-start = ((bf16[4,8,3840]{2,1,0:T(8,128)(2,1)}), bf16[4,8,3840]{2,1,0:T(8,128)(2,1)S(1)}, u32[]{:S(2)}, u32[]{:S(2)}) async-start(bf16[4,8,3840]{2,1,0:T(8,128)(2,1)} %bitcast.1), calls=%async_computation | async-start | bytes 491520 | tf_op jit(solution)/shard_map/all_to_all | solution.py:17
  18.8 0.0 copy-done.9
  18.8 0.2 convert_reduce_fusion
  19.0 0.1 iota_compare_fusion.2
  19.1 0.1 lt.34
  19.2 0.1 mul.20
  19.3 14.2 %all-to-all-done.parts_ref = bf16[4,8,3840]{2,1,0:T(8,128)(2,1)S(1)} async-done(((bf16[4,8,3840]{2,1,0:T(8,128)(2,1)}), bf16[4,8,3840]{2,1,0:T(8,128)(2,1)S(1)}, u32[]{:S(2)}, u32[]{:S(2)}) %all-to-all-start) | async-done | bytes 245792 | tf_op jit(solution)/shard_map/all_to_all | solution.py:17
  33.5 0.0 copy-done.7
  33.6 0.0 copy-done.8
  33.6 1.6 %shard_map.83 = bf16[192,1280]{1,0:T(8,128)(2,1)} custom-call(bf16[4,8,3840]{2,1,0:T(8,128)(2,1)S(1)} %all-to-all-done.parts_ref, f32[1,5120]{1,0:T(1,128)S(1)} %bitcast.31, bf16[24,5120]{1,0:T(8,128)(2,1)S(1)} %bitcast.30, f32[8,24]{1,0:T(8,128)S(1)} %pad_convert_fusion.member_ref, bf16[192,32]{1,0:T(8,128)(2,1)S(1)} %fusion.1.placing_ref), custom_call_target="tpu_custom_call" | custom-call | tf_op jit(solution)/shard_map/pallas_call | solution.py:145
  35.2 9.3 %all-to-all-start.1 = ((bf16[24,8,1280]{2,1,0:T(8,128)(2,1)}), bf16[24,8,1280]{2,1,0:T(8,128)(2,1)S(1)}, u32[]{:S(2)}, u32[]{:S(2)}) async-start(bf16[24,8,1280]{2,1,0:T(8,128)(2,1)} %bitcast.8), calls=%async_computation.1 | async-start | bytes 983040 | tf_op jit(solution)/shard_map/all_to_all | solution.py:17
  44.5 0.0 copy-done
  44.5 1.9 %collective-permute-start = (bf16[5120,128]{1,0:T(8,128)(2,1)S(1)}, bf16[5120,128]{1,0:T(8,128)(2,1)S(1)}, u32[]{:S(2)}, u32[]{:S(2)}) collective-permute-start(bf16[5120,128]{1,0:T(8,128)(2,1)S(1)} %bitcast.24), channel_id=1, source_target_pairs={{0,96},{96,0},{1,97},{97,1},{2,98},{98,2},{3,99},{99,3},{4,100},{1... | collective-permute-start | bytes 3932168 | tf_op jit(solution)/shard_map/ppermute | solution.py:303
  46.5 0.0 copy-done.1
  46.5 2.4 %collective-permute-start.1 = (bf16[5120,128]{1,0:T(8,128)(2,1)S(1)}, bf16[5120,128]{1,0:T(8,128)(2,1)S(1)}, u32[]{:S(2)}, u32[]{:S(2)}) collective-permute-start(bf16[5120,128]{1,0:T(8,128)(2,1)S(1)} %bitcast.26), channel_id=1, source_target_pairs={{0,96},{96,0},{1,97},{97,1},{2,98},{98,2},{3,99},{99,3},{4,100},{1... | collective-permute-start | bytes 3932168 | tf_op jit(solution)/shard_map/ppermute | solution.py:303
  48.9 1.9 %collective-permute-start.2 = (bf16[128,5120]{1,0:T(8,128)(2,1)}, bf16[128,5120]{1,0:T(8,128)(2,1)}, u32[]{:S(2)}, u32[]{:S(2)}) collective-permute-start(bf16[128,5120]{1,0:T(8,128)(2,1)} %bitcast.28), channel_id=1, source_target_pairs={{0,96},{96,0},{1,97},{97,1},{2,98},{98,2},{3,99},{99,3},{4,100},{1... | collective-permute-start | bytes 3932168 | tf_op jit(solution)/shard_map/ppermute | solution.py:303
  50.8 0.0 collective-permute-done.gate2_ref
  50.8 0.0 copy-start.3
  50.9 1.1 copy-done.3
  51.9 0.0 collective-permute-done.1.up2_ref
  51.9 0.0 copy-start.5
  51.9 1.1 copy-done.5
  53.0 1.2 collective-permute-done.2.source_ref
  54.2 4.3 %all-to-all-done.1 = bf16[24,8,1280]{2,1,0:T(8,128)(2,1)S(1)} async-done(((bf16[24,8,1280]{2,1,0:T(8,128)(2,1)}), bf16[24,8,1280]{2,1,0:T(8,128)(2,1)S(1)}, u32[]{:S(2)}, u32[]{:S(2)}) %all-to-all-start.1) | async-done | bytes 491552 | tf_op jit(solution)/shard_map/all_to_all | solution.py:17
  58.5 0.7 shard_map.84
  59.2 21.2 %all_to_all.48 = bf16[4,8,5120]{2,1,0:T(8,128)(2,1)S(1)} all-to-all(bf16[4,8,5120]{2,1,0:T(8,128)(2,1)S(1)} %get-tuple-element.23), channel_id=1, replica_groups=mesh['x'=4,'core'=2,'tensor'=4,'y'=8,'w'=3] {'tensor'}, dimensions={0} | all-to-all | bytes 655360 | tf_op jit(solution)/shard_map/all_to_all | solution.py:17
  80.4 0.0 copy-start.6
  80.4 0.1 broadcast_in_dim.22
  80.5 0.0 copy-start.2
  80.5 0.0 copy-start.4
  80.5 16.7 %all_to_all.49 = bf16[4,32,5120]{2,1,0:T(8,128)(2,1)S(1)} all-to-all(bf16[4,32,5120]{2,1,0:T(8,128)(2,1)S(1)} %broadcast_in_dim.22), channel_id=1, replica_groups=mesh['x'=4,'core'=2,'tensor'=4,'y'=8,'w'=3] {'x'}, dimensions={0} | all-to-all | bytes 2621440 | tf_op jit(solution)/shard_map/all_to_all | solution.py:17
  97.2 0.0 copy-done.6
  97.2 0.0 copy-done.2
  97.2 0.0 copy-done.4
  97.2 3.5 %shard_map.85 = bf16[128,5120]{1,0:T(8,128)(2,1)S(1)} custom-call(bf16[128,5120]{1,0:T(8,128)(2,1)S(1)} %bitcast.19, bf16[5120,128]{1,0:T(8,128)(2,1)S(1)} %bitcast.25, bf16[5120,128]{1,0:T(8,128)(2,1)S(1)} %bitcast.27, bf16[128,5120]{1,0:T(8,128)(2,1)S(1)} %bitcast.29, bf16[5120,128]{1,0:T(8,128)(2,1)S(1)} %copy-done.4, bf16[5120,128]{1,0:T(8,128)(2,1)S(1)} %copy-done.6, ...), custom_call_target="tpu_custom_call" | custom-call | tf_op jit(solution)/shard_map/pallas_call | solution.py:252
  100.7 14.7 %all_to_all.50 = bf16[4,32,5120]{2,1,0:T(8,128)(2,1)S(1)} all-to-all(bf16[4,32,5120]{2,1,0:T(8,128)(2,1)S(1)} %bitcast.20), channel_id=1, replica_groups=mesh['x'=4,'core'=2,'tensor'=4,'y'=8,'w'=3] {'x'}, dimensions={0} | all-to-all | bytes 2621440 | tf_op jit(solution)/shard_map/all_to_all | solution.py:17
  115.4 0.2 fusion
  115.6 15.1 %all_to_all.51.parts_ref = bf16[4,8,5120]{2,1,0:T(8,128)(2,1)S(1)} all-to-all(bf16[4,8,5120]{2,1,0:T(8,128)(2,1)S(1)} %fusion), channel_id=1, replica_groups=mesh['x'=4,'core'=2,'tensor'=4,'y'=8,'w'=3] {'tensor'}, dimensions={0} | all-to-all | bytes 655360 | tf_op jit(solution)/shard_map/all_to_all | solution.py:17
  130.7 0.3 shard_map.86
  131.0 28.9 %all_to_all.52 = bf16[24,8,1280]{2,1,0:T(8,128)(2,1)S(1)} all-to-all(bf16[24,8,1280]{2,1,0:T(8,128)(2,1)S(1)} %bitcast.22), channel_id=1, replica_groups=mesh['x'=4,'core'=2,'tensor'=4,'y'=8,'w'=3] {'y','w'}, dimensions={0} | all-to-all | bytes 983040 | tf_op jit(solution)/shard_map/all_to_all | solution.py:17
  159.9 0.9 shard_map.87
  (8 shorter events, 0.1 us)
Async XLA Ops:
  0.0 18.8 %copy-start.9 = (s32[1,6,1]{1,2,0:T(1,128)S(1)}, s32[1,6,1]{1,2,0:T(1,128)}, u32[]{:S(2)}) copy-start(s32[1,6,1]{1,2,0:T(1,128)} %param.12) | copy-start | bytes 76
  0.0 33.5 %copy-start.7 = (bf16[5120,24]{0,1:T(8,128)(2,1)S(1)}, bf16[5120,24]{0,1:T(8,128)(2,1)}, u32[]{:S(2)}) copy-start(bf16[5120,24]{0,1:T(8,128)(2,1)} %param.11) | copy-start | bytes 737284
  0.0 33.5 %copy-start.8 = (f32[5120]{0:T(1024)S(1)}, f32[5120]{0:T(1024)}, u32[]{:S(2)}) copy-start(f32[5120]{0:T(1024)} %param.10) | copy-start | bytes 61444
  4.2 40.4 %copy-start = (bf16[1,5120,128]{2,1,0:T(8,128)(2,1)S(1)}, bf16[1,5120,128]{2,1,0:T(8,128)(2,1)}, u32[]{:S(2)}) copy-start(bf16[1,5120,128]{2,1,0:T(8,128)(2,1)} %param.13) | copy-start | bytes 3932164
  4.2 42.3 %copy-start.1 = (bf16[1,5120,128]{2,1,0:T(8,128)(2,1)S(1)}, bf16[1,5120,128]{2,1,0:T(8,128)(2,1)}, u32[]{:S(2)}) copy-start(bf16[1,5120,128]{2,1,0:T(8,128)(2,1)} %param.14) | copy-start | bytes 3932164
  4.2 29.4 %all-to-all-start = ((bf16[4,8,3840]{2,1,0:T(8,128)(2,1)}), bf16[4,8,3840]{2,1,0:T(8,128)(2,1)S(1)}, u32[]{:S(2)}, u32[]{:S(2)}) async-start(bf16[4,8,3840]{2,1,0:T(8,128)(2,1)} %bitcast.1), calls=%async_computation | async-start | bytes 491520 | tf_op jit(solution)/shard_map/all_to_all | solution.py:17
  35.2 23.3 %all-to-all-start.1 = ((bf16[24,8,1280]{2,1,0:T(8,128)(2,1)}), bf16[24,8,1280]{2,1,0:T(8,128)(2,1)S(1)}, u32[]{:S(2)}, u32[]{:S(2)}) async-start(bf16[24,8,1280]{2,1,0:T(8,128)(2,1)} %bitcast.8), calls=%async_computation.1 | async-start | bytes 983040 | tf_op jit(solution)/shard_map/all_to_all | solution.py:17
  44.5 6.3 %collective-permute-start = (bf16[5120,128]{1,0:T(8,128)(2,1)S(1)}, bf16[5120,128]{1,0:T(8,128)(2,1)S(1)}, u32[]{:S(2)}, u32[]{:S(2)}) collective-permute-start(bf16[5120,128]{1,0:T(8,128)(2,1)S(1)} %bitcast.24), channel_id=1, source_target_pairs={{0,96},{96,0},{1,97},{97,1},{2,98},{98,2},{3,99},{99,3},{4,100},{1... | collective-permute-start | bytes 3932168 | tf_op jit(solution)/shard_map/ppermute | solution.py:303
  46.5 5.4 %collective-permute-start.1 = (bf16[5120,128]{1,0:T(8,128)(2,1)S(1)}, bf16[5120,128]{1,0:T(8,128)(2,1)S(1)}, u32[]{:S(2)}, u32[]{:S(2)}) collective-permute-start(bf16[5120,128]{1,0:T(8,128)(2,1)S(1)} %bitcast.26), channel_id=1, source_target_pairs={{0,96},{96,0},{1,97},{97,1},{2,98},{98,2},{3,99},{99,3},{4,100},{1... | collective-permute-start | bytes 3932168 | tf_op jit(solution)/shard_map/ppermute | solution.py:303
  48.9 5.3 %collective-permute-start.2 = (bf16[128,5120]{1,0:T(8,128)(2,1)}, bf16[128,5120]{1,0:T(8,128)(2,1)}, u32[]{:S(2)}, u32[]{:S(2)}) collective-permute-start(bf16[128,5120]{1,0:T(8,128)(2,1)} %bitcast.28), channel_id=1, source_target_pairs={{0,96},{96,0},{1,97},{97,1},{2,98},{98,2},{3,99},{99,3},{4,100},{1... | collective-permute-start | bytes 3932168 | tf_op jit(solution)/shard_map/ppermute | solution.py:303
  50.8 1.1 copy-start.3
  51.9 1.1 copy-start.5
  80.4 16.8 %copy-start.6 = (bf16[5120,128]{1,0:T(8,128)(2,1)S(1)}, bf16[5120,128]{1,0:T(8,128)(2,1)}, u32[]{:S(2)}) copy-start(bf16[5120,128]{1,0:T(8,128)(2,1)} %copy-done.5) | copy-start | bytes 3932164
  80.5 16.7 %copy-start.2 = (bf16[1,128,5120]{2,1,0:T(8,128)(2,1)S(1)}, bf16[1,128,5120]{2,1,0:T(8,128)(2,1)}, u32[]{:S(2)}) copy-start(bf16[1,128,5120]{2,1,0:T(8,128)(2,1)} %param.15) | copy-start | bytes 3932164
  80.5 16.7 %copy-start.4 = (bf16[5120,128]{1,0:T(8,128)(2,1)S(1)}, bf16[5120,128]{1,0:T(8,128)(2,1)}, u32[]{:S(2)}) copy-start(bf16[5120,128]{1,0:T(8,128)(2,1)} %copy-done.3) | copy-start | bytes 3932164

commit v9 on v8

--- a/solution.py
+++ b/solution.py
@@ -10,7 +10,7 @@
 BF = jnp.bfloat16
 F32 = jnp.float32
 LANES = 128
-PIECES = 4
+PIECE = 64
 
 
 def exchange(value, axis):
@@ -51,23 +51,28 @@
     return wide, [(k, tok_rows + k // each, k % each * rest) for k in range(tok_rows)]
 
 
-def project_kernel(chunks, tok_rows, source_ref, weight_ref, out_ref, heads_ref, held, packed, sems):
-    depth = weight_ref.shape[0] // chunks
-    width = weight_ref.shape[1]
-    fetch = pltpu.make_async_copy(source_ref, heads_ref, sems.at[chunks * PIECES])
+def start_copies(source_ref, target_ref, sems, piece):
+    copies = []
+    for i in range(source_ref.shape[0] // piece):
+        rows = pl.ds(i * piece, piece)
+        copies.append(pltpu.make_async_copy(source_ref.at[rows], target_ref.at[rows], sems.at[i]))
+        copies[i].start()
+    return copies
+
+
+def project_kernel(tok_rows, source_ref, weight_ref, out_ref, heads_ref, held, packed, sem, sems):
+    depth, width = weight_ref.shape
+    fetch = pltpu.make_async_copy(source_ref, heads_ref, sem)
     fetch.start()
-    copies = []
-    for i in range(chunks * PIECES):
-        rows = pl.ds(i * (depth // PIECES), depth // PIECES)
-        copies.append(pltpu.make_async_copy(weight_ref.at[rows], held.at[rows], sems.at[i]))
-        copies[i].start()
+    copies = start_copies(weight_ref, held, sems, PIECE)
     fetch.wait()
-    total = jnp.zeros((heads_ref.shape[0], width), F32)
-    for i in range(chunks):
-        for copy in copies[i * PIECES : (i + 1) * PIECES]:
+    total = None
+    for start in range(0, depth, 256):
+        stop = min(start + 256, depth)
+        for copy in copies[start // PIECE : stop // PIECE]:
             copy.wait()
-        span = slice(i * depth, (i + 1) * depth)
-        total = total + jnp.dot(heads_ref[:, span], held[span], preferred_element_type=F32)
+        part = jnp.dot(heads_ref[:, start:stop], held[start:stop], preferred_element_type=F32)
+        total = part if total is None else total + part
     wide, places = folds(tok_rows, width)
     for peer in range(heads_ref.shape[0] // tok_rows):
         token = peer * tok_rows
@@ -80,12 +85,11 @@
 
 
 def project(heads, weight, tok_rows):
-    chunks = weight.shape[0] // LANES
     wide, _ = folds(tok_rows, weight.shape[1])
     packed_shape = (heads.shape[0] // tok_rows * 8, wide)
     whole = pl.BlockSpec(memory_space=pltpu.VMEM)
     return pl.pallas_call(
-        functools.partial(project_kernel, chunks, tok_rows),
+        functools.partial(project_kernel, tok_rows),
         out_shape=pltpu.VMEM(packed_shape, BF),
         in_specs=[pl.BlockSpec(memory_space=pl.ANY)] * 2,
         out_specs=whole,
@@ -93,7 +97,8 @@
             pltpu.VMEM(heads.shape, BF),
             pltpu.VMEM(weight.shape, BF),
             pltpu.VMEM(packed_shape, F32),
-            pltpu.SemaphoreType.DMA((chunks * PIECES + 1,)),
+            pltpu.SemaphoreType.DMA,
+            pltpu.SemaphoreType.DMA((weight.shape[0] // PIECE,)),
         ],
         compiler_params=pltpu.CompilerParams(vmem_limit_bytes=14 << 20),
     )(*[pltpu.with_memory_space_constraint(operand, pltpu.HBM) for operand in (heads, weight)])
@@ -231,13 +236,13 @@
 
 
 def expert_kernel(rows_ref, gate_ref, up_ref, down_ref, gate2_ref, up2_ref, source_ref, *refs):
-    out_ref, down2_ref, sem = refs
-    fetch = pltpu.make_async_copy(source_ref, down2_ref, sem)
-    fetch.start()
+    out_ref, down2_ref, sems = refs
+    copies = start_copies(source_ref, down2_ref, sems, 16)
     rows = rows_ref[...]
     first = hidden_of(rows, gate_ref, up_ref)
     second = hidden_of(rows, gate2_ref, up2_ref)
-    fetch.wait()
+    for copy in copies:
+        copy.wait()
     block = 1280
     for start in range(0, out_ref.shape[1], block):
         span = slice(start, start + block)
@@ -254,7 +259,10 @@
         out_shape=pltpu.VMEM(rows.shape, BF),
         in_specs=[whole] * 6 + [pl.BlockSpec(memory_space=pl.ANY)],
         out_specs=whole,
-        scratch_shapes=[pltpu.VMEM(down.shape, BF), pltpu.SemaphoreType.DMA],
+        scratch_shapes=[
+            pltpu.VMEM(down.shape, BF),
+            pltpu.SemaphoreType.DMA((down.shape[0] // 16,)),
+        ],
         compiler_params=pltpu.CompilerParams(vmem_limit_bytes=14 << 20),
     )(rows, *own, *other[:2], down)
 

time: 161 us -> 162 us (level)
  no operation moved by 1% of the time
where the time goes in v9:
time: 162 us
  blocking collectives  96.5 us (60%)
  starting transfers between devices  30.2 us (19%)
  waiting for transfers between devices  19.8 us (12%)
  Pallas kernels  11.9 us (7%)
  local copies, waits for them, and re-layouts  2.46 us (2%)
    all_to_all x5, blocking collectives, exchange(): return lax.all_to_all(value, axis, split_axis=0, concat_axis=0, tiled=True)  96.5 us
    all_to_all x2, starting transfers between devices, exchange(): return lax.all_to_all(value, axis, split_axis=0, concat_axis=0, tiled=True)  24 us
    all_to_all x2, waiting for transfers between devices, exchange(): return lax.all_to_all(value, axis, split_axis=0, concat_axis=0, tiled=True)  18.5 us
    ppermute x3, starting transfers between devices, on_device(): other = [lax.ppermute(weight, 'core', swap) for weight in own]  6.25 us
    pallas_call x1, Pallas kernels, project(): pl.pallas_call(functools.partial(project_kernel, tok_rows), out_shape=plt...  4.81 us
    pallas_call x1, Pallas kernels, expert(): pl.pallas_call(expert_kernel, out_shape=pltpu.VMEM(rows.shape, BF), in_sp...  3.64 us
  transfers between devices with their start and end apart: 5, of which 3 were waited for; matrix products, arithmetic and copies ran while one was open for 0% of the time, Pallas kernels for 0%

profile of v9, /device:TPU:8, one launch (start us, length us, event | category | flops | bytes accessed | tf_op | source)
XLA Modules:
  0.0 161.5 jit_solution(6380710250302451013)
XLA Ops:
  0.0 0.0 copy-start.9
  0.0 0.0 copy-start.7
  0.0 0.0 copy-start.8
  0.0 4.8 %shard_map.82 = bf16[32,3840]{1,0:T(8,128)(2,1)} custom-call(bf16[24,640]{1,0:T(8,128)(2,1)} %bitcast.33, bf16[640,5120]{1,0:T(8,128)(2,1)} %weight_ref.1), custom_call_target="tpu_custom_call" | custom-call | tf_op jit(solution)/shard_map/pallas_call | solution.py:91
  4.8 0.0 copy-start
  4.8 0.0 copy-start.1
  4.9 14.6 %all-to-all-start = ((bf16[4,8,3840]{2,1,0:T(8,128)(2,1)}), bf16[4,8,3840]{2,1,0:T(8,128)(2,1)S(1)}, u32[]{:S(2)}, u32[]{:S(2)}) async-start(bf16[4,8,3840]{2,1,0:T(8,128)(2,1)} %bitcast.1), calls=%async_computation | async-start | bytes 491520 | tf_op jit(solution)/shard_map/all_to_all | solution.py:17
  19.5 0.0 copy-done.9
  19.5 0.2 convert_reduce_fusion
  19.7 0.1 iota_compare_fusion.2
  19.8 0.1 lt.34
  19.9 0.1 mul.20
  20.0 14.2 %all-to-all-done.parts_ref = bf16[4,8,3840]{2,1,0:T(8,128)(2,1)S(1)} async-done(((bf16[4,8,3840]{2,1,0:T(8,128)(2,1)}), bf16[4,8,3840]{2,1,0:T(8,128)(2,1)S(1)}, u32[]{:S(2)}, u32[]{:S(2)}) %all-to-all-start) | async-done | bytes 245792 | tf_op jit(solution)/shard_map/all_to_all | solution.py:17
  34.2 0.0 copy-done.7
  34.2 0.0 copy-done.8
  34.2 1.6 %shard_map.83 = bf16[192,1280]{1,0:T(8,128)(2,1)} custom-call(bf16[4,8,3840]{2,1,0:T(8,128)(2,1)S(1)} %all-to-all-done.parts_ref, f32[1,5120]{1,0:T(1,128)S(1)} %bitcast.31, bf16[24,5120]{1,0:T(8,128)(2,1)S(1)} %bitcast.30, f32[8,24]{1,0:T(8,128)S(1)} %pad_convert_fusion.member_ref, bf16[192,32]{1,0:T(8,128)(2,1)S(1)} %fusion.1.placing_ref), custom_call_target="tpu_custom_call" | custom-call | tf_op jit(solution)/shard_map/pallas_call | solution.py:150
  35.9 9.3 %all-to-all-start.1 = ((bf16[24,8,1280]{2,1,0:T(8,128)(2,1)}), bf16[24,8,1280]{2,1,0:T(8,128)(2,1)S(1)}, u32[]{:S(2)}, u32[]{:S(2)}) async-start(bf16[24,8,1280]{2,1,0:T(8,128)(2,1)} %bitcast.8), calls=%async_computation.1 | async-start | bytes 983040 | tf_op jit(solution)/shard_map/all_to_all | solution.py:17
  45.2 0.0 copy-done
  45.2 1.9 %collective-permute-start = (bf16[5120,128]{1,0:T(8,128)(2,1)S(1)}, bf16[5120,128]{1,0:T(8,128)(2,1)S(1)}, u32[]{:S(2)}, u32[]{:S(2)}) collective-permute-start(bf16[5120,128]{1,0:T(8,128)(2,1)S(1)} %bitcast.24), channel_id=1, source_target_pairs={{0,96},{96,0},{1,97},{97,1},{2,98},{98,2},{3,99},{99,3},{4,100},{1... | collective-permute-start | bytes 3932168 | tf_op jit(solution)/shard_map/ppermute | solution.py:311
  47.2 0.0 copy-done.1
  47.2 2.4 %collective-permute-start.1 = (bf16[5120,128]{1,0:T(8,128)(2,1)S(1)}, bf16[5120,128]{1,0:T(8,128)(2,1)S(1)}, u32[]{:S(2)}, u32[]{:S(2)}) collective-permute-start(bf16[5120,128]{1,0:T(8,128)(2,1)S(1)} %bitcast.26), channel_id=1, source_target_pairs={{0,96},{96,0},{1,97},{97,1},{2,98},{98,2},{3,99},{99,3},{4,100},{1... | collective-permute-start | bytes 3932168 | tf_op jit(solution)/shard_map/ppermute | solution.py:311
  49.6 1.9 %collective-permute-start.2 = (bf16[128,5120]{1,0:T(8,128)(2,1)}, bf16[128,5120]{1,0:T(8,128)(2,1)}, u32[]{:S(2)}, u32[]{:S(2)}) collective-permute-start(bf16[128,5120]{1,0:T(8,128)(2,1)} %bitcast.28), channel_id=1, source_target_pairs={{0,96},{96,0},{1,97},{97,1},{2,98},{98,2},{3,99},{99,3},{4,100},{1... | collective-permute-start | bytes 3932168 | tf_op jit(solution)/shard_map/ppermute | solution.py:311
  51.5 0.0 collective-permute-done.gate2_ref
  51.5 0.0 copy-start.3
  51.5 1.1 copy-done.3
  52.6 0.0 collective-permute-done.1.up2_ref
  52.6 0.0 copy-start.5
  52.6 1.1 copy-done.5
  53.7 1.2 collective-permute-done.2.source_ref
  54.9 4.3 %all-to-all-done.1 = bf16[24,8,1280]{2,1,0:T(8,128)(2,1)S(1)} async-done(((bf16[24,8,1280]{2,1,0:T(8,128)(2,1)}), bf16[24,8,1280]{2,1,0:T(8,128)(2,1)S(1)}, u32[]{:S(2)}, u32[]{:S(2)}) %all-to-all-start.1) | async-done | bytes 491552 | tf_op jit(solution)/shard_map/all_to_all | solution.py:17
  59.2 0.7 shard_map.84
  59.9 21.2 %all_to_all.48 = bf16[4,8,5120]{2,1,0:T(8,128)(2,1)S(1)} all-to-all(bf16[4,8,5120]{2,1,0:T(8,128)(2,1)S(1)} %get-tuple-element.23), channel_id=1, replica_groups=mesh['x'=4,'core'=2,'tensor'=4,'y'=8,'w'=3] {'tensor'}, dimensions={0} | all-to-all | bytes 655360 | tf_op jit(solution)/shard_map/all_to_all | solution.py:17
  81.0 0.0 copy-start.6
  81.0 0.1 broadcast_in_dim.22
  81.2 0.0 copy-start.2
  81.2 0.0 copy-start.4
  81.2 16.7 %all_to_all.49 = bf16[4,32,5120]{2,1,0:T(8,128)(2,1)S(1)} all-to-all(bf16[4,32,5120]{2,1,0:T(8,128)(2,1)S(1)} %broadcast_in_dim.22), channel_id=1, replica_groups=mesh['x'=4,'core'=2,'tensor'=4,'y'=8,'w'=3] {'x'}, dimensions={0} | all-to-all | bytes 2621440 | tf_op jit(solution)/shard_map/all_to_all | solution.py:17
  97.9 0.0 copy-done.6
  97.9 0.0 copy-done.2
  97.9 0.0 copy-done.4
  97.9 3.6 %shard_map.85 = bf16[128,5120]{1,0:T(8,128)(2,1)S(1)} custom-call(bf16[128,5120]{1,0:T(8,128)(2,1)S(1)} %bitcast.19, bf16[5120,128]{1,0:T(8,128)(2,1)S(1)} %bitcast.25, bf16[5120,128]{1,0:T(8,128)(2,1)S(1)} %bitcast.27, bf16[128,5120]{1,0:T(8,128)(2,1)S(1)} %bitcast.29, bf16[5120,128]{1,0:T(8,128)(2,1)S(1)} %copy-done.4, bf16[5120,128]{1,0:T(8,128)(2,1)S(1)} %copy-done.6, ...), custom_call_target="tpu_custom_call" | custom-call | tf_op jit(solution)/shard_map/pallas_call | solution.py:257
  101.5 14.7 %all_to_all.50 = bf16[4,32,5120]{2,1,0:T(8,128)(2,1)S(1)} all-to-all(bf16[4,32,5120]{2,1,0:T(8,128)(2,1)S(1)} %bitcast.20), channel_id=1, replica_groups=mesh['x'=4,'core'=2,'tensor'=4,'y'=8,'w'=3] {'x'}, dimensions={0} | all-to-all | bytes 2621440 | tf_op jit(solution)/shard_map/all_to_all | solution.py:17
  116.2 0.2 fusion
  116.4 15.1 %all_to_all.51.parts_ref = bf16[4,8,5120]{2,1,0:T(8,128)(2,1)S(1)} all-to-all(bf16[4,8,5120]{2,1,0:T(8,128)(2,1)S(1)} %fusion), channel_id=1, replica_groups=mesh['x'=4,'core'=2,'tensor'=4,'y'=8,'w'=3] {'tensor'}, dimensions={0} | all-to-all | bytes 655360 | tf_op jit(solution)/shard_map/all_to_all | solution.py:17
  131.5 0.3 shard_map.86
  131.8 28.8 %all_to_all.52 = bf16[24,8,1280]{2,1,0:T(8,128)(2,1)S(1)} all-to-all(bf16[24,8,1280]{2,1,0:T(8,128)(2,1)S(1)} %bitcast.22), channel_id=1, replica_groups=mesh['x'=4,'core'=2,'tensor'=4,'y'=8,'w'=3] {'y','w'}, dimensions={0} | all-to-all | bytes 983040 | tf_op jit(solution)/shard_map/all_to_all | solution.py:17
  160.6 0.9 shard_map.87
  (8 shorter events, 0.1 us)
Async XLA Ops:
  0.0 19.5 %copy-start.9 = (s32[1,6,1]{1,2,0:T(1,128)S(1)}, s32[1,6,1]{1,2,0:T(1,128)}, u32[]{:S(2)}) copy-start(s32[1,6,1]{1,2,0:T(1,128)} %param.12) | copy-start | bytes 76
  0.0 34.2 %copy-start.7 = (bf16[5120,24]{0,1:T(8,128)(2,1)S(1)}, bf16[5120,24]{0,1:T(8,128)(2,1)}, u32[]{:S(2)}) copy-start(bf16[5120,24]{0,1:T(8,128)(2,1)} %param.11) | copy-start | bytes 737284
  0.0 34.2 %copy-start.8 = (f32[5120]{0:T(1024)S(1)}, f32[5120]{0:T(1024)}, u32[]{:S(2)}) copy-start(f32[5120]{0:T(1024)} %param.10) | copy-start | bytes 61444
  4.8 40.4 %copy-start = (bf16[1,5120,128]{2,1,0:T(8,128)(2,1)S(1)}, bf16[1,5120,128]{2,1,0:T(8,128)(2,1)}, u32[]{:S(2)}) copy-start(bf16[1,5120,128]{2,1,0:T(8,128)(2,1)} %param.13) | copy-start | bytes 3932164
  4.8 42.3 %copy-start.1 = (bf16[1,5120,128]{2,1,0:T(8,128)(2,1)S(1)}, bf16[1,5120,128]{2,1,0:T(8,128)(2,1)}, u32[]{:S(2)}) copy-start(bf16[1,5120,128]{2,1,0:T(8,128)(2,1)} %param.14) | copy-start | bytes 3932164
  4.9 29.4 %all-to-all-start = ((bf16[4,8,3840]{2,1,0:T(8,128)(2,1)}), bf16[4,8,3840]{2,1,0:T(8,128)(2,1)S(1)}, u32[]{:S(2)}, u32[]{:S(2)}) async-start(bf16[4,8,3840]{2,1,0:T(8,128)(2,1)} %bitcast.1), calls=%async_computation | async-start | bytes 491520 | tf_op jit(solution)/shard_map/all_to_all | solution.py:17
  35.9 23.3 %all-to-all-start.1 = ((bf16[24,8,1280]{2,1,0:T(8,128)(2,1)}), bf16[24,8,1280]{2,1,0:T(8,128)(2,1)S(1)}, u32[]{:S(2)}, u32[]{:S(2)}) async-start(bf16[24,8,1280]{2,1,0:T(8,128)(2,1)} %bitcast.8), calls=%async_computation.1 | async-start | bytes 983040 | tf_op jit(solution)/shard_map/all_to_all | solution.py:17
  45.2 6.3 %collective-permute-start = (bf16[5120,128]{1,0:T(8,128)(2,1)S(1)}, bf16[5120,128]{1,0:T(8,128)(2,1)S(1)}, u32[]{:S(2)}, u32[]{:S(2)}) collective-permute-start(bf16[5120,128]{1,0:T(8,128)(2,1)S(1)} %bitcast.24), channel_id=1, source_target_pairs={{0,96},{96,0},{1,97},{97,1},{2,98},{98,2},{3,99},{99,3},{4,100},{1... | collective-permute-start | bytes 3932168 | tf_op jit(solution)/shard_map/ppermute | solution.py:311
  47.2 5.4 %collective-permute-start.1 = (bf16[5120,128]{1,0:T(8,128)(2,1)S(1)}, bf16[5120,128]{1,0:T(8,128)(2,1)S(1)}, u32[]{:S(2)}, u32[]{:S(2)}) collective-permute-start(bf16[5120,128]{1,0:T(8,128)(2,1)S(1)} %bitcast.26), channel_id=1, source_target_pairs={{0,96},{96,0},{1,97},{97,1},{2,98},{98,2},{3,99},{99,3},{4,100},{1... | collective-permute-start | bytes 3932168 | tf_op jit(solution)/shard_map/ppermute | solution.py:311
  49.6 5.3 %collective-permute-start.2 = (bf16[128,5120]{1,0:T(8,128)(2,1)}, bf16[128,5120]{1,0:T(8,128)(2,1)}, u32[]{:S(2)}, u32[]{:S(2)}) collective-permute-start(bf16[128,5120]{1,0:T(8,128)(2,1)} %bitcast.28), channel_id=1, source_target_pairs={{0,96},{96,0},{1,97},{97,1},{2,98},{98,2},{3,99},{99,3},{4,100},{1... | collective-permute-start | bytes 3932168 | tf_op jit(solution)/shard_map/ppermute | solution.py:311
  51.5 1.1 copy-start.3
  52.6 1.1 copy-start.5
  81.0 16.8 %copy-start.6 = (bf16[5120,128]{1,0:T(8,128)(2,1)S(1)}, bf16[5120,128]{1,0:T(8,128)(2,1)}, u32[]{:S(2)}) copy-start(bf16[5120,128]{1,0:T(8,128)(2,1)} %copy-done.5) | copy-start | bytes 3932164
  81.2 16.7 %copy-start.2 = (bf16[1,128,5120]{2,1,0:T(8,128)(2,1)S(1)}, bf16[1,128,5120]{2,1,0:T(8,128)(2,1)}, u32[]{:S(2)}) copy-start(bf16[1,128,5120]{2,1,0:T(8,128)(2,1)} %param.15) | copy-start | bytes 3932164
  81.2 16.7 %copy-start.4 = (bf16[5120,128]{1,0:T(8,128)(2,1)S(1)}, bf16[5120,128]{1,0:T(8,128)(2,1)}, u32[]{:S(2)}) copy-start(bf16[5120,128]{1,0:T(8,128)(2,1)} %copy-done.3) | copy-start | bytes 3932164

commit v10 on v8

--- a/solution.py
+++ b/solution.py
@@ -11,6 +11,7 @@
 F32 = jnp.float32
 LANES = 128
 PIECES = 4
+BLOCK = 1280
 
 
 def exchange(value, axis):
@@ -231,17 +232,20 @@
 
 
 def expert_kernel(rows_ref, gate_ref, up_ref, down_ref, gate2_ref, up2_ref, source_ref, *refs):
-    out_ref, down2_ref, sem = refs
-    fetch = pltpu.make_async_copy(source_ref, down2_ref, sem)
-    fetch.start()
+    out_ref, down2_ref, sems = refs
+    spans = [pl.ds(i * BLOCK, BLOCK) for i in range(out_ref.shape[1] // BLOCK)]
+    copies = [
+        pltpu.make_async_copy(source_ref.at[:, span], down2_ref.at[:, span], sems.at[i])
+        for i, span in enumerate(spans)
+    ]
+    for copy in copies:
+        copy.start()
     rows = rows_ref[...]
     first = hidden_of(rows, gate_ref, up_ref)
     second = hidden_of(rows, gate2_ref, up2_ref)
-    fetch.wait()
-    block = 1280
-    for start in range(0, out_ref.shape[1], block):
-        span = slice(start, start + block)
+    for copy, span in zip(copies, spans):
         total = jnp.dot(first, down_ref[:, span], preferred_element_type=F32)
+        copy.wait()
         total = total + jnp.dot(second, down2_ref[:, span], preferred_element_type=F32)
         out_ref[:, span] = total.astype(BF)
 
@@ -254,7 +258,10 @@
         out_shape=pltpu.VMEM(rows.shape, BF),
         in_specs=[whole] * 6 + [pl.BlockSpec(memory_space=pl.ANY)],
         out_specs=whole,
-        scratch_shapes=[pltpu.VMEM(down.shape, BF), pltpu.SemaphoreType.DMA],
+        scratch_shapes=[
+            pltpu.VMEM(down.shape, BF),
+            pltpu.SemaphoreType.DMA((down.shape[1] // BLOCK,)),
+        ],
         compiler_params=pltpu.CompilerParams(vmem_limit_bytes=14 << 20),
     )(rows, *own, *other[:2], down)
 

time: 161 us -> 162 us (level)
  no operation moved by 1% of the time
where the time goes in v10:
time: 162 us; the launch traced here: 161 us
  blocking collectives  96.6 us (60%)
  starting transfers between devices  30.2 us (19%)
  waiting for transfers between devices  19.8 us (12%)
  Pallas kernels  11.5 us (7%)
  local copies, waits for them, and re-layouts  2.46 us (2%)
    all_to_all x5, blocking collectives, exchange(): return lax.all_to_all(value, axis, split_axis=0, concat_axis=0, tiled=True)  96.6 us
    all_to_all x2, starting transfers between devices, exchange(): return lax.all_to_all(value, axis, split_axis=0, concat_axis=0, tiled=True)  24 us
    all_to_all x2, waiting for transfers between devices, exchange(): return lax.all_to_all(value, axis, split_axis=0, concat_axis=0, tiled=True)  18.5 us
    ppermute x3, starting transfers between devices, on_device(): other = [lax.ppermute(weight, 'core', swap) for weight in own]  6.25 us
    pallas_call x1, Pallas kernels, project(): pl.pallas_call(functools.partial(project_kernel, chunks, tok_rows), out_s...  4.13 us
    pallas_call x1, Pallas kernels, expert(): pl.pallas_call(expert_kernel, out_shape=pltpu.VMEM(rows.shape, BF), in_sp...  3.84 us
  transfers between devices with their start and end apart: 5, of which 3 were waited for; matrix products, arithmetic and copies ran while one was open for 0% of the time, Pallas kernels for 0%

profile of v10, /device:TPU:8, one launch (start us, length us, event | category | flops | bytes accessed | tf_op | source)
XLA Modules:
  0.0 161.1 jit_solution(7952502711621960776)
XLA Ops:
  0.0 0.0 copy-start.9
  0.0 0.0 copy-start.7
  0.0 0.0 copy-start.8
  0.0 4.1 %shard_map.82 = bf16[32,3840]{1,0:T(8,128)(2,1)} custom-call(bf16[24,640]{1,0:T(8,128)(2,1)} %bitcast.33, bf16[640,5120]{1,0:T(8,128)(2,1)} %weight_ref.1), custom_call_target="tpu_custom_call" | custom-call | tf_op jit(solution)/shard_map/pallas_call | solution.py:88
  4.2 0.0 copy-start
  4.2 0.0 copy-start.1
  4.2 14.6 %all-to-all-start = ((bf16[4,8,3840]{2,1,0:T(8,128)(2,1)}), bf16[4,8,3840]{2,1,0:T(8,128)(2,1)S(1)}, u32[]{:S(2)}, u32[]{:S(2)}) async-start(bf16[4,8,3840]{2,1,0:T(8,128)(2,1)} %bitcast.1), calls=%async_computation | async-start | bytes 491520 | tf_op jit(solution)/shard_map/all_to_all | solution.py:18
  18.8 0.0 copy-done.9
  18.8 0.2 convert_reduce_fusion
  19.0 0.1 iota_compare_fusion.2
  19.1 0.1 lt.34
  19.2 0.1 mul.20
  19.3 14.2 %all-to-all-done.parts_ref = bf16[4,8,3840]{2,1,0:T(8,128)(2,1)S(1)} async-done(((bf16[4,8,3840]{2,1,0:T(8,128)(2,1)}), bf16[4,8,3840]{2,1,0:T(8,128)(2,1)S(1)}, u32[]{:S(2)}, u32[]{:S(2)}) %all-to-all-start) | async-done | bytes 245792 | tf_op jit(solution)/shard_map/all_to_all | solution.py:18
  33.5 0.0 copy-done.7
  33.6 0.0 copy-done.8
  33.6 1.6 %shard_map.83 = bf16[192,1280]{1,0:T(8,128)(2,1)} custom-call(bf16[4,8,3840]{2,1,0:T(8,128)(2,1)S(1)} %all-to-all-done.parts_ref, f32[1,5120]{1,0:T(1,128)S(1)} %bitcast.31, bf16[24,5120]{1,0:T(8,128)(2,1)S(1)} %bitcast.30, f32[8,24]{1,0:T(8,128)S(1)} %pad_convert_fusion.member_ref, bf16[192,32]{1,0:T(8,128)(2,1)S(1)} %fusion.1.placing_ref), custom_call_target="tpu_custom_call" | custom-call | tf_op jit(solution)/shard_map/pallas_call | solution.py:146
  35.2 9.3 %all-to-all-start.1 = ((bf16[24,8,1280]{2,1,0:T(8,128)(2,1)}), bf16[24,8,1280]{2,1,0:T(8,128)(2,1)S(1)}, u32[]{:S(2)}, u32[]{:S(2)}) async-start(bf16[24,8,1280]{2,1,0:T(8,128)(2,1)} %bitcast.8), calls=%async_computation.1 | async-start | bytes 983040 | tf_op jit(solution)/shard_map/all_to_all | solution.py:18
  44.5 0.0 copy-done
  44.5 1.9 %collective-permute-start = (bf16[5120,128]{1,0:T(8,128)(2,1)S(1)}, bf16[5120,128]{1,0:T(8,128)(2,1)S(1)}, u32[]{:S(2)}, u32[]{:S(2)}) collective-permute-start(bf16[5120,128]{1,0:T(8,128)(2,1)S(1)} %bitcast.24), channel_id=1, source_target_pairs={{0,96},{96,0},{1,97},{97,1},{2,98},{98,2},{3,99},{99,3},{4,100},{1... | collective-permute-start | bytes 3932168 | tf_op jit(solution)/shard_map/ppermute | solution.py:310
  46.5 0.0 copy-done.1
  46.5 2.4 %collective-permute-start.1 = (bf16[5120,128]{1,0:T(8,128)(2,1)S(1)}, bf16[5120,128]{1,0:T(8,128)(2,1)S(1)}, u32[]{:S(2)}, u32[]{:S(2)}) collective-permute-start(bf16[5120,128]{1,0:T(8,128)(2,1)S(1)} %bitcast.26), channel_id=1, source_target_pairs={{0,96},{96,0},{1,97},{97,1},{2,98},{98,2},{3,99},{99,3},{4,100},{1... | collective-permute-start | bytes 3932168 | tf_op jit(solution)/shard_map/ppermute | solution.py:310
  48.9 1.9 %collective-permute-start.2 = (bf16[128,5120]{1,0:T(8,128)(2,1)}, bf16[128,5120]{1,0:T(8,128)(2,1)}, u32[]{:S(2)}, u32[]{:S(2)}) collective-permute-start(bf16[128,5120]{1,0:T(8,128)(2,1)} %bitcast.28), channel_id=1, source_target_pairs={{0,96},{96,0},{1,97},{97,1},{2,98},{98,2},{3,99},{99,3},{4,100},{1... | collective-permute-start | bytes 3932168 | tf_op jit(solution)/shard_map/ppermute | solution.py:310
  50.8 0.0 collective-permute-done.gate2_ref
  50.8 0.0 copy-start.3
  50.9 1.1 copy-done.3
  51.9 0.0 collective-permute-done.1.up2_ref
  51.9 0.0 copy-start.5
  51.9 1.1 copy-done.5
  53.0 1.2 collective-permute-done.2.source_ref
  54.2 4.3 %all-to-all-done.1 = bf16[24,8,1280]{2,1,0:T(8,128)(2,1)S(1)} async-done(((bf16[24,8,1280]{2,1,0:T(8,128)(2,1)}), bf16[24,8,1280]{2,1,0:T(8,128)(2,1)S(1)}, u32[]{:S(2)}, u32[]{:S(2)}) %all-to-all-start.1) | async-done | bytes 491552 | tf_op jit(solution)/shard_map/all_to_all | solution.py:18
  58.5 0.7 shard_map.84
  59.2 21.2 %all_to_all.48 = bf16[4,8,5120]{2,1,0:T(8,128)(2,1)S(1)} all-to-all(bf16[4,8,5120]{2,1,0:T(8,128)(2,1)S(1)} %get-tuple-element.23), channel_id=1, replica_groups=mesh['x'=4,'core'=2,'tensor'=4,'y'=8,'w'=3] {'tensor'}, dimensions={0} | all-to-all | bytes 655360 | tf_op jit(solution)/shard_map/all_to_all | solution.py:18
  80.4 0.0 copy-start.6
  80.4 0.1 broadcast_in_dim.22
  80.5 0.0 copy-start.2
  80.5 0.0 copy-start.4
  80.5 16.7 %all_to_all.49 = bf16[4,32,5120]{2,1,0:T(8,128)(2,1)S(1)} all-to-all(bf16[4,32,5120]{2,1,0:T(8,128)(2,1)S(1)} %broadcast_in_dim.22), channel_id=1, replica_groups=mesh['x'=4,'core'=2,'tensor'=4,'y'=8,'w'=3] {'x'}, dimensions={0} | all-to-all | bytes 2621440 | tf_op jit(solution)/shard_map/all_to_all | solution.py:18
  97.2 0.0 copy-done.6
  97.2 0.0 copy-done.2
  97.2 0.0 copy-done.4
  97.2 3.8 %shard_map.85 = bf16[128,5120]{1,0:T(8,128)(2,1)S(1)} custom-call(bf16[128,5120]{1,0:T(8,128)(2,1)S(1)} %bitcast.19, bf16[5120,128]{1,0:T(8,128)(2,1)S(1)} %bitcast.25, bf16[5120,128]{1,0:T(8,128)(2,1)S(1)} %bitcast.27, bf16[128,5120]{1,0:T(8,128)(2,1)S(1)} %bitcast.29, bf16[5120,128]{1,0:T(8,128)(2,1)S(1)} %copy-done.4, bf16[5120,128]{1,0:T(8,128)(2,1)S(1)} %copy-done.6, ...), custom_call_target="tpu_custom_call" | custom-call | tf_op jit(solution)/shard_map/pallas_call | solution.py:256
  101.0 14.7 %all_to_all.50 = bf16[4,32,5120]{2,1,0:T(8,128)(2,1)S(1)} all-to-all(bf16[4,32,5120]{2,1,0:T(8,128)(2,1)S(1)} %bitcast.20), channel_id=1, replica_groups=mesh['x'=4,'core'=2,'tensor'=4,'y'=8,'w'=3] {'x'}, dimensions={0} | all-to-all | bytes 2621440 | tf_op jit(solution)/shard_map/all_to_all | solution.py:18
  115.8 0.2 fusion
  115.9 15.1 %all_to_all.51.parts_ref = bf16[4,8,5120]{2,1,0:T(8,128)(2,1)S(1)} all-to-all(bf16[4,8,5120]{2,1,0:T(8,128)(2,1)S(1)} %fusion), channel_id=1, replica_groups=mesh['x'=4,'core'=2,'tensor'=4,'y'=8,'w'=3] {'tensor'}, dimensions={0} | all-to-all | bytes 655360 | tf_op jit(solution)/shard_map/all_to_all | solution.py:18
  131.1 0.3 shard_map.86
  131.3 28.9 %all_to_all.52 = bf16[24,8,1280]{2,1,0:T(8,128)(2,1)S(1)} all-to-all(bf16[24,8,1280]{2,1,0:T(8,128)(2,1)S(1)} %bitcast.22), channel_id=1, replica_groups=mesh['x'=4,'core'=2,'tensor'=4,'y'=8,'w'=3] {'y','w'}, dimensions={0} | all-to-all | bytes 983040 | tf_op jit(solution)/shard_map/all_to_all | solution.py:18
  160.2 0.9 shard_map.87
  (8 shorter events, 0.1 us)
Async XLA Ops:
  0.0 18.8 %copy-start.9 = (s32[1,6,1]{1,2,0:T(1,128)S(1)}, s32[1,6,1]{1,2,0:T(1,128)}, u32[]{:S(2)}) copy-start(s32[1,6,1]{1,2,0:T(1,128)} %param.12) | copy-start | bytes 76
  0.0 33.5 %copy-start.7 = (bf16[5120,24]{0,1:T(8,128)(2,1)S(1)}, bf16[5120,24]{0,1:T(8,128)(2,1)}, u32[]{:S(2)}) copy-start(bf16[5120,24]{0,1:T(8,128)(2,1)} %param.11) | copy-start | bytes 737284
  0.0 33.5 %copy-start.8 = (f32[5120]{0:T(1024)S(1)}, f32[5120]{0:T(1024)}, u32[]{:S(2)}) copy-start(f32[5120]{0:T(1024)} %param.10) | copy-start | bytes 61444
  4.2 40.4 %copy-start = (bf16[1,5120,128]{2,1,0:T(8,128)(2,1)S(1)}, bf16[1,5120,128]{2,1,0:T(8,128)(2,1)}, u32[]{:S(2)}) copy-start(bf16[1,5120,128]{2,1,0:T(8,128)(2,1)} %param.13) | copy-start | bytes 3932164
  4.2 42.3 %copy-start.1 = (bf16[1,5120,128]{2,1,0:T(8,128)(2,1)S(1)}, bf16[1,5120,128]{2,1,0:T(8,128)(2,1)}, u32[]{:S(2)}) copy-start(bf16[1,5120,128]{2,1,0:T(8,128)(2,1)} %param.14) | copy-start | bytes 3932164
  4.2 29.4 %all-to-all-start = ((bf16[4,8,3840]{2,1,0:T(8,128)(2,1)}), bf16[4,8,3840]{2,1,0:T(8,128)(2,1)S(1)}, u32[]{:S(2)}, u32[]{:S(2)}) async-start(bf16[4,8,3840]{2,1,0:T(8,128)(2,1)} %bitcast.1), calls=%async_computation | async-start | bytes 491520 | tf_op jit(solution)/shard_map/all_to_all | solution.py:18
  35.2 23.3 %all-to-all-start.1 = ((bf16[24,8,1280]{2,1,0:T(8,128)(2,1)}), bf16[24,8,1280]{2,1,0:T(8,128)(2,1)S(1)}, u32[]{:S(2)}, u32[]{:S(2)}) async-start(bf16[24,8,1280]{2,1,0:T(8,128)(2,1)} %bitcast.8), calls=%async_computation.1 | async-start | bytes 983040 | tf_op jit(solution)/shard_map/all_to_all | solution.py:18
  44.5 6.3 %collective-permute-start = (bf16[5120,128]{1,0:T(8,128)(2,1)S(1)}, bf16[5120,128]{1,0:T(8,128)(2,1)S(1)}, u32[]{:S(2)}, u32[]{:S(2)}) collective-permute-start(bf16[5120,128]{1,0:T(8,128)(2,1)S(1)} %bitcast.24), channel_id=1, source_target_pairs={{0,96},{96,0},{1,97},{97,1},{2,98},{98,2},{3,99},{99,3},{4,100},{1... | collective-permute-start | bytes 3932168 | tf_op jit(solution)/shard_map/ppermute | solution.py:310
  46.5 5.4 %collective-permute-start.1 = (bf16[5120,128]{1,0:T(8,128)(2,1)S(1)}, bf16[5120,128]{1,0:T(8,128)(2,1)S(1)}, u32[]{:S(2)}, u32[]{:S(2)}) collective-permute-start(bf16[5120,128]{1,0:T(8,128)(2,1)S(1)} %bitcast.26), channel_id=1, source_target_pairs={{0,96},{96,0},{1,97},{97,1},{2,98},{98,2},{3,99},{99,3},{4,100},{1... | collective-permute-start | bytes 3932168 | tf_op jit(solution)/shard_map/ppermute | solution.py:310
  48.9 5.3 %collective-permute-start.2 = (bf16[128,5120]{1,0:T(8,128)(2,1)}, bf16[128,5120]{1,0:T(8,128)(2,1)}, u32[]{:S(2)}, u32[]{:S(2)}) collective-permute-start(bf16[128,5120]{1,0:T(8,128)(2,1)} %bitcast.28), channel_id=1, source_target_pairs={{0,96},{96,0},{1,97},{97,1},{2,98},{98,2},{3,99},{99,3},{4,100},{1... | collective-permute-start | bytes 3932168 | tf_op jit(solution)/shard_map/ppermute | solution.py:310
  50.8 1.1 copy-start.3
  51.9 1.1 copy-start.5
  80.4 16.8 %copy-start.6 = (bf16[5120,128]{1,0:T(8,128)(2,1)S(1)}, bf16[5120,128]{1,0:T(8,128)(2,1)}, u32[]{:S(2)}) copy-start(bf16[5120,128]{1,0:T(8,128)(2,1)} %copy-done.5) | copy-start | bytes 3932164
  80.5 16.7 %copy-start.2 = (bf16[1,128,5120]{2,1,0:T(8,128)(2,1)S(1)}, bf16[1,128,5120]{2,1,0:T(8,128)(2,1)}, u32[]{:S(2)}) copy-start(bf16[1,128,5120]{2,1,0:T(8,128)(2,1)} %param.15) | copy-start | bytes 3932164
  80.5 16.7 %copy-start.4 = (bf16[5120,128]{1,0:T(8,128)(2,1)S(1)}, bf16[5120,128]{1,0:T(8,128)(2,1)}, u32[]{:S(2)}) copy-start(bf16[5120,128]{1,0:T(8,128)(2,1)} %copy-done.3) | copy-start | bytes 3932164

commit v11 on v8

--- a/solution.py
+++ b/solution.py
@@ -230,33 +230,18 @@
     return (jax.nn.silu(gate_value) * up_value).astype(BF)
 
 
-def expert_kernel(rows_ref, gate_ref, up_ref, down_ref, gate2_ref, up2_ref, source_ref, *refs):
-    out_ref, down2_ref, sem = refs
-    fetch = pltpu.make_async_copy(source_ref, down2_ref, sem)
-    fetch.start()
+def expert_kernel(
+    rows_ref, gate_ref, up_ref, down_ref, gate2_ref, up2_ref, down2_ref, out_ref
+):
     rows = rows_ref[...]
     first = hidden_of(rows, gate_ref, up_ref)
     second = hidden_of(rows, gate2_ref, up2_ref)
-    fetch.wait()
     block = 1280
     for start in range(0, out_ref.shape[1], block):
         span = slice(start, start + block)
         total = jnp.dot(first, down_ref[:, span], preferred_element_type=F32)
         total = total + jnp.dot(second, down2_ref[:, span], preferred_element_type=F32)
         out_ref[:, span] = total.astype(BF)
-
-
-def expert(rows, own, other):
-    whole = pl.BlockSpec(memory_space=pltpu.VMEM)
-    down = pltpu.with_memory_space_constraint(other[2], pltpu.HBM)
-    return pl.pallas_call(
-        expert_kernel,
-        out_shape=pltpu.VMEM(rows.shape, BF),
-        in_specs=[whole] * 6 + [pl.BlockSpec(memory_space=pl.ANY)],
-        out_specs=whole,
-        scratch_shapes=[pltpu.VMEM(down.shape, BF), pltpu.SemaphoreType.DMA],
-        compiler_params=pltpu.CompilerParams(vmem_limit_bytes=14 << 20),
-    )(rows, *own, *other[:2], down)
 
 
 def on_device(attn_heads, out_proj, norm_gain, router, expert_ids, w_gate, w_up, w_down):
@@ -306,7 +291,7 @@
     compact, selector = compact_rows(arrived, fold, recv_cap, tensor_count)
     rows = exchange(compact, "tensor").reshape(tensor_count * recv_cap, width)
     rows = spread(rows, "x").reshape(x_count * tensor_count * recv_cap, width)
-    pair_sum = expert(rows, own, other)
+    pair_sum = local_call(expert_kernel, rows.shape, rows, *own, *other)
     plane_sum = total_of(
         exchange(pair_sum.reshape(x_count, tensor_count * recv_cap, width), "x")
     ).astype(BF)

time: 161 us -> 161 us (level)
    pallas_call x1 -> x0, Pallas kernels: 3.51 us -> none  [expert(): pl.pallas_call(expert_kernel, out_shape=pltpu.VMEM(rows.shape, BF), in_sp...]
    pallas_call x1 -> x2, Pallas kernels: 0.27 us -> 2.57 us  [local_call(): pl.pallas_call(kernel, out_shape=pltpu.VMEM(shape, BF), in_specs=[whole]...]
    unnamed x20 -> x24, local copies, waits for them, and re-layouts: 2.16 us -> 3.25 us
where the time goes in v11:
time: 161 us
  blocking collectives  97.8 us (61%)
  starting transfers between devices  30.2 us (19%)
  waiting for transfers between devices  18.7 us (12%)
  Pallas kernels  9.91 us (6%)
  local copies, waits for them, and re-layouts  3.55 us (2%)
    all_to_all x5, blocking collectives, exchange(): return lax.all_to_all(value, axis, split_axis=0, concat_axis=0, tiled=True)  97.8 us
    all_to_all x2, starting transfers between devices, exchange(): return lax.all_to_all(value, axis, split_axis=0, concat_axis=0, tiled=True)  24 us
    all_to_all x2, waiting for transfers between devices, exchange(): return lax.all_to_all(value, axis, split_axis=0, concat_axis=0, tiled=True)  17.6 us
    ppermute x3, starting transfers between devices, on_device(): other = [lax.ppermute(weight, 'core', swap) for weight in own]  6.25 us
    pallas_call x1, Pallas kernels, project(): pl.pallas_call(functools.partial(project_kernel, chunks, tok_rows), out_s...  4.13 us
    unnamed x24, local copies, waits for them, and re-layouts  3.25 us
  transfers between devices with their start and end apart: 5, of which 3 were waited for; matrix products, arithmetic and copies ran while one was open for 0% of the time, Pallas kernels for 0%

profile of v11, /device:TPU:8, one launch (start us, length us, event | category | flops | bytes accessed | tf_op | source)
XLA Modules:
  0.0 160.8 jit_solution(12550817606843841490)
XLA Ops:
  0.0 0.0 copy-start.11
  0.0 0.0 copy-start.9
  0.0 0.0 copy-start.10
  0.0 4.1 %shard_map.82 = bf16[32,3840]{1,0:T(8,128)(2,1)} custom-call(bf16[24,640]{1,0:T(8,128)(2,1)} %bitcast.33, bf16[640,5120]{1,0:T(8,128)(2,1)} %weight_ref.1), custom_call_target="tpu_custom_call" | custom-call | tf_op jit(solution)/shard_map/pallas_call | solution.py:87
  4.1 0.0 copy-start
  4.2 0.0 copy-start.1
  4.2 14.6 %all-to-all-start = ((bf16[4,8,3840]{2,1,0:T(8,128)(2,1)}), bf16[4,8,3840]{2,1,0:T(8,128)(2,1)S(1)}, u32[]{:S(2)}, u32[]{:S(2)}) async-start(bf16[4,8,3840]{2,1,0:T(8,128)(2,1)} %bitcast.1), calls=%async_computation | async-start | bytes 491520 | tf_op jit(solution)/shard_map/all_to_all | solution.py:17
  18.8 0.0 copy-done.11
  18.8 0.2 convert_reduce_fusion
  19.0 0.1 iota_compare_fusion.2
  19.1 0.1 lt.34
  19.2 0.1 mul.20
  19.3 14.2 %all-to-all-done.parts_ref = bf16[4,8,3840]{2,1,0:T(8,128)(2,1)S(1)} async-done(((bf16[4,8,3840]{2,1,0:T(8,128)(2,1)}), bf16[4,8,3840]{2,1,0:T(8,128)(2,1)S(1)}, u32[]{:S(2)}, u32[]{:S(2)}) %all-to-all-start) | async-done | bytes 245792 | tf_op jit(solution)/shard_map/all_to_all | solution.py:17
  33.5 0.0 copy-done.9
  33.5 0.0 copy-done.10
  33.5 1.6 %shard_map.83 = bf16[192,1280]{1,0:T(8,128)(2,1)} custom-call(bf16[4,8,3840]{2,1,0:T(8,128)(2,1)S(1)} %all-to-all-done.parts_ref, f32[1,5120]{1,0:T(1,128)S(1)} %bitcast.31, bf16[24,5120]{1,0:T(8,128)(2,1)S(1)} %bitcast.30, f32[8,24]{1,0:T(8,128)S(1)} %pad_convert_fusion.member_ref, bf16[192,32]{1,0:T(8,128)(2,1)S(1)} %fusion.1.placing_ref), custom_call_target="tpu_custom_call" | custom-call | tf_op jit(solution)/shard_map/pallas_call | solution.py:145
  35.2 9.3 %all-to-all-start.1 = ((bf16[24,8,1280]{2,1,0:T(8,128)(2,1)}), bf16[24,8,1280]{2,1,0:T(8,128)(2,1)S(1)}, u32[]{:S(2)}, u32[]{:S(2)}) async-start(bf16[24,8,1280]{2,1,0:T(8,128)(2,1)} %bitcast.8), calls=%async_computation.1 | async-start | bytes 983040 | tf_op jit(solution)/shard_map/all_to_all | solution.py:17
  44.5 0.0 copy-done
  44.5 1.9 %collective-permute-start = (bf16[5120,128]{1,0:T(8,128)(2,1)S(1)}, bf16[5120,128]{1,0:T(8,128)(2,1)S(1)}, u32[]{:S(2)}, u32[]{:S(2)}) collective-permute-start(bf16[5120,128]{1,0:T(8,128)(2,1)S(1)} %bitcast.24), channel_id=1, source_target_pairs={{0,96},{96,0},{1,97},{97,1},{2,98},{98,2},{3,99},{99,3},{4,100},{1... | collective-permute-start | bytes 3932168 | tf_op jit(solution)/shard_map/ppermute | solution.py:288
  46.5 0.0 copy-done.1
  46.5 2.4 %collective-permute-start.1 = (bf16[5120,128]{1,0:T(8,128)(2,1)S(1)}, bf16[5120,128]{1,0:T(8,128)(2,1)S(1)}, u32[]{:S(2)}, u32[]{:S(2)}) collective-permute-start(bf16[5120,128]{1,0:T(8,128)(2,1)S(1)} %bitcast.26), channel_id=1, source_target_pairs={{0,96},{96,0},{1,97},{97,1},{2,98},{98,2},{3,99},{99,3},{4,100},{1... | collective-permute-start | bytes 3932168 | tf_op jit(solution)/shard_map/ppermute | solution.py:288
  48.9 1.9 %collective-permute-start.2 = (bf16[128,5120]{1,0:T(8,128)(2,1)}, bf16[128,5120]{1,0:T(8,128)(2,1)S(1)}, u32[]{:S(2)}, u32[]{:S(2)}) collective-permute-start(bf16[128,5120]{1,0:T(8,128)(2,1)} %bitcast.28), channel_id=1, source_target_pairs={{0,96},{96,0},{1,97},{97,1},{2,98},{98,2},{3,99},{99,3},{4,100},{1... | collective-permute-start | bytes 3932168 | tf_op jit(solution)/shard_map/ppermute | solution.py:288
  50.8 0.0 collective-permute-done.gate2_ref
  50.8 0.0 copy-start.3
  50.8 1.1 copy-done.3
  51.9 0.0 collective-permute-done.1.up2_ref
  51.9 0.0 copy-start.5
  51.9 1.1 copy-done.5
  53.0 1.0 collective-permute-done.2.down2_ref
  54.0 1.1 copy-done.7
  55.1 3.4 %all-to-all-done.1 = bf16[24,8,1280]{2,1,0:T(8,128)(2,1)S(1)} async-done(((bf16[24,8,1280]{2,1,0:T(8,128)(2,1)}), bf16[24,8,1280]{2,1,0:T(8,128)(2,1)S(1)}, u32[]{:S(2)}, u32[]{:S(2)}) %all-to-all-start.1) | async-done | bytes 491552 | tf_op jit(solution)/shard_map/all_to_all | solution.py:17
  58.5 0.7 shard_map.84
  59.2 21.2 %all_to_all.48 = bf16[4,8,5120]{2,1,0:T(8,128)(2,1)S(1)} all-to-all(bf16[4,8,5120]{2,1,0:T(8,128)(2,1)S(1)} %get-tuple-element.23), channel_id=1, replica_groups=mesh['x'=4,'core'=2,'tensor'=4,'y'=8,'w'=3] {'tensor'}, dimensions={0} | all-to-all | bytes 655360 | tf_op jit(solution)/shard_map/all_to_all | solution.py:17
  80.4 0.1 broadcast_in_dim.22
  80.5 0.0 copy-start.2
  80.5 0.0 copy-start.4
  80.5 16.9 %all_to_all.49 = bf16[4,32,5120]{2,1,0:T(8,128)(2,1)S(1)} all-to-all(bf16[4,32,5120]{2,1,0:T(8,128)(2,1)S(1)} %broadcast_in_dim.22), channel_id=1, replica_groups=mesh['x'=4,'core'=2,'tensor'=4,'y'=8,'w'=3] {'x'}, dimensions={0} | all-to-all | bytes 2621440 | tf_op jit(solution)/shard_map/all_to_all | solution.py:17
  97.4 0.0 copy-done.8
  97.4 0.0 copy-done.6
  97.4 0.0 copy-done.2
  97.4 0.0 copy-done.4
  97.4 2.3 %shard_map.85 = bf16[128,5120]{1,0:T(8,128)(2,1)S(1)} custom-call(bf16[128,5120]{1,0:T(8,128)(2,1)S(1)} %bitcast.19, bf16[5120,128]{1,0:T(8,128)(2,1)S(1)} %bitcast.25, bf16[5120,128]{1,0:T(8,128)(2,1)S(1)} %bitcast.27, bf16[128,5120]{1,0:T(8,128)(2,1)S(1)} %bitcast.29, bf16[5120,128]{1,0:T(8,128)(2,1)S(1)} %copy-done.4, bf16[5120,128]{1,0:T(8,128)(2,1)S(1)} %copy-done.6, ...), custom_call_target="tpu_custom_call" | custom-call | tf_op jit(solution)/shard_map/pallas_call | solution.py:38
  99.7 14.7 %all_to_all.50 = bf16[4,32,5120]{2,1,0:T(8,128)(2,1)S(1)} all-to-all(bf16[4,32,5120]{2,1,0:T(8,128)(2,1)S(1)} %bitcast.20), channel_id=1, replica_groups=mesh['x'=4,'core'=2,'tensor'=4,'y'=8,'w'=3] {'x'}, dimensions={0} | all-to-all | bytes 2621440 | tf_op jit(solution)/shard_map/all_to_all | solution.py:17
  114.5 0.2 fusion
  114.6 14.2 %all_to_all.51.parts_ref = bf16[4,8,5120]{2,1,0:T(8,128)(2,1)S(1)} all-to-all(bf16[4,8,5120]{2,1,0:T(8,128)(2,1)S(1)} %fusion), channel_id=1, replica_groups=mesh['x'=4,'core'=2,'tensor'=4,'y'=8,'w'=3] {'tensor'}, dimensions={0} | all-to-all | bytes 655360 | tf_op jit(solution)/shard_map/all_to_all | solution.py:17
  128.9 0.3 shard_map.86
  129.1 30.8 %all_to_all.52 = bf16[24,8,1280]{2,1,0:T(8,128)(2,1)S(1)} all-to-all(bf16[24,8,1280]{2,1,0:T(8,128)(2,1)S(1)} %bitcast.22), channel_id=1, replica_groups=mesh['x'=4,'core'=2,'tensor'=4,'y'=8,'w'=3] {'y','w'}, dimensions={0} | all-to-all | bytes 983040 | tf_op jit(solution)/shard_map/all_to_all | solution.py:17
  159.9 0.9 shard_map.87
  (11 shorter events, 0.1 us)
Async XLA Ops:
  0.0 18.8 %copy-start.11 = (s32[1,6,1]{1,2,0:T(1,128)S(1)}, s32[1,6,1]{1,2,0:T(1,128)}, u32[]{:S(2)}) copy-start(s32[1,6,1]{1,2,0:T(1,128)} %param.12) | copy-start | bytes 76
  0.0 33.5 %copy-start.9 = (bf16[5120,24]{0,1:T(8,128)(2,1)S(1)}, bf16[5120,24]{0,1:T(8,128)(2,1)}, u32[]{:S(2)}) copy-start(bf16[5120,24]{0,1:T(8,128)(2,1)} %param.11) | copy-start | bytes 737284
  0.0 33.5 %copy-start.10 = (f32[5120]{0:T(1024)S(1)}, f32[5120]{0:T(1024)}, u32[]{:S(2)}) copy-start(f32[5120]{0:T(1024)} %param.10) | copy-start | bytes 61444
  4.1 40.4 %copy-start = (bf16[1,5120,128]{2,1,0:T(8,128)(2,1)S(1)}, bf16[1,5120,128]{2,1,0:T(8,128)(2,1)}, u32[]{:S(2)}) copy-start(bf16[1,5120,128]{2,1,0:T(8,128)(2,1)} %param.13) | copy-start | bytes 3932164
  4.2 42.3 %copy-start.1 = (bf16[1,5120,128]{2,1,0:T(8,128)(2,1)S(1)}, bf16[1,5120,128]{2,1,0:T(8,128)(2,1)}, u32[]{:S(2)}) copy-start(bf16[1,5120,128]{2,1,0:T(8,128)(2,1)} %param.14) | copy-start | bytes 3932164
  4.2 29.4 %all-to-all-start = ((bf16[4,8,3840]{2,1,0:T(8,128)(2,1)}), bf16[4,8,3840]{2,1,0:T(8,128)(2,1)S(1)}, u32[]{:S(2)}, u32[]{:S(2)}) async-start(bf16[4,8,3840]{2,1,0:T(8,128)(2,1)} %bitcast.1), calls=%async_computation | async-start | bytes 491520 | tf_op jit(solution)/shard_map/all_to_all | solution.py:17
  35.2 23.3 %all-to-all-start.1 = ((bf16[24,8,1280]{2,1,0:T(8,128)(2,1)}), bf16[24,8,1280]{2,1,0:T(8,128)(2,1)S(1)}, u32[]{:S(2)}, u32[]{:S(2)}) async-start(bf16[24,8,1280]{2,1,0:T(8,128)(2,1)} %bitcast.8), calls=%async_computation.1 | async-start | bytes 983040 | tf_op jit(solution)/shard_map/all_to_all | solution.py:17
  44.5 6.3 %collective-permute-start = (bf16[5120,128]{1,0:T(8,128)(2,1)S(1)}, bf16[5120,128]{1,0:T(8,128)(2,1)S(1)}, u32[]{:S(2)}, u32[]{:S(2)}) collective-permute-start(bf16[5120,128]{1,0:T(8,128)(2,1)S(1)} %bitcast.24), channel_id=1, source_target_pairs={{0,96},{96,0},{1,97},{97,1},{2,98},{98,2},{3,99},{99,3},{4,100},{1... | collective-permute-start | bytes 3932168 | tf_op jit(solution)/shard_map/ppermute | solution.py:288
  46.5 5.4 %collective-permute-start.1 = (bf16[5120,128]{1,0:T(8,128)(2,1)S(1)}, bf16[5120,128]{1,0:T(8,128)(2,1)S(1)}, u32[]{:S(2)}, u32[]{:S(2)}) collective-permute-start(bf16[5120,128]{1,0:T(8,128)(2,1)S(1)} %bitcast.26), channel_id=1, source_target_pairs={{0,96},{96,0},{1,97},{97,1},{2,98},{98,2},{3,99},{99,3},{4,100},{1... | collective-permute-start | bytes 3932168 | tf_op jit(solution)/shard_map/ppermute | solution.py:288
  48.9 5.1 %collective-permute-start.2 = (bf16[128,5120]{1,0:T(8,128)(2,1)}, bf16[128,5120]{1,0:T(8,128)(2,1)S(1)}, u32[]{:S(2)}, u32[]{:S(2)}) collective-permute-start(bf16[128,5120]{1,0:T(8,128)(2,1)} %bitcast.28), channel_id=1, source_target_pairs={{0,96},{96,0},{1,97},{97,1},{2,98},{98,2},{3,99},{99,3},{4,100},{1... | collective-permute-start | bytes 3932168 | tf_op jit(solution)/shard_map/ppermute | solution.py:288
  50.8 1.1 copy-start.3
  51.9 1.1 copy-start.5
  54.0 1.1 copy-start.7
  58.5 38.9 %copy-start.8 = (bf16[128,5120]{1,0:T(8,128)(2,1)S(1)}, bf16[128,5120]{1,0:T(8,128)(2,1)}, u32[]{:S(2)}) copy-start(bf16[128,5120]{1,0:T(8,128)(2,1)} %copy-done.7) | copy-start | bytes 3932164
  80.4 17.0 %copy-start.6 = (bf16[5120,128]{1,0:T(8,128)(2,1)S(1)}, bf16[5120,128]{1,0:T(8,128)(2,1)}, u32[]{:S(2)}) copy-start(bf16[5120,128]{1,0:T(8,128)(2,1)} %copy-done.5) | copy-start | bytes 3932164
  80.5 16.9 %copy-start.2 = (bf16[1,128,5120]{2,1,0:T(8,128)(2,1)S(1)}, bf16[1,128,5120]{2,1,0:T(8,128)(2,1)}, u32[]{:S(2)}) copy-start(bf16[1,128,5120]{2,1,0:T(8,128)(2,1)} %param.15) | copy-start | bytes 3932164
  80.5 16.9 %copy-start.4 = (bf16[5120,128]{1,0:T(8,128)(2,1)S(1)}, bf16[5120,128]{1,0:T(8,128)(2,1)}, u32[]{:S(2)}) copy-start(bf16[5120,128]{1,0:T(8,128)(2,1)} %copy-done.3) | copy-start | bytes 3932164
